TPU v7x, 512 devices: a whole 4x8x8 slice. The times are simulated.
512 devices in a mesh: dp: 64 (over y_lo, z, x), tensor: 8 (over y_hi, core).
Axes of the slice: x: 4, y: 8 (y_hi: 4, y_lo: 2; y = y_hi * 2 + y_lo), z: 8, core: 2. Of those that a mesh axis runs over, the one named last changes fastest.
Arguments:
- activations: bfloat16 [65536, 3072], P(('dp', 'tensor'))
- norm_gain: bfloat16 [3072], replicated, may hold values from 0.099609375 to 1.8984375
- query_weight: bfloat16 [3072, 3072], P('dp', 'tensor')
- key_weight: bfloat16 [3072, 512], P('dp')
- value_matrix: bfloat16 [3072, 512], P('dp'), may hold values from -0.109375 to 0.109375
- output_weight: bfloat16 [3072, 3072], P('dp', 'tensor'), may hold values from -0.109375 to 0.109375
- document_lengths: int32 [64, 3], replicated, may hold values from 1 to 3, 8 in all within a row
- doc_dest: int32 [64, 3], replicated, may hold values from 0 to 63, as said below
Outputs:
- attended: bfloat16 [131072, 3072], P('dp', 'tensor')
Inputs may be any that keep to these rules, and one draw needn't show every extreme that they name: `document_lengths`: each row sums to 8; its largest entry is exactly 3. doc_dest[s, j] is either s or the next shard s + 1, the last shard wrapping to shard 0.
All inputs are finite; a program needn't handle non-finite values.
Results may differ from a plain program's by a relative error of at most 0.012.
The roundings to bfloat16 on the way count: a program that leaves them out, or rounds other values in their place, can miss the bound.
Values may be sent and summed in bfloat16 or wider, within the bound.
No kernel may reach another device: no remote copies, remote signals or barrier semaphores. Data moves between devices by JAX's collectives and lax.ppermute only.
A program may use at most 64 MiB of HBM per device.

v0:
```python
import math

import jax
import jax.numpy as jnp
from jax import lax
from jax.sharding import PartitionSpec as P

QUERY_HEADS = 24
KEY_VALUE_HEADS = 4
HEAD_SIZE = 128
BLK = 128
LMAX = 3


EPS = 1e-05


def passed_along(value, axis, steps):
    count = lax.axis_size(axis)
    pairs = [(source, (source + steps) % count) for source in range(count)]
    return lax.ppermute(value, axis, pairs)


def block_documents(length_row, count_of_rows):
    doc_ends = jnp.cumsum(length_row) * BLK
    positions = jnp.arange(count_of_rows, dtype=jnp.int32)
    return jnp.sum((positions[:, None] >= doc_ends[None, :]).astype(jnp.int32), axis=1)


def moved_rows(doc_ids, dest_row, shard_index):
    doc_slots = jnp.arange(dest_row.shape[0], dtype=jnp.int32)
    target = jnp.sum(
        jnp.where(doc_ids[:, None] == doc_slots[None, :], dest_row[None, :], 0), axis=1
    )
    return (target != shard_index).astype(jnp.bfloat16)


def region_attention(query_rows, rows_of_key, rows_of_value, doc_ids, kv_count):
    count_of_rows = query_rows.shape[0]
    head_width = query_rows.shape[1]
    per_kv = head_width // HEAD_SIZE // kv_count
    block_rows = 512
    window_len = min(block_rows + (LMAX - 1) * BLK, count_of_rows)
    query_blocks = query_rows.reshape(
        count_of_rows // block_rows, block_rows, kv_count, per_kv, HEAD_SIZE
    )
    heads_of_key = rows_of_key.reshape(count_of_rows, kv_count, HEAD_SIZE)
    heads_of_value = rows_of_value.reshape(count_of_rows, kv_count, HEAD_SIZE)

    def one_block(block_item):
        query_block, first_row = block_item
        window_start = jnp.maximum(first_row + block_rows - window_len, 0)
        window_keys = lax.dynamic_slice_in_dim(heads_of_key, window_start, window_len, 0)
        window_values = lax.dynamic_slice_in_dim(heads_of_value, window_start, window_len, 0)
        window_docs = lax.dynamic_slice_in_dim(doc_ids, window_start, window_len, 0)
        window_positions = window_start + jnp.arange(window_len, dtype=jnp.int32)
        block_positions = first_row + jnp.arange(block_rows, dtype=jnp.int32)
        block_docs = lax.dynamic_slice_in_dim(doc_ids, first_row, block_rows)
        allowed = (block_docs[:, None] == window_docs[None, :]) & (
            window_positions[None, :] <= block_positions[:, None]
        )
        scores = jnp.einsum(
            "qkgd,skd->kgqs", query_block, window_keys, preferred_element_type=jnp.float32
        ) / math.sqrt(HEAD_SIZE)
        scores = jnp.where(allowed[None, None], scores, -jnp.inf)
        row_max = jnp.max(scores, axis=-1, keepdims=True)
        exponent = jnp.exp(scores - row_max)
        row_total = jnp.sum(exponent, axis=-1)
        mixed_values = jnp.einsum(
            "kgqs,skd->qkgd",
            exponent.astype(jnp.bfloat16),
            window_values,
            preferred_element_type=jnp.float32,
        )
        outputs = mixed_values / jnp.transpose(row_total, (2, 0, 1))[..., None]
        return outputs.reshape(block_rows, head_width).astype(jnp.bfloat16)

    first_rows = jnp.arange(count_of_rows // block_rows, dtype=jnp.int32) * block_rows
    return lax.map(one_block, (query_blocks, first_rows)).reshape(count_of_rows, head_width)


def shards(
    activations,
    norm_gain,
    query_weight,
    key_weight,
    value_matrix,
    output_weight,
    document_lengths,
    doc_dest,
):
    inputs = activations.astype(jnp.float32)
    mean_square = jnp.mean(inputs * inputs, axis=1, keepdims=True)
    normed = (inputs * lax.rsqrt(mean_square + EPS) * norm_gain.astype(jnp.float32)).astype(
        jnp.bfloat16
    )
    tensor_index = lax.axis_index("tensor")
    query_width = query_weight.shape[1]
    local_heads = query_width // HEAD_SIZE
    group_width = QUERY_HEADS // KEY_VALUE_HEADS
    kv_count = max(local_heads // group_width, 1)
    kv_width = kv_count * HEAD_SIZE
    kv_first = tensor_index * local_heads // group_width
    key_local = lax.dynamic_slice_in_dim(key_weight, kv_first * HEAD_SIZE, kv_width, 1)
    value_local = lax.dynamic_slice_in_dim(value_matrix, kv_first * HEAD_SIZE, kv_width, 1)
    gathered = lax.all_gather(normed, "tensor", axis=0, tiled=True)
    pieces = (
        lax.all_gather(query_weight, "dp", axis=0, tiled=True),
        lax.all_gather(key_local, "dp", axis=0, tiled=True),
        lax.all_gather(value_local, "dp", axis=0, tiled=True),
    )
    columns = gathered
    query_sum, key_sum, value_sum = tuple(
        (
            jnp.dot(columns, weight_piece, preferred_element_type=jnp.float32)
            for weight_piece in pieces
        )
    )
    query_rows = query_sum.astype(jnp.bfloat16)
    rows_of_key = key_sum.astype(jnp.bfloat16)
    rows_of_value = value_sum.astype(jnp.bfloat16)
    shard_index = lax.axis_index("dp")
    count_of_rows = query_rows.shape[0]
    own_docs = block_documents(
        lax.dynamic_index_in_dim(document_lengths, shard_index, 0, keepdims=False), count_of_rows
    )
    own_moved = moved_rows(
        own_docs, lax.dynamic_index_in_dim(doc_dest, shard_index, 0, keepdims=False), shard_index
    )
    own_attention = region_attention(query_rows, rows_of_key, rows_of_value, own_docs, kv_count)
    all_heads = lax.all_gather(own_attention, "tensor", axis=1, tiled=True)
    columns = all_heads
    output_sum = jnp.dot(
        columns,
        lax.all_gather(output_weight, "dp", axis=0, tiled=True),
        preferred_element_type=jnp.float32,
    )
    projected = output_sum.astype(jnp.bfloat16)
    staying = projected * (1 - own_moved)[:, None]
    leaving = projected * own_moved[:, None]
    arriving = passed_along(leaving, "dp", 1)
    return jnp.concatenate([staying, arriving], axis=0)


def solution(mesh):
    in_specs = (
        P(("dp", "tensor"), None),
        P(),
        P("dp", "tensor"),
        P("dp", None),
        P("dp", None),
        P("dp", "tensor"),
        P(),
        P(),
    )
    out_specs = P("dp", "tensor")
    return jax.shard_map(shards, mesh=mesh, in_specs=in_specs, out_specs=out_specs, check_vma=False)
```

profile of v0, /device:TPU:1, one launch (start us, length us, event | category | flops | bytes accessed | tf_op | source)
XLA Modules:
  0.0 810.3 jit_solution(7313757349730768166)
XLA Ops:
  6.5 0.0 copy-start
  6.5 0.0 copy-start.4
  6.5 0.0 copy-start.3
  6.5 0.0 all-gather.7.cloned.1.call-start
  6.5 0.7 all-gather.7.cloned.1.call-update
  7.3 0.0 all-gather.5.cloned.1.call-start
  7.3 0.7 convert_element_type.63
  8.0 1.4 fusion.27
  9.4 2.3 fusion.29
  11.7 0.0 all-gather.5.cloned.1.call-update
  11.7 0.0 all-gather.11.cloned.1.call-start
  11.7 0.7 all-gather.11.cloned.1.call-update
  12.4 0.0 all-gather.9.cloned.1.call-start
  12.5 0.0 copy-done
  12.6 142.1 %all_gather.19 = bf16[3072,128]{1,0:T(8,128)(2,1)S(1)} all-gather(bf16[48,128]{1,0:T(8,128)(2,1)S(1)} %constant_dynamic-slice_fusion.1), channel_id=1, replica_groups=mesh['dp'=64,'tensor'=8] {'dp'}, dimensions={0}, use_global_device_ids=true | all-gather | bytes 798720 | tf_op jit(solution)/shard_map/all_gather | solution.py:110
  154.7 0.7 constant_dynamic-slice_fusion
  155.4 138.5 %all_gather.20 = bf16[3072,128]{1,0:T(8,128)(2,1)} all-gather(bf16[48,128]{1,0:T(8,128)(2,1)S(1)} %constant_dynamic-slice_fusion), channel_id=1, replica_groups=mesh['dp'=64,'tensor'=8] {'dp'}, dimensions={0}, use_global_device_ids=true | all-gather | bytes 798720 | tf_op jit(solution)/shard_map/all_gather | solution.py:109
  294.0 0.0 copy-done.4
  294.0 0.0 copy-done.3
  294.0 0.2 dynamic-slice_reduce_fusion
  294.2 0.2 reduce-window.8
  294.4 0.1 convert_reduce_fusion
  294.5 0.0 all-gather.7.cloned.1.call-done
  294.5 96.5 %all-gather.5.cloned.1.call-done = bf16[1024,3072]{1,0:T(8,128)(2,1)} async-done(((bf16[128,3072]{1,0:T(8,128)(2,1)}), bf16[1024,3072]{1,0:T(8,128)(2,1)}) %all-gather.5.cloned.1.call-update) | async-done | bytes 6291472 | tf_op jit(solution)/shard_map/all_gather | solution.py:106
  391.0 6.9 convolution_convert_fusion.1
  397.8 0.3 reshape.223
  398.1 0.1 copy.20
  398.2 0.0 copy-start.2
  398.2 4.6 fusion.30
  402.9 0.0 copy-done.2
  402.9 4.6 fusion.31
  407.5 16.5 %while.14 = (s32[]{:T(128)}, bf16[2,512,384]{2,1,0:T(8,128)(2,1)S(1)}, s32[2]{0:T(128)S(1)}, bf16[1024,1,128]{2,0,1:T(8,128)(2,1)S(1)}, s32[1024]{0:T(1024)S(1)}...) while((s32[]{:T(128)}, ...), condition=%wide.region_6.7_spmd, body=%wide.region_3.6_spmd.sunk | while | flops 618526976 | bytes 18541780 | solution.py:79
  407.5 0.6 dynamic_slice.102
  410.0 0.1 dynamic_slice.103
  410.8 0.1 dynamic_slice.104
  410.8 0.6 iota_add_fusion.4
  411.5 0.4 compare_and_fusion.2
  411.9 1.0 fusion.47
  412.9 1.0 fusion.48
  413.9 1.5 fusion.49
  415.4 0.2 copy.29
  415.7 0.1 constant_dynamic-update-slice_fusion.2
  415.7 0.6 dynamic_slice.102
  418.3 0.1 dynamic_slice.103
  419.0 0.1 dynamic_slice.104
  419.1 0.6 iota_add_fusion.4
  419.7 0.4 compare_and_fusion.2
  420.1 1.0 fusion.47
  421.1 1.0 fusion.48
  422.2 1.5 fusion.49
  423.7 0.2 copy.29
  423.9 0.1 constant_dynamic-update-slice_fusion.2
  424.0 0.0 copy-start.1
  424.0 0.9 copy-done.1
  424.9 0.0 all-gather.9.cloned.1.call-update
  424.9 0.1 select_reduce_fusion
  425.0 227.1 %all-gather.11.cloned.1.call-done = bf16[3072,384]{1,0:T(8,128)(2,1)} async-done(((bf16[48,384]{1,0:T(8,128)(2,1)}), bf16[3072,384]{1,0:T(8,128)(2,1)}) %all-gather.11.cloned.1.call-update) | async-done | bytes 2359312 | tf_op jit(solution)/shard_map/all_gather | solution.py:135
  652.1 110.3 %all-gather.9.cloned.1.call-done = bf16[1024,3072]{1,0:T(8,128)(2,1)} async-done(((bf16[1024,384]{1,0:T(8,128)(2,1)}), bf16[1024,3072]{1,0:T(8,128)(2,1)}) %all-gather.9.cloned.1.call-update) | async-done | bytes 6291472 | tf_op jit(solution)/shard_map/all_gather | solution.py:131
  762.4 6.9 broadcast_multiply_fusion.1
  769.3 3.1 collective-permute-start
  772.4 30.1 %collective-permute-done = bf16[1024,384]{1,0:T(8,128)(2,1)S(1)} collective-permute-done((bf16[1024,384]{1,0:T(8,128)(2,1)S(1)}, bf16[1024,384]{1,0:T(8,128)(2,1)S(1)}, u32[]{:S(2)}, u32[]{:S(2)}) %collective-permute-start) | collective-permute-done | bytes 786464 | tf_op jit(solution)/shard_map/ppermute | solution.py:21
  802.5 1.3 pad_maximum_fusion
  (8 shorter events, 0.0 us)
Async XLA Ops:
  6.5 6.0 copy-start
  6.5 287.4 %copy-start.4 = (s32[64,3]{0,1:T(4,128)S(1)}, s32[64,3]{0,1:T(4,128)}, u32[]{:S(2)}) copy-start(s32[64,3]{0,1:T(4,128)} %param.16) | copy-start | bytes 2308
  6.5 287.4 %copy-start.3 = (s32[64,3]{0,1:T(4,128)S(1)}, s32[64,3]{0,1:T(4,128)}, u32[]{:S(2)}) copy-start(s32[64,3]{0,1:T(4,128)} %param.17) | copy-start | bytes 2308
  6.5 287.9 %all-gather.7.cloned.1.call-start = ((), (), s32[]{:S(2)}) async-start(), calls=%async_computation.1 | async-start | bytes 2396160 | tf_op jit(solution)/shard_map/all_gather | solution.py:108
  7.3 383.7 %all-gather.5.cloned.1.call-start = ((), (), s32[]{:S(2)}) async-start(), calls=%async_computation | async-start | bytes 7077888 | tf_op jit(solution)/shard_map/all_gather | solution.py:106
  11.7 640.4 %all-gather.11.cloned.1.call-start = ((), (), s32[]{:S(2)}) async-start(), calls=%async_computation.3 | async-start | bytes 2396160 | tf_op jit(solution)/shard_map/all_gather | solution.py:135
  12.4 750.0 %all-gather.9.cloned.1.call-start = ((), (), s32[]{:S(2)}) async-start(), calls=%async_computation.2 | async-start | bytes 7077888 | tf_op jit(solution)/shard_map/all_gather | solution.py:131
  398.2 4.7 copy-start.2
  424.0 0.9 copy-start.1
  769.3 33.2 %collective-permute-start = (bf16[1024,384]{1,0:T(8,128)(2,1)S(1)}, bf16[1024,384]{1,0:T(8,128)(2,1)S(1)}, u32[]{:S(2)}, u32[]{:S(2)}) collective-permute-start(bf16[1024,384]{1,0:T(8,128)(2,1)S(1)} %get-tuple-element.187), channel_id=1, source_target_pairs={{0,8},{8,16},{16,24},{24,32},{32,40},{40,48},{48,56},{56,64},{64,7... | collective-permute-start | bytes 2359304 | tf_op jit(solution)/shard_map/ppermute | solution.py:21
Sparse Core Ops, SparseCore 0:
  9.4 266.8 all-gather.6
  278.4 112.4 all-gather.4
  393.0 258.9 all-gather.10
  654.0 108.2 all-gather.8
where the time goes:
time: 811 us; the launch traced here: 810 us
  waiting for transfers between devices  465 us (57%)
  blocking collectives  281 us (35%)
  matrix products  28 us (3%)
  between operations  13.3 us (2%)
  other arithmetic  10.2 us (1%)
    all_gather x1, waiting for transfers between devices, shards(): lax.all_gather(output_weight, 'dp', axis=0, tiled=True)  227 us
    all_gather x1, blocking collectives, shards(): lax.all_gather(value_local, 'dp', axis=0, tiled=True)  142 us
    all_gather x1, blocking collectives, shards(): lax.all_gather(key_local, 'dp', axis=0, tiled=True)  139 us
    all_gather x1, waiting for transfers between devices, shards(): all_heads = lax.all_gather(own_attention, 'tensor', axis=1, tiled=True)  110 us
    all_gather x1, waiting for transfers between devices, shards(): gathered = lax.all_gather(normed, 'tensor', axis=0, tiled=True)  96.5 us
    ppermute x1, waiting for transfers between devices, passed_along(): return lax.ppermute(value, axis, pairs)  30.1 us
  transfers between devices with their start and end apart: 5, of which 4 were waited for; matrix products, arithmetic and copies ran while one was open for 4% of the time, Pallas kernels for 0%

commit v1 on v0

v1 whole, which is shorter than its diff:
```python
import math

import jax
import jax.numpy as jnp
import numpy as np
from jax import lax
from jax.experimental import pallas as pl
from jax.experimental.pallas import tpu as pltpu
from jax.sharding import Mesh, PartitionSpec as P

HEAD_SIZE = 128
BLK = 128
EPS = 1e-05
AXES = ("yl", "z", "x", "yh", "c")
SIZES = (2, 8, 4, 4, 2)
EXTENT = dict(zip(AXES, SIZES))
VMEM = 56 * 1024 * 1024
HEAD_ORDER = (0, 1, 3, 4, 2, 5)


def shift(value, axis, steps):
    count = EXTENT[axis]
    return lax.ppermute(value, axis, [(i, (i + steps) % count) for i in range(count)])


def scatter_pairs(round_index):
    pairs = []
    for yl in range(2):
        for yh in range(4):
            for c in range(2):
                target = ((yh >> 1) * 4 + ((2 * yl + c) ^ round_index)) * 2 + (yh & 1)
                pairs.append(((yl * 4 + yh) * 2 + c, target))
    return pairs


def collect_pairs(round_index):
    pairs = []
    for yl in range(2):
        for yh in range(4):
            for c in range(2):
                slot = yh ^ round_index
                target = ((slot >> 1) * 4 + 2 * yl + c) * 2 + (slot & 1)
                pairs.append(((yl * 4 + yh) * 2 + c, target))
    return pairs


def ring_x(block):
    half = block.shape[0] // 2
    below = shift(block, "x", 1)
    above = shift(block, "x", -1)
    far_low = shift(below[:half], "x", 1)
    far_high = shift(above[half:], "x", -1)
    return block, below, above, far_low, far_high


def copies_of_ring(refs, target, columns, x):
    own, below, above, far_low, far_high = refs
    half = own.shape[0] // 2
    full = own.shape[0]
    pairs = []
    for ref, start, size, offset in (
        (own, 0, full, 0),
        (below, 0, full, 3),
        (above, 0, full, 1),
        (far_low, 0, half, 2),
        (far_high, half, full - half, 2),
    ):
        for yl in range(2):
            pairs.append(
                (ref.at[:, yl], target.at[yl, pl.ds(start, size), (x + offset) & 3, :, columns])
            )
    return pairs


def start_all(pairs, sems, first):
    made = []
    for i, (source, target) in enumerate(pairs):
        copy = pltpu.make_async_copy(source, target, sems.at[first + i])
        copy.start()
        made.append(copy)
    return made


def rows_pairs(pieces, target, yl, c):
    pairs = []
    for i, piece in enumerate(pieces):
        place = 2 * (yl ^ (i >> 1)) + (c ^ (i & 1))
        pairs.append((piece, target.at[place]))
    return pairs


def key_value_kernel(where, n0, n1, n2, n3, b0, b1, b2, b3, b4, out, rows, weight, sems):
    yl, x, c = where[0], where[2], where[4]
    made = start_all(rows_pairs((n0, n1, n2, n3), rows, yl, c), sems, 0)
    made += start_all(
        copies_of_ring((b0, b1, b2, b3, b4), weight, slice(0, 256), x), sems, 4
    )
    for copy in made:
        copy.wait()
    out[...] = jnp.dot(
        rows[...].reshape(512, 3072),
        weight[...].reshape(3072, 256),
        preferred_element_type=jnp.float32,
    ).astype(jnp.bfloat16)


def attention_kernel(
    where, n0, n1, n2, n3, wide, b0, b1, b2, b3, b4, own_kv, halo_kv, out, rows, weight, query, sems
):
    yl, x, yh, c = where[0], where[2], where[3], where[4]
    made = start_all(rows_pairs((n0, n1, n2, n3), rows, yl, c), sems, 0)
    made += start_all(
        [(wide.at[:, :, i], weight.at[i, :, :, :, 0:512]) for i in range(2)], sems, 4
    )
    made += start_all(
        copies_of_ring((b0, b1, b2, b3, b4), weight, slice(512, 768), x), sems, 6
    )
    for copy in made:
        copy.wait()
    query[...] = jnp.dot(
        rows[...].reshape(512, 3072),
        weight[...].reshape(3072, 768),
        preferred_element_type=jnp.float32,
    ).astype(jnp.bfloat16)
    row = lax.broadcasted_iota(jnp.int32, (BLK, 3 * BLK), 0)
    column = lax.broadcasted_iota(jnp.int32, (BLK, 3 * BLK), 1)
    causal = (column >= 2 * BLK) & (column - 2 * BLK <= row)
    scale = 1.0 / math.sqrt(HEAD_SIZE)
    for shard in range(2):
        first_end = where[5 + 2 * shard]
        second_end = where[6 + 2 * shard]

        def document(block):
            return (block >= first_end).astype(jnp.int32) + (block >= second_end).astype(jnp.int32)

        keys = jnp.concatenate(
            [
                halo_kv[shard * 256 : shard * 256 + 256, 0:128],
                own_kv[shard * 256 : shard * 256 + 256, 0:128],
            ],
            axis=0,
        )
        values = jnp.concatenate(
            [
                halo_kv[shard * 256 : shard * 256 + 256, 128:256],
                own_kv[shard * 256 : shard * 256 + 256, 128:256],
            ],
            axis=0,
        )
        for j in range(2):
            block = 2 * yh + j
            mine = document(block)
            near = ((block >= 1) & (document(block - 1) == mine)).astype(jnp.int32)
            far = ((block >= 2) & (document(block - 2) == mine)).astype(jnp.int32)
            open_before = jnp.where(column < BLK, far, near)
            allowed = causal | ((column < 2 * BLK) & (open_before == 1))
            at = shard * 256 + j * BLK
            stacked = jnp.concatenate(
                [query[at : at + BLK, i * 128 : i * 128 + 128] for i in range(6)], axis=0
            )
            window = keys[j * BLK : j * BLK + 3 * BLK]
            scores = (
                lax.dot_general(
                    stacked, window, (((1,), (1,)), ((), ())), preferred_element_type=jnp.float32
                )
                * scale
            )
            scores = jnp.where(allowed[None], scores.reshape(6, BLK, 3 * BLK), -jnp.inf)
            exponent = jnp.exp(scores - jnp.max(scores, axis=-1, keepdims=True))
            total = jnp.sum(exponent, axis=-1, keepdims=True)
            mixed = jnp.dot(
                exponent.astype(jnp.bfloat16).reshape(6 * BLK, 3 * BLK),
                values[j * BLK : j * BLK + 3 * BLK],
                preferred_element_type=jnp.float32,
            )
            mixed = (mixed / total.reshape(6 * BLK, 1)).astype(jnp.bfloat16)
            for i, head in enumerate(HEAD_ORDER):
                out[at : at + BLK, head * 128 : head * 128 + 128] = mixed[i * BLK : i * BLK + BLK]


def output_kernel(
    where, a0, a1, a2, a3, wide, b0, b1, b2, b3, b4, s0, s1, s2, s3, weight, blocks, sems
):
    yl, x, yh, c = where[0], where[2], where[3], where[4]
    made = start_all(
        [(wide.at[:, :, i], weight.at[i, :, :, :, 0:384]) for i in range(2)], sems, 0
    )
    made += start_all(
        copies_of_ring((b0, b1, b2, b3, b4), weight, slice(384, 768), x), sems, 2
    )
    for copy in made:
        copy.wait()
    total = jnp.zeros((512, 768), jnp.float32)
    for i, piece in enumerate((a0, a1, a2, a3)):
        part = weight[yl ^ (i >> 1), pl.ds(4 * (c ^ (i & 1)), 4)]
        total = total + jnp.dot(
            piece[...], part.reshape(768, 768), preferred_element_type=jnp.float32
        )
    for shard in range(2):
        for half in range(2):
            blocks[2 * shard + half] = total[
                shard * 256 : shard * 256 + 256, half * 384 : half * 384 + 384
            ].astype(jnp.bfloat16)
    for r, out in enumerate((s0, s1, s2, s3)):
        out[...] = blocks[yh ^ r]


SMEM_SPEC = pl.BlockSpec(memory_space=pltpu.SMEM)
ANY_SPEC = pl.BlockSpec(memory_space=pl.ANY)
VMEM_SPEC = pl.BlockSpec(memory_space=pltpu.VMEM)
PARAMS = pltpu.CompilerParams(vmem_limit_bytes=VMEM)


def project_key_value(where, pieces, ring):
    return pl.pallas_call(
        key_value_kernel,
        out_shape=jax.ShapeDtypeStruct((512, 256), jnp.bfloat16),
        in_specs=[SMEM_SPEC] + [ANY_SPEC] * 9,
        out_specs=VMEM_SPEC,
        scratch_shapes=[
            pltpu.VMEM((4, 128, 3072), jnp.bfloat16),
            pltpu.VMEM((2, 8, 4, 48, 256), jnp.bfloat16),
            pltpu.SemaphoreType.DMA((14,)),
        ],
        compiler_params=PARAMS,
        name="key_value",
    )(where, *pieces, *ring)


def attend(where, pieces, wide, ring, own_kv, halo_kv):
    return pl.pallas_call(
        attention_kernel,
        out_shape=jax.ShapeDtypeStruct((512, 768), jnp.bfloat16),
        in_specs=[SMEM_SPEC] + [ANY_SPEC] * 10 + [VMEM_SPEC] * 2,
        out_specs=VMEM_SPEC,
        scratch_shapes=[
            pltpu.VMEM((4, 128, 3072), jnp.bfloat16),
            pltpu.VMEM((2, 8, 4, 48, 768), jnp.bfloat16),
            pltpu.VMEM((512, 768), jnp.bfloat16),
            pltpu.SemaphoreType.DMA((16,)),
        ],
        compiler_params=PARAMS,
        name="attend",
    )(where, *pieces, wide, *ring, own_kv, halo_kv)


def project_output(where, pieces, wide, ring):
    piece = jax.ShapeDtypeStruct((256, 384), jnp.bfloat16)
    return pl.pallas_call(
        output_kernel,
        out_shape=(piece,) * 4,
        in_specs=[SMEM_SPEC] + [VMEM_SPEC] * 4 + [ANY_SPEC] * 6,
        out_specs=(VMEM_SPEC,) * 4,
        scratch_shapes=[
            pltpu.VMEM((2, 8, 4, 48, 768), jnp.bfloat16),
            pltpu.VMEM((4, 256, 384), jnp.bfloat16),
            pltpu.SemaphoreType.DMA((12,)),
        ],
        compiler_params=PARAMS,
        name="project_output",
    )(where, *pieces, wide, *ring)


def exchanged(value):
    other = shift(value, "yl", 1)
    return value, shift(value, "c", 1), other, shift(other, "c", 1)


def shards(
    activations,
    norm_gain,
    query_weight,
    key_weight,
    value_matrix,
    output_weight,
    document_lengths,
    doc_dest,
):
    yl, z, x, yh, c = (lax.axis_index(axis) for axis in AXES)
    shard_index = (yl * 8 + z) * 4 + x
    ends = jnp.cumsum(document_lengths, axis=1)

    def row_of(table, index):
        return lax.dynamic_index_in_dim(table, index, 0, keepdims=False)

    group_ends = [row_of(ends, (i * 8 + z) * 4 + x) for i in range(2)]
    where = jnp.stack(
        [yl, z, x, yh, c]
        + [group_ends[0][0], group_ends[0][1], group_ends[1][0], group_ends[1][1]]
    ).astype(jnp.int32)

    key_or_value = lax.dynamic_slice_in_dim(
        jnp.where(c == 0, key_weight, value_matrix), yh * 128, 128, 1
    )
    packed = jnp.concatenate([key_or_value, query_weight, output_weight], axis=1)
    rounds = jnp.stack(
        [lax.ppermute(packed, ("yl", "yh", "c"), scatter_pairs(r)) for r in range(4)]
    )
    slots = [lax.dynamic_index_in_dim(rounds, s ^ yh, 0, keepdims=False) for s in range(4)]
    low = jnp.stack([slots[0], slots[2]])
    high = jnp.stack([slots[1], slots[3]])
    wide_part = jnp.concatenate(
        [low[..., 128:384], high[..., 128:384], low[..., 512:896]], axis=2
    )
    ring_part = jnp.concatenate(
        [
            low[..., 0:128],
            high[..., 0:128],
            low[..., 384:512],
            high[..., 384:512],
            high[..., 512:896],
        ],
        axis=2,
    )
    wide_x = lax.all_gather(wide_part, "x", axis=0, tiled=False)
    ring_z = lax.all_gather(ring_part, "z", axis=0, tiled=False)
    wide_query = lax.all_gather(wide_x[..., 0:512], "z", axis=0, tiled=False)
    wide_output = lax.all_gather(wide_x[..., 512:896], "z", axis=0, tiled=False)

    inputs = activations.astype(jnp.float32)
    mean_square = jnp.mean(inputs * inputs, axis=1, keepdims=True)
    normed = (inputs * lax.rsqrt(mean_square + EPS) * norm_gain.astype(jnp.float32)).astype(
        jnp.bfloat16
    )
    pieces = exchanged(normed)

    ring_key_value = ring_x(ring_z[..., 0:256])
    own_kv = project_key_value(where, pieces, ring_key_value)
    halo_kv = shift(own_kv, "yh", 1)
    ring_query = ring_x(ring_z[..., 256:512])
    attention = attend(where, pieces, wide_query, ring_query, own_kv, halo_kv)
    ring_output = ring_x(ring_z[..., 512:896])
    gathered = exchanged(attention)
    sent = project_output(where, gathered, wide_output, ring_output)

    taken = [
        lax.ppermute(sent[r], ("yl", "yh", "c"), collect_pairs(r)) for r in range(4)
    ]
    own_slot = 2 * yl + c
    own_ends = row_of(ends, shard_index)
    own_dest = row_of(doc_dest, shard_index)
    blocks = jnp.arange(8, dtype=jnp.int32)
    block_docs = (blocks >= own_ends[0]).astype(jnp.int32) + (blocks >= own_ends[1]).astype(
        jnp.int32
    )
    target = jnp.sum(
        jnp.where(block_docs[:, None] == jnp.arange(3)[None, :], own_dest[None, :], 0), axis=1
    )
    moved = (target != shard_index).astype(jnp.bfloat16)
    leaving = []
    staying = []
    for r in range(4):
        flags = lax.dynamic_slice_in_dim(moved, 2 * (own_slot ^ r), 2, 0)
        flags = jnp.broadcast_to(flags[:, None, None], (2, BLK, 1)).reshape(2 * BLK, 1)
        leaving.append(taken[r] * flags)
        staying.append(taken[r] * (1 - flags))
    count = 64
    pairs = [(i, (i + 1) % count) for i in range(count)]
    arrived = []
    for i in range(2):
        arrived.append(
            lax.ppermute(
                jnp.stack([leaving[2 * i], leaving[2 * i + 1]]), ("yl", "z", "x"), pairs
            )
        )
    arrived = jnp.concatenate(arrived, axis=0)
    kept = jnp.stack(staying)
    before = (shard_index + 63) % 64
    before_slot = 2 * (before // 32) + c
    parts = [lax.dynamic_index_in_dim(kept, q ^ own_slot, 0, keepdims=False) for q in range(4)]
    parts += [
        lax.dynamic_index_in_dim(arrived, q ^ before_slot, 0, keepdims=False) for q in range(4)
    ]
    return jnp.concatenate(parts, axis=0)


def solution(mesh):
    fine = Mesh(np.asarray(mesh.devices).reshape(SIZES), AXES)
    dp, tensor = ("yl", "z", "x"), ("yh", "c")
    in_specs = (
        P(dp + tensor, None),
        P(),
        P(dp, tensor),
        P(dp, None),
        P(dp, None),
        P(dp, tensor),
        P(),
        P(),
    )
    return jax.shard_map(
        shards, mesh=fine, in_specs=in_specs, out_specs=P(dp, tensor), check_vma=False
    )
```

time: 811 us -> 248 us (0.31)
  waiting for transfers between devices: 465 us -> 57.4 us
  blocking collectives: 281 us -> 11.3 us
  starting transfers between devices: 3.21 us -> 116 us
  matrix products: 28 us -> 0 us
  Pallas kernels: 0 us -> 23.8 us
  local copies, waits for them, and re-layouts: 4.24 us -> 19.6 us
    all_gather x4 -> x3, waiting for transfers between devices: 434 us -> 5.4 us  [the longest x1 4.84 us: shards(): ring_z = lax.all_gather(ring_part, 'z', axis=0, tiled=False)]
    all_gather x2 -> x1, blocking collectives: 281 us -> 11.3 us  [shards(): wide_x = lax.all_gather(wide_part, 'x', axis=0, tiled=False)]
    ppermute x1 -> x29, starting transfers between devices: 3.09 us -> 115 us  [the longest x19 76.4 us: shift(): lax.ppermute(value, axis, [(i, (i + steps) % count) for i in range(count)])]
    dot_general x8 -> x0, matrix products: 28 us -> none  [the longest x3 16.1 us: shards(): jnp.dot(columns, weight_piece, preferred_element_type=jnp.float32)]
    pallas_call x0 -> x3, Pallas kernels: none -> 23.8 us  [the longest x1 11.2 us: attend(): pl.pallas_call(attention_kernel, out_shape=jax.ShapeDtypeStruct((512, 768...]
    ppermute x1 -> x29, waiting for transfers between devices: 30.1 us -> 51.9 us  [the longest x2 24 us: shards(): lax.ppermute(jnp.stack([leaving[2 * i], leaving[2 * i + 1]]), ('yl', 'z',...]
    slice x0 -> x12, local copies, waits for them, and re-layouts: none -> 12.5 us  [the longest x3 3.39 us: ring_x(): far_low = shift(below[:half], 'x', 1)]
  transfers between devices with their start and end apart: 5 -> 32, of which waited for: 4 -> 13; matrix products, arithmetic and copies ran while one was open for 4% -> 8% of each run, Pallas kernels for 0% -> 6%
where the time goes in v1:
time: 248 us; the launch traced here: 247 us
  starting transfers between devices  116 us (47%)
  waiting for transfers between devices  57.4 us (23%)
  Pallas kernels  23.8 us (10%)
  local copies, waits for them, and re-layouts  19.6 us (8%)
  between operations  13.9 us (6%)
  blocking collectives  11.3 us (5%)
  other arithmetic  5.28 us (2%)
    ppermute x19, starting transfers between devices, shift(): lax.ppermute(value, axis, [(i, (i + steps) % count) for i in range(count)])  76.4 us
    ppermute x2, waiting for transfers between devices, shards(): lax.ppermute(jnp.stack([leaving[2 * i], leaving[2 * i + 1]]), ('yl', 'z',...  24 us
    ppermute x19, waiting for transfers between devices, shift(): lax.ppermute(value, axis, [(i, (i + steps) % count) for i in range(count)])  18.3 us
    ppermute x4, starting transfers between devices, shards(): lax.ppermute(packed, ('yl', 'yh', 'c'), scatter_pairs(r))  17.1 us
    ppermute x4, starting transfers between devices, shards(): lax.ppermute(sent[r], ('yl', 'yh', 'c'), collect_pairs(r))  17 us
    all_gather x1, blocking collectives, shards(): wide_x = lax.all_gather(wide_part, 'x', axis=0, tiled=False)  11.3 us
    pallas_call x1, Pallas kernels, attend(): pl.pallas_call(attention_kernel, out_shape=jax.ShapeDtypeStruct((512, 768...  11.2 us
    pallas_call x1, Pallas kernels, project_output(): pl.pallas_call(output_kernel, out_shape=(piece,) * 4, in_specs=[SMEM_SPEC...  7.8 us
  transfers between devices with their start and end apart: 32, of which 13 were waited for; matrix products, arithmetic and copies ran while one was open for 8% of the time, Pallas kernels for 6%

profile of v1, /device:TPU:1, one launch (start us, length us, event | category | flops | bytes accessed | tf_op | source)
XLA Modules:
  0.0 246.8 jit_solution(7932100434393271597)
XLA Ops:
  6.5 0.7 dynamic-slice_select_fusion
  7.3 0.8 pad_maximum_fusion.4
  8.1 8.8 %collective-permute-start.4 = (bf16[48,896]{1,0:T(8,128)(2,1)S(1)}, bf16[48,896]{1,0:T(8,128)(2,1)S(1)}, u32[]{:S(2)}, u32[]{:S(2)}) collective-permute-start(bf16[48,896]{1,0:T(8,128)(2,1)S(1)} %pad_maximum_fusion.4), channel_id=1, source_target_pairs={{0,2},{1,0},{2,3},{3,1},{4,258},{5,256},{6,259},{7,257},{256,6},{2... | collective-permute-start | bytes 258056 | tf_op jit(solution)/shard_map/ppermute | solution.py:297
  16.9 1.9 collective-permute-start.5
  18.8 3.4 %collective-permute-start.6 = (bf16[48,896]{1,0:T(8,128)(2,1)S(1)}, bf16[48,896]{1,0:T(8,128)(2,1)S(1)}, u32[]{:S(2)}, u32[]{:S(2)}) collective-permute-start(bf16[48,896]{1,0:T(8,128)(2,1)S(1)} %pad_maximum_fusion.4), channel_id=1, source_target_pairs={{0,6},{1,4},{2,7},{3,5},{4,262},{5,260},{6,263},{7,261},{256,2},{2... | collective-permute-start | bytes 258056 | tf_op jit(solution)/shard_map/ppermute | solution.py:297
  22.2 2.9 %collective-permute-start.3 = (bf16[48,896]{1,0:T(8,128)(2,1)S(1)}, bf16[48,896]{1,0:T(8,128)(2,1)S(1)}, u32[]{:S(2)}, u32[]{:S(2)}) collective-permute-start(bf16[48,896]{1,0:T(8,128)(2,1)S(1)} %pad_maximum_fusion.4), channel_id=1, source_target_pairs={{0,0},{1,2},{2,1},{3,3},{4,256},{5,258},{6,257},{7,259},{256,4},{2... | collective-permute-start | bytes 258056 | tf_op jit(solution)/shard_map/ppermute | solution.py:297
  25.2 2.0 collective-permute-done.6
  27.2 2.4 collective-permute-done.3
  29.8 0.7 fusion.16
  30.6 11.3 %all-gather = bf16[8,48,896]{2,1,0:T(8,128)(2,1)S(1)} all-gather(bf16[2,48,896]{2,1,0:T(8,128)(2,1)S(1)} %get-tuple-element.28), channel_id=2, replica_groups=mesh['yl'=2,'z'=8,'x'=4,'yh'=4,'c'=2] {'x'}, dimensions={0}, use_global_device_ids=true | all-gather | bytes 860160 | tf_op jit(solution)/shard_map/all_gather | solution.py:315
  41.8 0.8 slice.120
  43.0 0.8 slice.129
  44.1 5.2 %collective-permute-start.1 = (bf16[128,3072]{1,0:T(8,128)(2,1)S(1)}, bf16[128,3072]{1,0:T(8,128)(2,1)S(1)}, u32[]{:S(2)}, u32[]{:S(2)}) collective-permute-start(bf16[128,3072]{1,0:T(8,128)(2,1)S(1)} %fusion.2.n0), channel_id=1, source_target_pairs={{0,256},{256,0},{1,257},{257,1},{2,258},{258,2},{3,259},{259,3},{4... | collective-permute-start | bytes 2359304 | tf_op jit(solution)/shard_map/ppermute | solution.py:23
  49.3 6.5 %collective-permute-start = (bf16[128,3072]{1,0:T(8,128)(2,1)S(1)}, bf16[128,3072]{1,0:T(8,128)(2,1)S(1)}, u32[]{:S(2)}, u32[]{:S(2)}) collective-permute-start(bf16[128,3072]{1,0:T(8,128)(2,1)S(1)} %fusion.2.n0), channel_id=1, source_target_pairs={{0,1},{1,0},{2,3},{3,2},{4,5},{5,4},{6,7},{7,6},{8,9},{9,8},{10,11... | collective-permute-start | bytes 2359304 | tf_op jit(solution)/shard_map/ppermute | solution.py:23
  55.7 7.2 %collective-permute-done.1.n2 = bf16[128,3072]{1,0:T(8,128)(2,1)S(1)} collective-permute-done((bf16[128,3072]{1,0:T(8,128)(2,1)S(1)}, bf16[128,3072]{1,0:T(8,128)(2,1)S(1)}, u32[]{:S(2)}, u32[]{:S(2)}) %collective-permute-start.1) | collective-permute-done | bytes 786464 | tf_op jit(solution)/shard_map/ppermute | solution.py:23
  62.9 6.7 %collective-permute-start.2 = (bf16[128,3072]{1,0:T(8,128)(2,1)S(1)}, bf16[128,3072]{1,0:T(8,128)(2,1)S(1)}, u32[]{:S(2)}, u32[]{:S(2)}) collective-permute-start(bf16[128,3072]{1,0:T(8,128)(2,1)S(1)} %collective-permute-done.1.n2), channel_id=1, source_target_pairs={{0,1},{1,0},{2,3},{3,2},{4,5},{5,4},{6,7},{7,6},{8,9},{9,8},{10,11... | collective-permute-start | bytes 2359304 | tf_op jit(solution)/shard_map/ppermute | solution.py:23
  69.6 4.8 %all-gather.10.cloned.1.call-done = bf16[16,48,896]{2,1,0:T(8,128)(2,1)} async-done(((bf16[2,48,896]{2,1,0:T(8,128)(2,1)}), bf16[16,48,896]{2,1,0:T(8,128)(2,1)}) %all-gather.10.cloned.1.call-update) | async-done | bytes 1376272 | tf_op jit(solution)/shard_map/all_gather | solution.py:316
  74.5 1.9 fusion.28
  76.4 3.1 %collective-permute-start.11 = (bf16[8,2,48,256]{3,2,1,0:T(8,128)(2,1)}, bf16[8,2,48,256]{3,2,1,0:T(8,128)(2,1)}, u32[]{:S(2)}, u32[]{:S(2)}) collective-permute-start(bf16[8,2,48,256]{3,2,1,0:T(8,128)(2,1)} %get-tuple-element.13.b0), channel_id=1, source_target_pairs={{0,8},{8,16},{16,24},{24,0},{1,9},{9,17},{17,25},{25,1},{2,10},{10... | collective-permute-start | bytes 1179656 | tf_op jit(solution)/shard_map/ppermute | solution.py:23
  79.5 3.4 %collective-permute-start.12 = (bf16[8,2,48,256]{3,2,1,0:T(8,128)(2,1)}, bf16[8,2,48,256]{3,2,1,0:T(8,128)(2,1)}, u32[]{:S(2)}, u32[]{:S(2)}) collective-permute-start(bf16[8,2,48,256]{3,2,1,0:T(8,128)(2,1)} %get-tuple-element.13.b0), channel_id=1, source_target_pairs={{0,24},{8,0},{16,8},{24,16},{1,25},{9,1},{17,9},{25,17},{2,26},{10... | collective-permute-start | bytes 1179656 | tf_op jit(solution)/shard_map/ppermute | solution.py:23
  82.9 3.1 %collective-permute-start.8 = (bf16[8,2,48,256]{3,2,1,0:T(8,128)(2,1)S(1)}, bf16[8,2,48,256]{3,2,1,0:T(8,128)(2,1)}, u32[]{:S(2)}, u32[]{:S(2)}) collective-permute-start(bf16[8,2,48,256]{3,2,1,0:T(8,128)(2,1)S(1)} %get-tuple-element.14.b0), channel_id=1, source_target_pairs={{0,24},{8,0},{16,8},{24,16},{1,25},{9,1},{17,9},{25,17},{2,26},{10... | collective-permute-start | bytes 1179656 | tf_op jit(solution)/shard_map/ppermute | solution.py:23
  86.4 1.9 collective-permute-start.7
  88.5 1.6 slice.127
  90.1 3.1 %collective-permute-start.13 = (bf16[4,2,48,256]{3,2,1,0:T(8,128)(2,1)}, bf16[4,2,48,256]{3,2,1,0:T(8,128)(2,1)}, u32[]{:S(2)}, u32[]{:S(2)}) collective-permute-start(bf16[4,2,48,256]{3,2,1,0:T(8,128)(2,1)} %slice.127), channel_id=1, source_target_pairs={{0,8},{8,16},{16,24},{24,0},{1,9},{9,17},{17,25},{25,1},{2,10},{10... | collective-permute-start | bytes 589832 | tf_op jit(solution)/shard_map/ppermute | solution.py:23
  93.2 1.6 slice.128
  94.8 3.4 %collective-permute-start.14 = (bf16[4,2,48,256]{3,2,1,0:T(8,128)(2,1)}, bf16[4,2,48,256]{3,2,1,0:T(8,128)(2,1)}, u32[]{:S(2)}, u32[]{:S(2)}) collective-permute-start(bf16[4,2,48,256]{3,2,1,0:T(8,128)(2,1)} %slice.128), channel_id=1, source_target_pairs={{0,24},{8,0},{16,8},{24,16},{1,25},{9,1},{17,9},{25,17},{2,26},{10... | collective-permute-start | bytes 589832 | tf_op jit(solution)/shard_map/ppermute | solution.py:23
  98.8 0.6 fusion.29
  99.3 3.1 %stack.81.where = s32[9]{0:T(128)} concatenate(s32[1]{0:T(128)} %bitcast, s32[1]{0:T(128)} %bitcast.1, s32[1]{0:T(128)} %bitcast.2, s32[1]{0:T(128)} %bitcast.3, s32[1]{0:T(128)} %bitcast.4, s32[1]{0:T(128)} %bitcast.5, s32[1]{0:T(128)} %bitcast.6, s32[1]{0:T(128)} %bitcast.7, s32[1]{0:T(128)} %bitcast.8), dimensions={0} | concatenate | bytes 72 | tf_op jit(solution)/shard_map/stack | solution.py:287
  102.4 0.9 collective-permute-done.14.b4
  103.4 4.8 %key_value.1.own_kv = bf16[512,256]{1,0:T(8,128)(2,1)} custom-call(s32[9]{0:T(128)} %stack.81.where, bf16[128,3072]{1,0:T(8,128)(2,1)} %copy-done.1, bf16[128,3072]{1,0:T(8,128)(2,1)} %copy-done.3, bf16[128,3072]{1,0:T(8,128)(2,1)} %copy-done.2, bf16[128,3072]{1,0:T(8,128)(2,1)} %copy-done.4, bf16[8,2,48,256]{3,2,1,0:T(8,128)(2,1)} %get-tuple-element.13.b0, ...), custom_call_target="tpu_custom_call" | custom-call | tf_op jit(solution)/shard_map/key_value/pallas_call | solution.py:215
  108.2 4.0 %collective-permute-start.15 = (bf16[512,256]{1,0:T(8,128)(2,1)}, bf16[512,256]{1,0:T(8,128)(2,1)S(1)}, u32[]{:S(2)}, u32[]{:S(2)}) collective-permute-start(bf16[512,256]{1,0:T(8,128)(2,1)} %key_value.1.own_kv), channel_id=1, source_target_pairs={{0,2},{2,4},{4,6},{6,0},{1,3},{3,5},{5,7},{7,1},{8,10},{10,12},{12... | collective-permute-start | bytes 786440 | tf_op jit(solution)/shard_map/ppermute | solution.py:23
  112.5 0.9 slice.125
  113.4 4.6 %collective-permute-start.10 = (bf16[4,2,48,256]{3,2,1,0:T(8,128)(2,1)S(1)}, bf16[4,2,48,256]{3,2,1,0:T(8,128)(2,1)S(1)}, u32[]{:S(2)}, u32[]{:S(2)}) collective-permute-start(bf16[4,2,48,256]{3,2,1,0:T(8,128)(2,1)S(1)} %slice.125), channel_id=1, source_target_pairs={{0,24},{8,0},{16,8},{24,16},{1,25},{9,1},{17,9},{25,17},{2,26},{10... | collective-permute-start | bytes 589832 | tf_op jit(solution)/shard_map/ppermute | solution.py:23
  118.1 0.9 slice.124
  119.0 1.9 collective-permute-start.9
  120.9 1.3 fusion.27
  122.3 4.7 %collective-permute-done.9.b3 = bf16[4,2,48,256]{3,2,1,0:T(8,128)(2,1)S(1)} collective-permute-done((bf16[4,2,48,256]{3,2,1,0:T(8,128)(2,1)S(1)}, bf16[4,2,48,256]{3,2,1,0:T(8,128)(2,1)S(1)}, u32[]{:S(2)}, u32[]{:S(2)}) %collective-permute-start.9) | collective-permute-done | bytes 196640 | tf_op jit(solution)/shard_map/ppermute | solution.py:23
  127.0 0.6 all-gather.8.cloned.1.call-done
  127.8 11.2 %attend.1.a0 = bf16[512,768]{1,0:T(8,128)(2,1)} custom-call(s32[9]{0:T(128)} %stack.81.where, bf16[128,3072]{1,0:T(8,128)(2,1)} %copy-done.1, bf16[128,3072]{1,0:T(8,128)(2,1)} %copy-done.3, bf16[128,3072]{1,0:T(8,128)(2,1)} %copy-done.2, bf16[128,3072]{1,0:T(8,128)(2,1)} %copy-done.4, bf16[8,4,2,48,512]{4,3,2,1,0:T(8,128)(2,1)} %bitcast.63, ...), custom_call_target="tpu_custom_call" | custom-call | tf_op jit(solution)/shard_map/attend/pallas_call | solution.py:231
  139.0 3.1 %collective-permute-start.17 = (bf16[512,768]{1,0:T(8,128)(2,1)}, bf16[512,768]{1,0:T(8,128)(2,1)S(1)}, u32[]{:S(2)}, u32[]{:S(2)}) collective-permute-start(bf16[512,768]{1,0:T(8,128)(2,1)} %attend.1.a0), channel_id=1, source_target_pairs={{0,256},{256,0},{1,257},{257,1},{2,258},{258,2},{3,259},{259,3},{4... | collective-permute-start | bytes 2359304 | tf_op jit(solution)/shard_map/ppermute | solution.py:23
  142.4 1.1 slice.130.b0
  143.6 2.9 %collective-permute-start.19 = (bf16[8,2,48,384]{3,2,1,0:T(8,128)(2,1)S(1)}, bf16[8,2,48,384]{3,2,1,0:T(8,128)(2,1)S(1)}, u32[]{:S(2)}, u32[]{:S(2)}) collective-permute-start(bf16[8,2,48,384]{3,2,1,0:T(8,128)(2,1)S(1)} %slice.130.b0), channel_id=1, source_target_pairs={{0,8},{8,16},{16,24},{24,0},{1,9},{9,17},{17,25},{25,1},{2,10},{10... | collective-permute-start | bytes 1769480 | tf_op jit(solution)/shard_map/ppermute | solution.py:23
  146.5 3.6 %collective-permute-start.20 = (bf16[8,2,48,384]{3,2,1,0:T(8,128)(2,1)S(1)}, bf16[8,2,48,384]{3,2,1,0:T(8,128)(2,1)S(1)}, u32[]{:S(2)}, u32[]{:S(2)}) collective-permute-start(bf16[8,2,48,384]{3,2,1,0:T(8,128)(2,1)S(1)} %slice.130.b0), channel_id=1, source_target_pairs={{0,24},{8,0},{16,8},{24,16},{1,25},{9,1},{17,9},{25,17},{2,26},{10... | collective-permute-start | bytes 1769480 | tf_op jit(solution)/shard_map/ppermute | solution.py:23
  150.1 11.4 %collective-permute-start.16 = (bf16[512,768]{1,0:T(8,128)(2,1)}, bf16[512,768]{1,0:T(8,128)(2,1)S(1)}, u32[]{:S(2)}, u32[]{:S(2)}) collective-permute-start(bf16[512,768]{1,0:T(8,128)(2,1)} %attend.1.a0), channel_id=1, source_target_pairs={{0,1},{1,0},{2,3},{3,2},{4,5},{5,4},{6,7},{7,6},{8,9},{9,8},{10,11... | collective-permute-start | bytes 2359304 | tf_op jit(solution)/shard_map/ppermute | solution.py:23
  161.5 2.1 collective-permute-start.18
  163.8 0.8 slice.131
  164.6 2.2 collective-permute-start.21
  166.9 0.8 slice.132
  167.7 4.2 %collective-permute-start.22 = (bf16[4,2,48,384]{3,2,1,0:T(8,128)(2,1)}, bf16[4,2,48,384]{3,2,1,0:T(8,128)(2,1)}, u32[]{:S(2)}, u32[]{:S(2)}) collective-permute-start(bf16[4,2,48,384]{3,2,1,0:T(8,128)(2,1)} %slice.132), channel_id=1, source_target_pairs={{0,24},{8,0},{16,8},{24,16},{1,25},{9,1},{17,9},{25,17},{2,26},{10... | collective-permute-start | bytes 884744 | tf_op jit(solution)/shard_map/ppermute | solution.py:23
  172.1 2.8 %collective-permute-done.21.b3 = bf16[4,2,48,384]{3,2,1,0:T(8,128)(2,1)} collective-permute-done((bf16[4,2,48,384]{3,2,1,0:T(8,128)(2,1)}, bf16[4,2,48,384]{3,2,1,0:T(8,128)(2,1)}, u32[]{:S(2)}, u32[]{:S(2)}) %collective-permute-start.21) | collective-permute-done | bytes 294944 | tf_op jit(solution)/shard_map/ppermute | solution.py:23
  174.9 2.2 collective-permute-done.22.b4
  177.1 0.8 copy-done.11
  178.0 7.8 %project_output.1 = (bf16[256,384]{1,0:T(8,128)(2,1)}, bf16[256,384]{1,0:T(8,128)(2,1)}, bf16[256,384]{1,0:T(8,128)(2,1)}, bf16[256,384]{1,0:T(8,128)(2,1)}) custom-call(s32[9]{0:T(128)} %stack.81.where, bf16[512,768]{1,0:T(8,128)(2,1)} %attend.1.a0, bf16[512,768]{1,0:T(8,128)(2,1)} %copy-done.11, bf16[512,768]{1,0:T(8,128)(2,1)} %copy-done.10, ...), custom_call_target="tpu_custom_call" | custom-call | tf_op jit(solution)/shard_map/project_output/pallas_call | solution.py:249
  185.8 7.5 %collective-permute-start.25 = (bf16[256,384]{1,0:T(8,128)(2,1)}, bf16[256,384]{1,0:T(8,128)(2,1)S(1)}, u32[]{:S(2)}, u32[]{:S(2)}) collective-permute-start(bf16[256,384]{1,0:T(8,128)(2,1)} %get-tuple-element.11), channel_id=1, source_target_pairs={{0,256},{1,258},{2,257},{3,259},{4,0},{5,2},{6,1},{7,3},{256,260},... | collective-permute-start | bytes 589832 | tf_op jit(solution)/shard_map/ppermute | solution.py:337
  193.4 2.9 %collective-permute-start.26 = (bf16[256,384]{1,0:T(8,128)(2,1)}, bf16[256,384]{1,0:T(8,128)(2,1)S(1)}, u32[]{:S(2)}, u32[]{:S(2)}) collective-permute-start(bf16[256,384]{1,0:T(8,128)(2,1)} %get-tuple-element.12), channel_id=1, source_target_pairs={{0,257},{1,259},{2,256},{3,258},{4,1},{5,3},{6,0},{7,2},{256,261},... | collective-permute-start | bytes 589832 | tf_op jit(solution)/shard_map/ppermute | solution.py:337
  196.3 4.6 %collective-permute-start.23 = (bf16[256,384]{1,0:T(8,128)(2,1)}, bf16[256,384]{1,0:T(8,128)(2,1)S(1)}, u32[]{:S(2)}, u32[]{:S(2)}) collective-permute-start(bf16[256,384]{1,0:T(8,128)(2,1)} %get-tuple-element.9), channel_id=1, source_target_pairs={{0,0},{1,2},{2,1},{3,3},{4,256},{5,258},{6,257},{7,259},{256,4},{2... | collective-permute-start | bytes 589832 | tf_op jit(solution)/shard_map/ppermute | solution.py:337
  200.9 1.9 collective-permute-start.24
  203.0 4.6 %collective-permute-done.26 = bf16[256,384]{1,0:T(8,128)(2,1)S(1)} collective-permute-done((bf16[256,384]{1,0:T(8,128)(2,1)}, bf16[256,384]{1,0:T(8,128)(2,1)S(1)}, u32[]{:S(2)}, u32[]{:S(2)}) %collective-permute-start.26) | collective-permute-done | bytes 196640 | tf_op jit(solution)/shard_map/ppermute | solution.py:337
  207.8 3.1 %collective-permute-start.28 = (bf16[2,256,384]{2,1,0:T(8,128)(2,1)S(1)}, bf16[2,256,384]{2,1,0:T(8,128)(2,1)S(1)}, u32[]{:S(2)}, u32[]{:S(2)}) collective-permute-start(bf16[2,256,384]{2,1,0:T(8,128)(2,1)S(1)} %pad_maximum_fusion.2), channel_id=1, source_target_pairs={{0,8},{8,16},{16,24},{24,32},{32,40},{40,48},{48,56},{56,64},{64,7... | collective-permute-start | bytes 1179656 | tf_op jit(solution)/shard_map/ppermute | solution.py:362
  211.1 0.6 collective-permute-done.24
  211.9 1.9 collective-permute-start.27
  214.1 24.0 %collective-permute-done.27 = bf16[2,256,384]{2,1,0:T(8,128)(2,1)S(1)} collective-permute-done((bf16[2,256,384]{2,1,0:T(8,128)(2,1)S(1)}, bf16[2,256,384]{2,1,0:T(8,128)(2,1)S(1)}, u32[]{:S(2)}, u32[]{:S(2)}) %collective-permute-start.27) | collective-permute-done | bytes 393248 | tf_op jit(solution)/shard_map/ppermute | solution.py:362
  238.4 1.1 copy-done.15
  239.6 0.7 bitcast_dynamic-update-slice_fusion
  (100 shorter events, 4.3 us)
Async XLA Ops:
  6.5 105.7 %copy-start = (s32[64,3]{0,1:T(4,128)S(1)}, s32[64,3]{0,1:T(4,128)}, u32[]{:S(2)}) copy-start(s32[64,3]{0,1:T(4,128)} %param.15) | copy-start | bytes 2308
  6.5 67.9 %all-gather.10.cloned.1.call-start = ((), (), s32[]{:S(2)}) async-start(), calls=%async_computation.1 | async-start | bytes 1548288 | tf_op jit(solution)/shard_map/all_gather | solution.py:316
  8.1 17.1 %collective-permute-start.4 = (bf16[48,896]{1,0:T(8,128)(2,1)S(1)}, bf16[48,896]{1,0:T(8,128)(2,1)S(1)}, u32[]{:S(2)}, u32[]{:S(2)}) collective-permute-start(bf16[48,896]{1,0:T(8,128)(2,1)S(1)} %pad_maximum_fusion.4), channel_id=1, source_target_pairs={{0,2},{1,0},{2,3},{3,1},{4,258},{5,256},{6,259},{7,257},{256,6},{2... | collective-permute-start | bytes 258056 | tf_op jit(solution)/shard_map/ppermute | solution.py:297
  16.9 8.3 %collective-permute-start.5 = (bf16[48,896]{1,0:T(8,128)(2,1)S(1)}, bf16[48,896]{1,0:T(8,128)(2,1)S(1)}, u32[]{:S(2)}, u32[]{:S(2)}) collective-permute-start(bf16[48,896]{1,0:T(8,128)(2,1)S(1)} %pad_maximum_fusion.4), channel_id=1, source_target_pairs={{0,4},{1,6},{2,5},{3,7},{4,260},{5,262},{6,261},{7,263},{256,0},{2... | collective-permute-start | bytes 258056 | tf_op jit(solution)/shard_map/ppermute | solution.py:297
  18.8 8.4 %collective-permute-start.6 = (bf16[48,896]{1,0:T(8,128)(2,1)S(1)}, bf16[48,896]{1,0:T(8,128)(2,1)S(1)}, u32[]{:S(2)}, u32[]{:S(2)}) collective-permute-start(bf16[48,896]{1,0:T(8,128)(2,1)S(1)} %pad_maximum_fusion.4), channel_id=1, source_target_pairs={{0,6},{1,4},{2,7},{3,5},{4,262},{5,260},{6,263},{7,261},{256,2},{2... | collective-permute-start | bytes 258056 | tf_op jit(solution)/shard_map/ppermute | solution.py:297
  22.2 7.4 %collective-permute-start.3 = (bf16[48,896]{1,0:T(8,128)(2,1)S(1)}, bf16[48,896]{1,0:T(8,128)(2,1)S(1)}, u32[]{:S(2)}, u32[]{:S(2)}) collective-permute-start(bf16[48,896]{1,0:T(8,128)(2,1)S(1)} %pad_maximum_fusion.4), channel_id=1, source_target_pairs={{0,0},{1,2},{2,1},{3,3},{4,256},{5,258},{6,257},{7,259},{256,4},{2... | collective-permute-start | bytes 258056 | tf_op jit(solution)/shard_map/ppermute | solution.py:297
  29.8 13.0 %copy-start.16 = (bf16[3072]{0:T(1024)(128)(2,1)S(1)}, bf16[3072]{0:T(1024)(128)(2,1)}, u32[]{:S(2)}) copy-start(bf16[3072]{0:T(1024)(128)(2,1)} %param.9) | copy-start | bytes 18436
  29.8 13.0 %copy-start.5 = (bf16[128,3072]{1,0:T(8,128)(2,1)S(1)}, bf16[128,3072]{1,0:T(8,128)(2,1)}, u32[]{:S(2)}) copy-start(bf16[128,3072]{1,0:T(8,128)(2,1)} %param.8) | copy-start | bytes 2359300
  30.5 97.1 %all-gather.8.cloned.1.call-start = ((), (), s32[]{:S(2)}) async-start(), calls=%async_computation | async-start | bytes 3538944 | tf_op jit(solution)/shard_map/all_gather | solution.py:317
  42.7 134.4 %all-gather.12.cloned.1.call-start = ((), (), s32[]{:S(2)}) async-start(), calls=%async_computation.2 | async-start | bytes 2654208 | tf_op jit(solution)/shard_map/all_gather | solution.py:318
  43.8 44.6 %copy-start.17 = (s32[64,3]{0,1:T(4,128)S(1)}, s32[64,3]{0,1:T(4,128)}, u32[]{:S(2)}) copy-start(s32[64,3]{0,1:T(4,128)} %param.14) | copy-start | bytes 2308
  44.1 59.3 %copy-start.1 = (bf16[128,3072]{1,0:T(8,128)(2,1)}, bf16[128,3072]{1,0:T(8,128)(2,1)S(1)}, u32[]{:S(2)}) copy-start(bf16[128,3072]{1,0:T(8,128)(2,1)S(1)} %fusion.2.n0) | copy-start | bytes 2359300
  44.1 18.8 %collective-permute-start.1 = (bf16[128,3072]{1,0:T(8,128)(2,1)S(1)}, bf16[128,3072]{1,0:T(8,128)(2,1)S(1)}, u32[]{:S(2)}, u32[]{:S(2)}) collective-permute-start(bf16[128,3072]{1,0:T(8,128)(2,1)S(1)} %fusion.2.n0), channel_id=1, source_target_pairs={{0,256},{256,0},{1,257},{257,1},{2,258},{258,2},{3,259},{259,3},{4... | collective-permute-start | bytes 2359304 | tf_op jit(solution)/shard_map/ppermute | solution.py:23
  49.3 45.5 %collective-permute-start = (bf16[128,3072]{1,0:T(8,128)(2,1)S(1)}, bf16[128,3072]{1,0:T(8,128)(2,1)S(1)}, u32[]{:S(2)}, u32[]{:S(2)}) collective-permute-start(bf16[128,3072]{1,0:T(8,128)(2,1)S(1)} %fusion.2.n0), channel_id=1, source_target_pairs={{0,1},{1,0},{2,3},{3,2},{4,5},{5,4},{6,7},{7,6},{8,9},{9,8},{10,11... | collective-permute-start | bytes 2359304 | tf_op jit(solution)/shard_map/ppermute | solution.py:23
  62.9 40.4 %copy-start.2 = (bf16[128,3072]{1,0:T(8,128)(2,1)}, bf16[128,3072]{1,0:T(8,128)(2,1)S(1)}, u32[]{:S(2)}) copy-start(bf16[128,3072]{1,0:T(8,128)(2,1)S(1)} %collective-permute-done.1.n2) | copy-start | bytes 2359300
  62.9 39.5 %collective-permute-start.2 = (bf16[128,3072]{1,0:T(8,128)(2,1)S(1)}, bf16[128,3072]{1,0:T(8,128)(2,1)S(1)}, u32[]{:S(2)}, u32[]{:S(2)}) collective-permute-start(bf16[128,3072]{1,0:T(8,128)(2,1)S(1)} %collective-permute-done.1.n2), channel_id=1, source_target_pairs={{0,1},{1,0},{2,3},{3,2},{4,5},{5,4},{6,7},{7,6},{8,9},{9,8},{10,11... | collective-permute-start | bytes 2359304 | tf_op jit(solution)/shard_map/ppermute | solution.py:23
  76.4 31.8 %copy-start.7 = (bf16[8,2,48,256]{3,2,1,0:T(8,128)(2,1)}, bf16[8,2,48,256]{3,2,1,0:T(8,128)(2,1)S(1)}, u32[]{:S(2)}) copy-start(bf16[8,2,48,256]{3,2,1,0:T(8,128)(2,1)S(1)} %get-tuple-element.14.b0) | copy-start | bytes 1179652
  76.4 10.0 %collective-permute-start.11 = (bf16[8,2,48,256]{3,2,1,0:T(8,128)(2,1)}, bf16[8,2,48,256]{3,2,1,0:T(8,128)(2,1)}, u32[]{:S(2)}, u32[]{:S(2)}) collective-permute-start(bf16[8,2,48,256]{3,2,1,0:T(8,128)(2,1)} %get-tuple-element.13.b0), channel_id=1, source_target_pairs={{0,8},{8,16},{16,24},{24,0},{1,9},{9,17},{17,25},{25,1},{2,10},{10... | collective-permute-start | bytes 1179656 | tf_op jit(solution)/shard_map/ppermute | solution.py:23
  79.5 10.6 %collective-permute-start.12 = (bf16[8,2,48,256]{3,2,1,0:T(8,128)(2,1)}, bf16[8,2,48,256]{3,2,1,0:T(8,128)(2,1)}, u32[]{:S(2)}, u32[]{:S(2)}) collective-permute-start(bf16[8,2,48,256]{3,2,1,0:T(8,128)(2,1)} %get-tuple-element.13.b0), channel_id=1, source_target_pairs={{0,24},{8,0},{16,8},{24,16},{1,25},{9,1},{17,9},{25,17},{2,26},{10... | collective-permute-start | bytes 1179656 | tf_op jit(solution)/shard_map/ppermute | solution.py:23
  82.9 29.6 %collective-permute-start.8 = (bf16[8,2,48,256]{3,2,1,0:T(8,128)(2,1)S(1)}, bf16[8,2,48,256]{3,2,1,0:T(8,128)(2,1)}, u32[]{:S(2)}, u32[]{:S(2)}) collective-permute-start(bf16[8,2,48,256]{3,2,1,0:T(8,128)(2,1)S(1)} %get-tuple-element.14.b0), channel_id=1, source_target_pairs={{0,24},{8,0},{16,8},{24,16},{1,25},{9,1},{17,9},{25,17},{2,26},{10... | collective-permute-start | bytes 1179656 | tf_op jit(solution)/shard_map/ppermute | solution.py:23
  86.4 31.6 %collective-permute-start.7 = (bf16[8,2,48,256]{3,2,1,0:T(8,128)(2,1)S(1)}, bf16[8,2,48,256]{3,2,1,0:T(8,128)(2,1)}, u32[]{:S(2)}, u32[]{:S(2)}) collective-permute-start(bf16[8,2,48,256]{3,2,1,0:T(8,128)(2,1)S(1)} %get-tuple-element.14.b0), channel_id=1, source_target_pairs={{0,8},{8,16},{16,24},{24,0},{1,9},{9,17},{17,25},{25,1},{2,10},{10... | collective-permute-start | bytes 1179656 | tf_op jit(solution)/shard_map/ppermute | solution.py:23
  90.1 12.3 %collective-permute-start.13 = (bf16[4,2,48,256]{3,2,1,0:T(8,128)(2,1)}, bf16[4,2,48,256]{3,2,1,0:T(8,128)(2,1)}, u32[]{:S(2)}, u32[]{:S(2)}) collective-permute-start(bf16[4,2,48,256]{3,2,1,0:T(8,128)(2,1)} %slice.127), channel_id=1, source_target_pairs={{0,8},{8,16},{16,24},{24,0},{1,9},{9,17},{17,25},{25,1},{2,10},{10... | collective-permute-start | bytes 589832 | tf_op jit(solution)/shard_map/ppermute | solution.py:23
  94.8 8.6 %copy-start.3 = (bf16[128,3072]{1,0:T(8,128)(2,1)}, bf16[128,3072]{1,0:T(8,128)(2,1)S(1)}, u32[]{:S(2)}) copy-start(bf16[128,3072]{1,0:T(8,128)(2,1)S(1)} %collective-permute-done.n1) | copy-start | bytes 2359300
  94.8 8.6 %collective-permute-start.14 = (bf16[4,2,48,256]{3,2,1,0:T(8,128)(2,1)}, bf16[4,2,48,256]{3,2,1,0:T(8,128)(2,1)}, u32[]{:S(2)}, u32[]{:S(2)}) collective-permute-start(bf16[4,2,48,256]{3,2,1,0:T(8,128)(2,1)} %slice.128), channel_id=1, source_target_pairs={{0,24},{8,0},{16,8},{24,16},{1,25},{9,1},{17,9},{25,17},{2,26},{10... | collective-permute-start | bytes 589832 | tf_op jit(solution)/shard_map/ppermute | solution.py:23
  102.4 1.0 copy-start.4
  108.2 18.8 %collective-permute-start.15 = (bf16[512,256]{1,0:T(8,128)(2,1)}, bf16[512,256]{1,0:T(8,128)(2,1)S(1)}, u32[]{:S(2)}, u32[]{:S(2)}) collective-permute-start(bf16[512,256]{1,0:T(8,128)(2,1)} %key_value.1.own_kv), channel_id=1, source_target_pairs={{0,2},{2,4},{4,6},{6,0},{1,3},{3,5},{5,7},{7,1},{8,10},{10,12},{12... | collective-permute-start | bytes 786440 | tf_op jit(solution)/shard_map/ppermute | solution.py:23
  113.4 8.9 %collective-permute-start.10 = (bf16[4,2,48,256]{3,2,1,0:T(8,128)(2,1)S(1)}, bf16[4,2,48,256]{3,2,1,0:T(8,128)(2,1)S(1)}, u32[]{:S(2)}, u32[]{:S(2)}) collective-permute-start(bf16[4,2,48,256]{3,2,1,0:T(8,128)(2,1)S(1)} %slice.125), channel_id=1, source_target_pairs={{0,24},{8,0},{16,8},{24,16},{1,25},{9,1},{17,9},{25,17},{2,26},{10... | collective-permute-start | bytes 589832 | tf_op jit(solution)/shard_map/ppermute | solution.py:23
  119.0 8.0 %collective-permute-start.9 = (bf16[4,2,48,256]{3,2,1,0:T(8,128)(2,1)S(1)}, bf16[4,2,48,256]{3,2,1,0:T(8,128)(2,1)S(1)}, u32[]{:S(2)}, u32[]{:S(2)}) collective-permute-start(bf16[4,2,48,256]{3,2,1,0:T(8,128)(2,1)S(1)} %slice.124), channel_id=1, source_target_pairs={{0,8},{8,16},{16,24},{24,0},{1,9},{9,17},{17,25},{25,1},{2,10},{10... | collective-permute-start | bytes 589832 | tf_op jit(solution)/shard_map/ppermute | solution.py:23
  122.3 5.3 %copy-start.13 = (bf16[4,2,48,256]{3,2,1,0:T(8,128)(2,1)}, bf16[4,2,48,256]{3,2,1,0:T(8,128)(2,1)S(1)}, u32[]{:S(2)}) copy-start(bf16[4,2,48,256]{3,2,1,0:T(8,128)(2,1)S(1)} %collective-permute-done.10.b4) | copy-start | bytes 589828
  127.0 0.7 copy-start.14
  127.0 0.8 copy-start.12
  139.0 22.5 %collective-permute-start.17 = (bf16[512,768]{1,0:T(8,128)(2,1)}, bf16[512,768]{1,0:T(8,128)(2,1)S(1)}, u32[]{:S(2)}, u32[]{:S(2)}) collective-permute-start(bf16[512,768]{1,0:T(8,128)(2,1)} %attend.1.a0), channel_id=1, source_target_pairs={{0,256},{256,0},{1,257},{257,1},{2,258},{258,2},{3,259},{259,3},{4... | collective-permute-start | bytes 2359304 | tf_op jit(solution)/shard_map/ppermute | solution.py:23
  143.6 33.5 %copy-start.6 = (bf16[8,2,48,384]{3,2,1,0:T(8,128)(2,1)}, bf16[8,2,48,384]{3,2,1,0:T(8,128)(2,1)S(1)}, u32[]{:S(2)}) copy-start(bf16[8,2,48,384]{3,2,1,0:T(8,128)(2,1)S(1)} %slice.130.b0) | copy-start | bytes 1769476
  143.6 20.2 %collective-permute-start.19 = (bf16[8,2,48,384]{3,2,1,0:T(8,128)(2,1)S(1)}, bf16[8,2,48,384]{3,2,1,0:T(8,128)(2,1)S(1)}, u32[]{:S(2)}, u32[]{:S(2)}) collective-permute-start(bf16[8,2,48,384]{3,2,1,0:T(8,128)(2,1)S(1)} %slice.130.b0), channel_id=1, source_target_pairs={{0,8},{8,16},{16,24},{24,0},{1,9},{9,17},{17,25},{25,1},{2,10},{10... | collective-permute-start | bytes 1769480 | tf_op jit(solution)/shard_map/ppermute | solution.py:23
  146.5 20.4 %collective-permute-start.20 = (bf16[8,2,48,384]{3,2,1,0:T(8,128)(2,1)S(1)}, bf16[8,2,48,384]{3,2,1,0:T(8,128)(2,1)S(1)}, u32[]{:S(2)}, u32[]{:S(2)}) collective-permute-start(bf16[8,2,48,384]{3,2,1,0:T(8,128)(2,1)S(1)} %slice.130.b0), channel_id=1, source_target_pairs={{0,24},{8,0},{16,8},{24,16},{1,25},{9,1},{17,9},{25,17},{2,26},{10... | collective-permute-start | bytes 1769480 | tf_op jit(solution)/shard_map/ppermute | solution.py:23
  150.1 26.9 %collective-permute-start.16 = (bf16[512,768]{1,0:T(8,128)(2,1)}, bf16[512,768]{1,0:T(8,128)(2,1)S(1)}, u32[]{:S(2)}, u32[]{:S(2)}) collective-permute-start(bf16[512,768]{1,0:T(8,128)(2,1)} %attend.1.a0), channel_id=1, source_target_pairs={{0,1},{1,0},{2,3},{3,2},{4,5},{5,4},{6,7},{7,6},{8,9},{9,8},{10,11... | collective-permute-start | bytes 2359304 | tf_op jit(solution)/shard_map/ppermute | solution.py:23
  161.5 15.6 %copy-start.10 = (bf16[512,768]{1,0:T(8,128)(2,1)}, bf16[512,768]{1,0:T(8,128)(2,1)S(1)}, u32[]{:S(2)}) copy-start(bf16[512,768]{1,0:T(8,128)(2,1)S(1)} %collective-permute-done.17.a2) | copy-start | bytes 2359300
  161.5 15.6 %collective-permute-start.18 = (bf16[512,768]{1,0:T(8,128)(2,1)S(1)}, bf16[512,768]{1,0:T(8,128)(2,1)}, u32[]{:S(2)}, u32[]{:S(2)}) collective-permute-start(bf16[512,768]{1,0:T(8,128)(2,1)S(1)} %collective-permute-done.17.a2), channel_id=1, source_target_pairs={{0,1},{1,0},{2,3},{3,2},{4,5},{5,4},{6,7},{7,6},{8,9},{9,8},{10,11... | collective-permute-start | bytes 2359304 | tf_op jit(solution)/shard_map/ppermute | solution.py:23
  163.8 13.3 %copy-start.8 = (bf16[8,2,48,384]{3,2,1,0:T(8,128)(2,1)}, bf16[8,2,48,384]{3,2,1,0:T(8,128)(2,1)S(1)}, u32[]{:S(2)}) copy-start(bf16[8,2,48,384]{3,2,1,0:T(8,128)(2,1)S(1)} %collective-permute-done.19.b1) | copy-start | bytes 1769476
  164.6 10.3 %collective-permute-start.21 = (bf16[4,2,48,384]{3,2,1,0:T(8,128)(2,1)}, bf16[4,2,48,384]{3,2,1,0:T(8,128)(2,1)}, u32[]{:S(2)}, u32[]{:S(2)}) collective-permute-start(bf16[4,2,48,384]{3,2,1,0:T(8,128)(2,1)} %slice.131), channel_id=1, source_target_pairs={{0,8},{8,16},{16,24},{24,0},{1,9},{9,17},{17,25},{25,1},{2,10},{10... | collective-permute-start | bytes 884744 | tf_op jit(solution)/shard_map/ppermute | solution.py:23
  166.9 10.2 %copy-start.9 = (bf16[8,2,48,384]{3,2,1,0:T(8,128)(2,1)}, bf16[8,2,48,384]{3,2,1,0:T(8,128)(2,1)S(1)}, u32[]{:S(2)}) copy-start(bf16[8,2,48,384]{3,2,1,0:T(8,128)(2,1)S(1)} %collective-permute-done.20.b2) | copy-start | bytes 1769476
  167.7 9.4 %collective-permute-start.22 = (bf16[4,2,48,384]{3,2,1,0:T(8,128)(2,1)}, bf16[4,2,48,384]{3,2,1,0:T(8,128)(2,1)}, u32[]{:S(2)}, u32[]{:S(2)}) collective-permute-start(bf16[4,2,48,384]{3,2,1,0:T(8,128)(2,1)} %slice.132), channel_id=1, source_target_pairs={{0,24},{8,0},{16,8},{24,16},{1,25},{9,1},{17,9},{25,17},{2,26},{10... | collective-permute-start | bytes 884744 | tf_op jit(solution)/shard_map/ppermute | solution.py:23
  177.1 0.9 copy-start.11
  185.8 17.1 %collective-permute-start.25 = (bf16[256,384]{1,0:T(8,128)(2,1)}, bf16[256,384]{1,0:T(8,128)(2,1)S(1)}, u32[]{:S(2)}, u32[]{:S(2)}) collective-permute-start(bf16[256,384]{1,0:T(8,128)(2,1)} %get-tuple-element.11), channel_id=1, source_target_pairs={{0,256},{1,258},{2,257},{3,259},{4,0},{5,2},{6,1},{7,3},{256,260},... | collective-permute-start | bytes 589832 | tf_op jit(solution)/shard_map/ppermute | solution.py:337
  193.4 14.2 %collective-permute-start.26 = (bf16[256,384]{1,0:T(8,128)(2,1)}, bf16[256,384]{1,0:T(8,128)(2,1)S(1)}, u32[]{:S(2)}, u32[]{:S(2)}) collective-permute-start(bf16[256,384]{1,0:T(8,128)(2,1)} %get-tuple-element.12), channel_id=1, source_target_pairs={{0,257},{1,259},{2,256},{3,258},{4,1},{5,3},{6,0},{7,2},{256,261},... | collective-permute-start | bytes 589832 | tf_op jit(solution)/shard_map/ppermute | solution.py:337
  196.3 14.6 %collective-permute-start.23 = (bf16[256,384]{1,0:T(8,128)(2,1)}, bf16[256,384]{1,0:T(8,128)(2,1)S(1)}, u32[]{:S(2)}, u32[]{:S(2)}) collective-permute-start(bf16[256,384]{1,0:T(8,128)(2,1)} %get-tuple-element.9), channel_id=1, source_target_pairs={{0,0},{1,2},{2,1},{3,3},{4,256},{5,258},{6,257},{7,259},{256,4},{2... | collective-permute-start | bytes 589832 | tf_op jit(solution)/shard_map/ppermute | solution.py:337
  200.9 10.7 %collective-permute-start.24 = (bf16[256,384]{1,0:T(8,128)(2,1)}, bf16[256,384]{1,0:T(8,128)(2,1)S(1)}, u32[]{:S(2)}, u32[]{:S(2)}) collective-permute-start(bf16[256,384]{1,0:T(8,128)(2,1)} %get-tuple-element.10), channel_id=1, source_target_pairs={{0,1},{1,3},{2,0},{3,2},{4,257},{5,259},{6,256},{7,258},{256,5},{2... | collective-permute-start | bytes 589832 | tf_op jit(solution)/shard_map/ppermute | solution.py:337
  207.8 30.4 %collective-permute-start.28 = (bf16[2,256,384]{2,1,0:T(8,128)(2,1)S(1)}, bf16[2,256,384]{2,1,0:T(8,128)(2,1)S(1)}, u32[]{:S(2)}, u32[]{:S(2)}) collective-permute-start(bf16[2,256,384]{2,1,0:T(8,128)(2,1)S(1)} %pad_maximum_fusion.2), channel_id=1, source_target_pairs={{0,8},{8,16},{16,24},{24,32},{32,40},{40,48},{48,56},{56,64},{64,7... | collective-permute-start | bytes 1179656 | tf_op jit(solution)/shard_map/ppermute | solution.py:362
  211.9 26.3 %collective-permute-start.27 = (bf16[2,256,384]{2,1,0:T(8,128)(2,1)S(1)}, bf16[2,256,384]{2,1,0:T(8,128)(2,1)S(1)}, u32[]{:S(2)}, u32[]{:S(2)}) collective-permute-start(bf16[2,256,384]{2,1,0:T(8,128)(2,1)S(1)} %pad_maximum_fusion.1), channel_id=1, source_target_pairs={{0,8},{8,16},{16,24},{24,32},{32,40},{40,48},{48,56},{56,64},{64,7... | collective-permute-start | bytes 1179656 | tf_op jit(solution)/shard_map/ppermute | solution.py:362
  238.4 1.1 copy-start.15
Sparse Core Ops, SparseCore 0:
  30.6 43.8 all-gather.9
  76.6 50.9 all-gather.7
  129.7 39.8 all-gather.11

commit v2 on v0

v2 whole, which is shorter than its diff:
```python
import functools
import math

import jax
import jax.numpy as jnp
import numpy as np
from jax import lax
from jax.experimental import pallas as pl
from jax.experimental.pallas import tpu as pltpu
from jax.sharding import Mesh, PartitionSpec as P

BLK = 128
EPS = 1e-05
SCALE = 1.0 / math.sqrt(128)
AXES = ("yl", "z", "x", "yh", "c")
SIZES = (2, 8, 4, 4, 2)
EXTENT = dict(zip(AXES, SIZES))
HALF = 512
VMEM = 56 * 1024 * 1024
PARAMS = pltpu.CompilerParams(vmem_limit_bytes=VMEM)
SMEM_SPEC = pl.BlockSpec(memory_space=pltpu.SMEM)
ANY_SPEC = pl.BlockSpec(memory_space=pl.ANY)
VMEM_SPEC = pl.BlockSpec(memory_space=pltpu.VMEM)
PLACES = np.stack(
    [(np.arange(512) // 8) % 4, np.arange(512) // 8], axis=1
).astype(np.int32)


def shift(value, axis, steps):
    count = EXTENT[axis]
    return lax.ppermute(value, axis, [(i, (i + steps) % count) for i in range(count)])


def ring_x(block):
    half = block.shape[0] // 2
    below = shift(block, "x", 1)
    above = shift(block, "x", -1)
    return (
        block,
        below,
        above,
        shift(below[:half], "x", 1),
        shift(above[half:], "x", -1),
    )


def ring_pairs(refs, weight, x):
    pairs = []
    for ref, first, offset in zip(refs, (0, 0, 0, 0, 4), (0, 3, 1, 2, 2)):
        for yl in range(2):
            pairs.append(
                (ref.at[:, yl], weight.at[yl, pl.ds(first, ref.shape[0]), (x + offset) & 3])
            )
    return pairs


def start_all(pairs, sems, first):
    made = []
    for i, (source, target) in enumerate(pairs):
        copy = pltpu.make_async_copy(source, target, sems.at[first + i])
        copy.start()
        made.append(copy)
    return made


def document_of(lengths, shard, block):
    first_end = lengths[shard, 0]
    second_end = first_end + lengths[shard, 1]
    return (block >= first_end).astype(jnp.int32) + (block >= second_end).astype(jnp.int32)


def attention_kernel(
    where, lengths, normed, b0, b1, b2, b3, b4, out, rows, weight, total, qkv, sems
):
    x, shard = where[0], where[1]
    ring = ring_pairs((b0, b1, b2, b3, b4), weight, x)
    made = []
    for yl in range(2):
        pairs = ring[yl::2]
        pairs += [
            (
                normed.at[half * HALF : half * HALF + HALF, yl * 1536 : yl * 1536 + 1536],
                rows.at[yl, half],
            )
            for half in range(2)
        ]
        made.append(start_all(pairs, sems, 7 * yl))
    for yl in range(2):
        for copy in made[yl][:5]:
            copy.wait()
        for half in range(2):
            made[yl][5 + half].wait()
            part = jnp.dot(
                rows[yl, half],
                weight[yl].reshape(1536, 640),
                preferred_element_type=jnp.float32,
            )
            here = slice(half * HALF, half * HALF + HALF)
            if yl == 0:
                total[here] = part
            else:
                qkv[256 + half * HALF : 256 + half * HALF + HALF] = (total[here] + part).astype(
                    jnp.bfloat16
                )
    qkv[0:256] = jnp.zeros((256, 640), jnp.bfloat16)
    row = lax.broadcasted_iota(jnp.int32, (BLK, 3 * BLK), 0)
    column = lax.broadcasted_iota(jnp.int32, (BLK, 3 * BLK), 1)
    causal = (column >= 2 * BLK) & (column - 2 * BLK <= row)
    for block in range(8):
        mine = document_of(lengths, shard, block)
        near, far = (
            (document_of(lengths, shard, block - k) == mine).astype(jnp.int32)
            if block >= k
            else jnp.int32(0)
            for k in (1, 2)
        )
        open_before = jnp.where(column < BLK, far, near)
        allowed = causal | ((column < 2 * BLK) & (open_before == 1))
        at = block * BLK
        window = slice(at, at + 3 * BLK)
        own = slice(at + 2 * BLK, at + 3 * BLK)
        stacked = jnp.concatenate(
            [qkv[own, 256 + i * 128 : 384 + i * 128] for i in range(3)], axis=0
        )
        scores = (
            lax.dot_general(
                stacked,
                qkv[window, 0:128],
                (((1,), (1,)), ((), ())),
                preferred_element_type=jnp.float32,
            )
            * SCALE
        )
        scores = jnp.where(allowed[None], scores.reshape(3, BLK, 3 * BLK), -jnp.inf)
        exponent = jnp.exp(scores - jnp.max(scores, axis=-1, keepdims=True))
        row_total = jnp.sum(exponent, axis=-1, keepdims=True)
        mixed = jnp.dot(
            exponent.astype(jnp.bfloat16).reshape(3 * BLK, 3 * BLK),
            qkv[window, 128:256],
            preferred_element_type=jnp.float32,
        )
        mixed = (mixed / row_total.reshape(3 * BLK, 1)).astype(jnp.bfloat16)
        for i in range(3):
            out[at : at + BLK, i * 128 : i * 128 + 128] = mixed[i * BLK : i * BLK + BLK]


def attend(where, lengths, normed, ring):
    return pl.pallas_call(
        attention_kernel,
        out_shape=jax.ShapeDtypeStruct((2 * HALF, 384), jnp.bfloat16),
        in_specs=[SMEM_SPEC] * 2 + [ANY_SPEC] * 6,
        out_specs=VMEM_SPEC,
        scratch_shapes=[
            pltpu.VMEM((2, 2, HALF, 1536), jnp.bfloat16),
            pltpu.VMEM((2, 8, 4, 48, 640), jnp.bfloat16),
            pltpu.VMEM((2 * HALF, 640), jnp.float32),
            pltpu.VMEM((256 + 2 * HALF, 640), jnp.bfloat16),
            pltpu.SemaphoreType.DMA((14,)),
        ],
        compiler_params=PARAMS,
        name="attend",
    )(where, lengths, normed, *ring)


def output_kernel(
    half, where, lengths, dest, heads, b0, b1, b2, b3, b4, stay, leave, rows, weight, sems
):
    x, shard = where[0], where[1]
    made = start_all(ring_pairs((b0, b1, b2, b3, b4), weight, x), sems, 0)
    parts = start_all(
        [(heads.at[t, pl.ds(half * HALF, HALF)], rows.at[t]) for t in range(8)], sems, 10
    )
    for copy in made:
        copy.wait()
    total = jnp.zeros((HALF, 384), jnp.float32)
    for t in range(8):
        parts[t].wait()
        part = weight[t >> 2, 2 * (t & 3) : 2 * (t & 3) + 2]
        total = total + jnp.dot(
            rows[t], part.reshape(384, 384), preferred_element_type=jnp.float32
        )
    for j in range(4):
        document = document_of(lengths, shard, 4 * half + j)
        target = jnp.where(
            document == 0,
            dest[shard, 0],
            jnp.where(document == 1, dest[shard, 1], dest[shard, 2]),
        )
        moved = (target != shard).astype(jnp.float32)
        here = slice(j * BLK, j * BLK + BLK)
        stay[here] = (total[here] * (1.0 - moved)).astype(jnp.bfloat16)
        leave[here] = (total[here] * moved).astype(jnp.bfloat16)


def project_output(half, where, lengths, dest, heads, ring):
    piece = jax.ShapeDtypeStruct((HALF, 384), jnp.bfloat16)
    return pl.pallas_call(
        functools.partial(output_kernel, half),
        out_shape=(piece, piece),
        in_specs=[SMEM_SPEC] * 3 + [ANY_SPEC] * 6,
        out_specs=(VMEM_SPEC, VMEM_SPEC),
        scratch_shapes=[
            pltpu.VMEM((8, HALF, 384), jnp.bfloat16),
            pltpu.VMEM((2, 8, 4, 48, 384), jnp.bfloat16),
            pltpu.SemaphoreType.DMA((18,)),
        ],
        compiler_params=PARAMS,
        name="project_output",
    )(where, lengths, dest, heads, *ring)


def shards(
    activations,
    norm_gain,
    query_weight,
    key_weight,
    value_matrix,
    output_weight,
    document_lengths,
    doc_dest,
):
    yh = lax.axis_index("yh")
    where = lax.dynamic_index_in_dim(
        jnp.asarray(PLACES), lax.axis_index(AXES), 0, keepdims=False
    )

    inputs = activations.astype(jnp.float32)
    mean_square = jnp.mean(inputs * inputs, axis=1, keepdims=True)
    normed = (inputs * lax.rsqrt(mean_square + EPS) * norm_gain.astype(jnp.float32)).astype(
        jnp.bfloat16
    )
    gathered = lax.all_gather(normed, ("yh", "c"), axis=0, tiled=True)

    packed = jnp.concatenate(
        [
            lax.dynamic_slice_in_dim(key_weight, yh * 128, 128, 1),
            lax.dynamic_slice_in_dim(value_matrix, yh * 128, 128, 1),
            query_weight,
            output_weight,
        ],
        axis=1,
    )
    packed = lax.all_gather(packed, "yl", axis=0, tiled=False)
    ring = ring_x(lax.all_gather(packed[..., 0:640], "z", axis=0, tiled=False))

    attention = attend(where, document_lengths, gathered, ring)
    heads = lax.all_gather(attention, ("yh", "c"), axis=0, tiled=False)

    columns = lax.optimization_barrier((packed[..., 640:1024], attention))[0]
    ring = ring_x(lax.all_gather(columns, "z", axis=0, tiled=False))
    pairs = [(i, (i + 1) % 64) for i in range(64)]
    staying, arrived = [], []
    for half in range(2):
        stay, leave = project_output(half, where, document_lengths, doc_dest, heads, ring)
        staying.append(stay)
        arrived.append(lax.ppermute(leave, ("yl", "z", "x"), pairs))
    return jnp.concatenate(staying + arrived, axis=0)


def solution(mesh):
    fine = Mesh(np.asarray(mesh.devices).reshape(SIZES), AXES)
    dp, tensor = ("yl", "z", "x"), ("yh", "c")
    in_specs = (
        P(dp + tensor, None),
        P(),
        P(dp, tensor),
        P(dp, None),
        P(dp, None),
        P(dp, tensor),
        P(),
        P(),
    )
    return jax.shard_map(
        shards, mesh=fine, in_specs=in_specs, out_specs=P(dp, tensor), check_vma=False
    )
```

time: 811 us -> 221 us (0.27)
  waiting for transfers between devices: 465 us -> 76.4 us
  blocking collectives: 281 us -> 54.6 us
  starting transfers between devices: 3.21 us -> 33.8 us
  Pallas kernels: 0 us -> 29.3 us
  matrix products: 28 us -> 0 us
    all_gather x4 -> x2, waiting for transfers between devices: 434 us -> 28.5 us  [the longest x1 23.5 us: shards(): heads = lax.all_gather(attention, ('yh', 'c'), axis=0, tiled=False)]
    all_gather x2 -> x3, blocking collectives: 281 us -> 54.6 us  [the longest x1 28.4 us: shards(): ring = ring_x(lax.all_gather(packed[..., 0:640], 'z', axis=0, tiled=False))]
    ppermute x1 -> x10, starting transfers between devices: 3.09 us -> 33.7 us  [the longest x8 27.7 us: shift(): lax.ppermute(value, axis, [(i, (i + steps) % count) for i in range(count)])]
    pallas_call x0 -> x3, Pallas kernels: none -> 29.3 us  [the longest x2 15.4 us: project_output(): pl.pallas_call(functools.partial(output_kernel, half), out_shape=(piece,...]
    dot_general x8 -> x0, matrix products: 28 us -> none  [the longest x3 16.1 us: shards(): jnp.dot(columns, weight_piece, preferred_element_type=jnp.float32)]
    ppermute x1 -> x10, waiting for transfers between devices: 30.1 us -> 47.9 us  [the longest x8 31.3 us: shift(): lax.ppermute(value, axis, [(i, (i + steps) % count) for i in range(count)])]
  transfers between devices with their start and end apart: 5 -> 12, of which waited for: 4 -> 10; matrix products, arithmetic and copies ran while one was open for 4% -> 2% of each run, Pallas kernels for 0% -> 4%
where the time goes in v2:
time: 221 us; the launch traced here: 220 us
  waiting for transfers between devices  76.4 us (35%)
  blocking collectives  54.6 us (25%)
  starting transfers between devices  33.8 us (15%)
  Pallas kernels  29.3 us (13%)
  between operations  13.7 us (6%)
  other arithmetic  6.75 us (3%)
  local copies, waits for them, and re-layouts  5.3 us (2%)
    ppermute x8, waiting for transfers between devices, shift(): lax.ppermute(value, axis, [(i, (i + steps) % count) for i in range(count)])  31.3 us
    all_gather x1, blocking collectives, shards(): ring = ring_x(lax.all_gather(packed[..., 0:640], 'z', axis=0, tiled=False))  28.4 us
    ppermute x8, starting transfers between devices, shift(): lax.ppermute(value, axis, [(i, (i + steps) % count) for i in range(count)])  27.7 us
    all_gather x1, waiting for transfers between devices, shards(): heads = lax.all_gather(attention, ('yh', 'c'), axis=0, tiled=False)  23.5 us
    all_gather x1, blocking collectives, shards(): ring = ring_x(lax.all_gather(columns, 'z', axis=0, tiled=False))  21.3 us
    ppermute x2, waiting for transfers between devices, shards(): arrived.append(lax.ppermute(leave, ('yl', 'z', 'x'), pairs))  16.6 us
    pallas_call x2, Pallas kernels, project_output(): pl.pallas_call(functools.partial(output_kernel, half), out_shape=(piece,...  15.4 us
    pallas_call x1, Pallas kernels, attend(): pl.pallas_call(attention_kernel, out_shape=jax.ShapeDtypeStruct((2 * HALF...  13.9 us
  transfers between devices with their start and end apart: 12, of which 10 were waited for; matrix products, arithmetic and copies ran while one was open for 2% of the time, Pallas kernels for 4%

profile of v2, /device:TPU:1, one launch (start us, length us, event | category | flops | bytes accessed | tf_op | source)
XLA Modules:
  0.0 219.8 jit_solution(12369838597753668998)
XLA Ops:
  6.5 0.0 copy-start.9
  6.5 0.0 copy-start.10
  6.5 0.0 all-gather.7.cloned.1.call-start
  6.5 1.4 fusion
  7.9 0.7 convert_element_type.10
  8.6 2.4 %fusion.2 = bf16[128,3072]{1,0:T(8,128)(2,1)} fusion(bf16[128,3072]{1,0:T(8,128)(2,1)} %param.9, f32[3072]{0:T(1024)S(1)} %convert_element_type.10, f32[128]{0:T(128)S(1)} %add_rsqrt_fusion), kind=kLoop, calls=%fused_computation.4 | loop fusion | flops 1572864 | bytes 1585664 | tf_op jit(solution)/shard_map/convert_element_type | solution.py:229
  11.0 0.0 all-gather.7.cloned.1.call-update
  11.0 0.0 all-gather.9.cloned.1.call-start
  11.1 0.7 constant_dynamic-slice_fusion
  11.8 0.0 copy-done.9
  11.8 0.0 copy-done.10
  11.8 4.8 %all-gather = bf16[96,1024]{1,0:T(8,128)(2,1)S(1)} all-gather(bf16[48,1024]{1,0:T(8,128)(2,1)S(1)} %pad_maximum_fusion.1), channel_id=2, replica_groups=mesh['yl'=2,'z'=8,'x'=4,'yh'=4,'c'=2] {'yl'}, dimensions={0}, use_global_device_ids=true | all-gather | bytes 294912 | tf_op jit(solution)/shard_map/all_gather | solution.py:243
  16.6 0.0 copy-start.11
  16.6 28.4 %all-gather.1 = bf16[16,48,640]{2,1,0:T(8,128)(2,1)S(1)} all-gather(bf16[2,48,640]{2,1,0:T(8,128)(2,1)S(1)} %slice.24), channel_id=3, replica_groups=mesh['yl'=2,'z'=8,'x'=4,'yh'=4,'c'=2] {'z'}, dimensions={0}, use_global_device_ids=true | all-gather | bytes 1105920 | tf_op jit(solution)/shard_map/all_gather | solution.py:244
  45.1 0.0 copy-start.1
  45.1 4.4 %collective-permute-start.1 = (bf16[8,2,48,640]{3,2,1,0:T(8,128)(2,1)S(1)}, bf16[8,2,48,640]{3,2,1,0:T(8,128)(2,1)S(1)}, u32[]{:S(2)}, u32[]{:S(2)}) collective-permute-start(bf16[8,2,48,640]{3,2,1,0:T(8,128)(2,1)S(1)} %bitcast.12), channel_id=1, source_target_pairs={{0,24},{8,0},{16,8},{24,16},{1,25},{9,1},{17,9},{25,17},{2,26},{10... | collective-permute-start | bytes 2949128 | tf_op jit(solution)/shard_map/ppermute | solution.py:31
  49.5 1.9 collective-permute-start
  51.4 12.2 %collective-permute-done.1.b2 = bf16[8,2,48,640]{3,2,1,0:T(8,128)(2,1)S(1)} collective-permute-done((bf16[8,2,48,640]{3,2,1,0:T(8,128)(2,1)S(1)}, bf16[8,2,48,640]{3,2,1,0:T(8,128)(2,1)S(1)}, u32[]{:S(2)}, u32[]{:S(2)}) %collective-permute-start.1) | collective-permute-done | bytes 983072 | tf_op jit(solution)/shard_map/ppermute | solution.py:31
  63.6 0.0 copy-start.4
  63.6 0.9 slice.26
  64.5 5.4 %collective-permute-start.3 = (bf16[4,2,48,640]{3,2,1,0:T(8,128)(2,1)}, bf16[4,2,48,640]{3,2,1,0:T(8,128)(2,1)}, u32[]{:S(2)}, u32[]{:S(2)}) collective-permute-start(bf16[4,2,48,640]{3,2,1,0:T(8,128)(2,1)} %slice.26), channel_id=1, source_target_pairs={{0,24},{8,0},{16,8},{24,16},{1,25},{9,1},{17,9},{25,17},{2,26},{10... | collective-permute-start | bytes 1474568 | tf_op jit(solution)/shard_map/ppermute | solution.py:31
  69.9 0.0 collective-permute-done.b1
  69.9 0.0 copy-start.5
  69.9 0.9 slice.25
  70.8 1.9 collective-permute-start.2
  72.8 0.0 copy-done.11
  72.8 0.7 copy.16.lengths
  73.5 1.2 fusion.3.where
  74.7 1.7 collective-permute-done.3.b4
  76.4 5.8 %collective-permute-done.2.b3 = bf16[4,2,48,640]{3,2,1,0:T(8,128)(2,1)} collective-permute-done((bf16[4,2,48,640]{3,2,1,0:T(8,128)(2,1)}, bf16[4,2,48,640]{3,2,1,0:T(8,128)(2,1)}, u32[]{:S(2)}, u32[]{:S(2)}) %collective-permute-start.2) | collective-permute-done | bytes 491552 | tf_op jit(solution)/shard_map/ppermute | solution.py:31
  82.2 5.0 %all-gather.7.cloned.1.call-done.normed = bf16[1024,3072]{1,0:T(8,128)(2,1)} async-done(((bf16[128,3072]{1,0:T(8,128)(2,1)}), bf16[1024,3072]{1,0:T(8,128)(2,1)}) %all-gather.7.cloned.1.call-update) | async-done | bytes 6291472 | tf_op jit(solution)/shard_map/all_gather | solution.py:232
  87.1 0.0 copy-done.1
  87.1 0.0 copy-done.4
  87.1 0.0 copy-done.5
  87.1 13.9 %attend.1 = bf16[1024,384]{1,0:T(8,128)(2,1)} custom-call(s32[2]{0:T(128)} %fusion.3.where, s32[64,3]{1,0:T(8,128)} %copy.16.lengths, bf16[1024,3072]{1,0:T(8,128)(2,1)} %all-gather.7.cloned.1.call-done.normed, bf16[8,2,48,640]{3,2,1,0:T(8,128)(2,1)} %bitcast.14, bf16[8,2,48,640]{3,2,1,0:T(8,128)(2,1)} %copy-done.5, bf16[8,2,48,640]{3,2,1,0:T(8,128)(2,1)} %copy-done.4, ...), custom_call_target="tpu_custom_call" | custom-call | tf_op jit(solution)/shard_map/attend/pallas_call | solution.py:148
  101.0 0.0 copy-start.12
  101.0 0.0 all-gather.9.cloned.1.call-update
  101.1 21.3 %all-gather.3 = bf16[16,48,384]{2,1,0:T(8,128)(2,1)S(1)} all-gather(bf16[2,48,384]{2,1,0:T(8,128)(2,1)S(1)} %slice.27), channel_id=5, replica_groups=mesh['yl'=2,'z'=8,'x'=4,'yh'=4,'c'=2] {'z'}, dimensions={0}, use_global_device_ids=true | all-gather | bytes 663552 | tf_op jit(solution)/shard_map/all_gather | solution.py:250
  122.4 4.7 %collective-permute-start.5 = (bf16[8,2,48,384]{3,2,1,0:T(8,128)(2,1)S(1)}, bf16[8,2,48,384]{3,2,1,0:T(8,128)(2,1)S(1)}, u32[]{:S(2)}, u32[]{:S(2)}) collective-permute-start(bf16[8,2,48,384]{3,2,1,0:T(8,128)(2,1)S(1)} %bitcast.8), channel_id=1, source_target_pairs={{0,24},{8,0},{16,8},{24,16},{1,25},{9,1},{17,9},{25,17},{2,26},{10... | collective-permute-start | bytes 1769480 | tf_op jit(solution)/shard_map/ppermute | solution.py:31
  127.2 1.9 collective-permute-start.4
  129.1 4.9 %collective-permute-done.5.b2 = bf16[8,2,48,384]{3,2,1,0:T(8,128)(2,1)S(1)} collective-permute-done((bf16[8,2,48,384]{3,2,1,0:T(8,128)(2,1)S(1)}, bf16[8,2,48,384]{3,2,1,0:T(8,128)(2,1)S(1)}, u32[]{:S(2)}, u32[]{:S(2)}) %collective-permute-start.5) | collective-permute-done | bytes 589856 | tf_op jit(solution)/shard_map/ppermute | solution.py:31
  134.0 5.5 %collective-permute-start.7 = (bf16[4,2,48,384]{3,2,1,0:T(8,128)(2,1)S(1)}, bf16[4,2,48,384]{3,2,1,0:T(8,128)(2,1)S(1)}, u32[]{:S(2)}, u32[]{:S(2)}) collective-permute-start(bf16[4,2,48,384]{3,2,1,0:T(8,128)(2,1)S(1)} %slice.29), channel_id=1, source_target_pairs={{0,24},{8,0},{16,8},{24,16},{1,25},{9,1},{17,9},{25,17},{2,26},{10... | collective-permute-start | bytes 884744 | tf_op jit(solution)/shard_map/ppermute | solution.py:31
  139.5 0.0 collective-permute-done.4.b1
  139.6 0.0 copy-start.3
  139.6 1.9 collective-permute-start.6
  141.5 0.0 copy-done.12
  141.5 0.7 copy.17.dest
  142.2 2.9 %collective-permute-done.7.b4 = bf16[4,2,48,384]{3,2,1,0:T(8,128)(2,1)S(1)} collective-permute-done((bf16[4,2,48,384]{3,2,1,0:T(8,128)(2,1)S(1)}, bf16[4,2,48,384]{3,2,1,0:T(8,128)(2,1)S(1)}, u32[]{:S(2)}, u32[]{:S(2)}) %collective-permute-start.7) | collective-permute-done | bytes 294944 | tf_op jit(solution)/shard_map/ppermute | solution.py:31
  145.1 3.9 %collective-permute-done.6.b3 = bf16[4,2,48,384]{3,2,1,0:T(8,128)(2,1)S(1)} collective-permute-done((bf16[4,2,48,384]{3,2,1,0:T(8,128)(2,1)S(1)}, bf16[4,2,48,384]{3,2,1,0:T(8,128)(2,1)S(1)}, u32[]{:S(2)}, u32[]{:S(2)}) %collective-permute-start.6) | collective-permute-done | bytes 294944 | tf_op jit(solution)/shard_map/ppermute | solution.py:31
  149.0 23.5 %all-gather.9.cloned.1.call-done = bf16[8192,384]{1,0:T(8,128)(2,1)} async-done(((bf16[1024,384]{1,0:T(8,128)(2,1)}), bf16[8192,384]{1,0:T(8,128)(2,1)}) %all-gather.9.cloned.1.call-update) | async-done | bytes 6291472 | tf_op jit(solution)/shard_map/all_gather | solution.py:247
  172.5 0.0 copy-done
  172.5 0.0 copy-done.2
  172.5 0.0 copy-done.3
  172.5 0.0 copy-done.6
  172.5 0.0 copy-done.7
  172.6 7.7 %project_output.3 = (bf16[512,384]{1,0:T(8,128)(2,1)}, bf16[512,384]{1,0:T(8,128)(2,1)}) custom-call(s32[2]{0:T(128)} %fusion.3.where, s32[64,3]{1,0:T(8,128)} %copy.16.lengths, s32[64,3]{1,0:T(8,128)} %copy.17.dest, bf16[8,1024,384]{2,1,0:T(8,128)(2,1)} %bitcast.6, bf16[8,2,48,384]{3,2,1,0:T(8,128)(2,1)} %bitcast.10, bf16[8,2,48,384]{3,2,1,0:T(8,128)(2,1)} %copy-done.3, ...), custom_call_target="tpu_custom_call" | custom-call | tf_op jit(solution)/shard_map/project_output/pallas_call | solution.py:197
  180.3 0.0 copy-start.8
  180.3 2.8 %collective-permute-start.9 = (bf16[512,384]{1,0:T(8,128)(2,1)}, bf16[512,384]{1,0:T(8,128)(2,1)S(1)}, u32[]{:S(2)}, u32[]{:S(2)}) collective-permute-start(bf16[512,384]{1,0:T(8,128)(2,1)} %get-tuple-element.14), channel_id=1, source_target_pairs={{0,8},{8,16},{16,24},{24,32},{32,40},{40,48},{48,56},{56,64},{64,7... | collective-permute-start | bytes 1179656 | tf_op jit(solution)/shard_map/ppermute | solution.py:256
  183.1 7.7 %project_output.2 = (bf16[512,384]{1,0:T(8,128)(2,1)}, bf16[512,384]{1,0:T(8,128)(2,1)}) custom-call(s32[2]{0:T(128)} %fusion.3.where, s32[64,3]{1,0:T(8,128)} %copy.16.lengths, s32[64,3]{1,0:T(8,128)} %copy.17.dest, bf16[8,1024,384]{2,1,0:T(8,128)(2,1)} %bitcast.7, bf16[8,2,48,384]{3,2,1,0:T(8,128)(2,1)} %bitcast.11, bf16[8,2,48,384]{3,2,1,0:T(8,128)(2,1)} %copy-done.3, ...), custom_call_target="tpu_custom_call" | custom-call | tf_op jit(solution)/shard_map/project_output/pallas_call | solution.py:197
  190.9 3.2 %collective-permute-start.8 = (bf16[512,384]{1,0:T(8,128)(2,1)}, bf16[512,384]{1,0:T(8,128)(2,1)S(1)}, u32[]{:S(2)}, u32[]{:S(2)}) collective-permute-start(bf16[512,384]{1,0:T(8,128)(2,1)} %get-tuple-element.13), channel_id=1, source_target_pairs={{0,8},{8,16},{16,24},{24,32},{32,40},{40,48},{48,56},{56,64},{64,7... | collective-permute-start | bytes 1179656 | tf_op jit(solution)/shard_map/ppermute | solution.py:256
  194.1 6.8 %collective-permute-done.9 = bf16[512,384]{1,0:T(8,128)(2,1)S(1)} collective-permute-done((bf16[512,384]{1,0:T(8,128)(2,1)}, bf16[512,384]{1,0:T(8,128)(2,1)S(1)}, u32[]{:S(2)}, u32[]{:S(2)}) %collective-permute-start.9) | collective-permute-done | bytes 393248 | tf_op jit(solution)/shard_map/ppermute | solution.py:256
  200.8 9.8 %collective-permute-done.8 = bf16[512,384]{1,0:T(8,128)(2,1)S(1)} collective-permute-done((bf16[512,384]{1,0:T(8,128)(2,1)}, bf16[512,384]{1,0:T(8,128)(2,1)S(1)}, u32[]{:S(2)}, u32[]{:S(2)}) %collective-permute-start.8) | collective-permute-done | bytes 393248 | tf_op jit(solution)/shard_map/ppermute | solution.py:256
  210.7 0.0 copy-done.8
  210.7 2.3 %pad_maximum_fusion = bf16[2048,384]{1,0:T(8,128)(2,1)} fusion(bf16[512,384]{1,0:T(8,128)(2,1)S(1)} %collective-permute-done.9, bf16[512,384]{1,0:T(8,128)(2,1)S(1)} %collective-permute-done.8, bf16[512,384]{1,0:T(8,128)(2,1)S(1)} %copy-done.8, bf16[512,384]{1,0:T(8,128)(2,1)} %get-tuple-element.11), kind=kLoop, calls=%fused_computation.5 | loop fusion | flops 6291456 | bytes 3145728 | tf_op jit(solution)/shard_map/concatenate | solution.py:257
  (10 shorter events, 0.1 us)
Async XLA Ops:
  6.5 5.3 %copy-start.9 = (bf16[48,384]{1,0:T(8,128)(2,1)S(1)}, bf16[48,384]{1,0:T(8,128)(2,1)}, u32[]{:S(2)}) copy-start(bf16[48,384]{1,0:T(8,128)(2,1)} %param.14) | copy-start | bytes 110596
  6.5 5.3 %copy-start.10 = (bf16[48,384]{1,0:T(8,128)(2,1)S(1)}, bf16[48,384]{1,0:T(8,128)(2,1)}, u32[]{:S(2)}) copy-start(bf16[48,384]{1,0:T(8,128)(2,1)} %param.11) | copy-start | bytes 110596
  6.5 80.6 %all-gather.7.cloned.1.call-start = ((), (), s32[]{:S(2)}) async-start(), calls=%async_computation | async-start | bytes 7077888 | tf_op jit(solution)/shard_map/all_gather | solution.py:232
  11.0 161.5 %all-gather.9.cloned.1.call-start = ((), (), s32[]{:S(2)}) async-start(), calls=%async_computation.1 | async-start | bytes 7077888 | tf_op jit(solution)/shard_map/all_gather | solution.py:247
  16.6 56.1 %copy-start.11 = (s32[64,3]{0,1:T(4,128)S(1)}, s32[64,3]{0,1:T(4,128)}, u32[]{:S(2)}) copy-start(s32[64,3]{0,1:T(4,128)} %param.15) | copy-start | bytes 2308
  45.1 42.0 %copy-start.1 = (bf16[16,48,640]{2,1,0:T(8,128)(2,1)}, bf16[16,48,640]{2,1,0:T(8,128)(2,1)S(1)}, u32[]{:S(2)}) copy-start(bf16[16,48,640]{2,1,0:T(8,128)(2,1)S(1)} %all-gather.1) | copy-start | bytes 2949124
  45.1 18.5 %collective-permute-start.1 = (bf16[8,2,48,640]{3,2,1,0:T(8,128)(2,1)S(1)}, bf16[8,2,48,640]{3,2,1,0:T(8,128)(2,1)S(1)}, u32[]{:S(2)}, u32[]{:S(2)}) collective-permute-start(bf16[8,2,48,640]{3,2,1,0:T(8,128)(2,1)S(1)} %bitcast.12), channel_id=1, source_target_pairs={{0,24},{8,0},{16,8},{24,16},{1,25},{9,1},{17,9},{25,17},{2,26},{10... | collective-permute-start | bytes 2949128 | tf_op jit(solution)/shard_map/ppermute | solution.py:31
  49.5 20.4 %collective-permute-start = (bf16[8,2,48,640]{3,2,1,0:T(8,128)(2,1)S(1)}, bf16[8,2,48,640]{3,2,1,0:T(8,128)(2,1)S(1)}, u32[]{:S(2)}, u32[]{:S(2)}) collective-permute-start(bf16[8,2,48,640]{3,2,1,0:T(8,128)(2,1)S(1)} %bitcast.13), channel_id=1, source_target_pairs={{0,8},{8,16},{16,24},{24,0},{1,9},{9,17},{17,25},{25,1},{2,10},{10... | collective-permute-start | bytes 2949128 | tf_op jit(solution)/shard_map/ppermute | solution.py:31
  63.6 23.5 %copy-start.4 = (bf16[8,2,48,640]{3,2,1,0:T(8,128)(2,1)}, bf16[8,2,48,640]{3,2,1,0:T(8,128)(2,1)S(1)}, u32[]{:S(2)}) copy-start(bf16[8,2,48,640]{3,2,1,0:T(8,128)(2,1)S(1)} %collective-permute-done.1.b2) | copy-start | bytes 2949124
  64.5 11.9 %collective-permute-start.3 = (bf16[4,2,48,640]{3,2,1,0:T(8,128)(2,1)}, bf16[4,2,48,640]{3,2,1,0:T(8,128)(2,1)}, u32[]{:S(2)}, u32[]{:S(2)}) collective-permute-start(bf16[4,2,48,640]{3,2,1,0:T(8,128)(2,1)} %slice.26), channel_id=1, source_target_pairs={{0,24},{8,0},{16,8},{24,16},{1,25},{9,1},{17,9},{25,17},{2,26},{10... | collective-permute-start | bytes 1474568 | tf_op jit(solution)/shard_map/ppermute | solution.py:31
  69.9 17.2 %copy-start.5 = (bf16[8,2,48,640]{3,2,1,0:T(8,128)(2,1)}, bf16[8,2,48,640]{3,2,1,0:T(8,128)(2,1)S(1)}, u32[]{:S(2)}) copy-start(bf16[8,2,48,640]{3,2,1,0:T(8,128)(2,1)S(1)} %collective-permute-done.b1) | copy-start | bytes 2949124
  70.8 11.3 %collective-permute-start.2 = (bf16[4,2,48,640]{3,2,1,0:T(8,128)(2,1)}, bf16[4,2,48,640]{3,2,1,0:T(8,128)(2,1)}, u32[]{:S(2)}, u32[]{:S(2)}) collective-permute-start(bf16[4,2,48,640]{3,2,1,0:T(8,128)(2,1)} %slice.25), channel_id=1, source_target_pairs={{0,8},{8,16},{16,24},{24,0},{1,9},{9,17},{17,25},{25,1},{2,10},{10... | collective-permute-start | bytes 1474568 | tf_op jit(solution)/shard_map/ppermute | solution.py:31
  101.0 40.5 %copy-start.12 = (s32[64,3]{0,1:T(4,128)S(1)}, s32[64,3]{0,1:T(4,128)}, u32[]{:S(2)}) copy-start(s32[64,3]{0,1:T(4,128)} %param.16) | copy-start | bytes 2308
  122.4 50.1 %copy-start = (bf16[16,48,384]{2,1,0:T(8,128)(2,1)}, bf16[16,48,384]{2,1,0:T(8,128)(2,1)S(1)}, u32[]{:S(2)}) copy-start(bf16[16,48,384]{2,1,0:T(8,128)(2,1)S(1)} %all-gather.3) | copy-start | bytes 1769476
  122.4 11.5 %collective-permute-start.5 = (bf16[8,2,48,384]{3,2,1,0:T(8,128)(2,1)S(1)}, bf16[8,2,48,384]{3,2,1,0:T(8,128)(2,1)S(1)}, u32[]{:S(2)}, u32[]{:S(2)}) collective-permute-start(bf16[8,2,48,384]{3,2,1,0:T(8,128)(2,1)S(1)} %bitcast.8), channel_id=1, source_target_pairs={{0,24},{8,0},{16,8},{24,16},{1,25},{9,1},{17,9},{25,17},{2,26},{10... | collective-permute-start | bytes 1769480 | tf_op jit(solution)/shard_map/ppermute | solution.py:31
  127.2 12.4 %collective-permute-start.4 = (bf16[8,2,48,384]{3,2,1,0:T(8,128)(2,1)S(1)}, bf16[8,2,48,384]{3,2,1,0:T(8,128)(2,1)S(1)}, u32[]{:S(2)}, u32[]{:S(2)}) collective-permute-start(bf16[8,2,48,384]{3,2,1,0:T(8,128)(2,1)S(1)} %bitcast.9), channel_id=1, source_target_pairs={{0,8},{8,16},{16,24},{24,0},{1,9},{9,17},{17,25},{25,1},{2,10},{10... | collective-permute-start | bytes 1769480 | tf_op jit(solution)/shard_map/ppermute | solution.py:31
  134.0 38.6 %copy-start.2 = (bf16[8,2,48,384]{3,2,1,0:T(8,128)(2,1)}, bf16[8,2,48,384]{3,2,1,0:T(8,128)(2,1)S(1)}, u32[]{:S(2)}) copy-start(bf16[8,2,48,384]{3,2,1,0:T(8,128)(2,1)S(1)} %collective-permute-done.5.b2) | copy-start | bytes 1769476
  134.0 11.1 %collective-permute-start.7 = (bf16[4,2,48,384]{3,2,1,0:T(8,128)(2,1)S(1)}, bf16[4,2,48,384]{3,2,1,0:T(8,128)(2,1)S(1)}, u32[]{:S(2)}, u32[]{:S(2)}) collective-permute-start(bf16[4,2,48,384]{3,2,1,0:T(8,128)(2,1)S(1)} %slice.29), channel_id=1, source_target_pairs={{0,24},{8,0},{16,8},{24,16},{1,25},{9,1},{17,9},{25,17},{2,26},{10... | collective-permute-start | bytes 884744 | tf_op jit(solution)/shard_map/ppermute | solution.py:31
  139.6 33.0 %copy-start.3 = (bf16[8,2,48,384]{3,2,1,0:T(8,128)(2,1)}, bf16[8,2,48,384]{3,2,1,0:T(8,128)(2,1)S(1)}, u32[]{:S(2)}) copy-start(bf16[8,2,48,384]{3,2,1,0:T(8,128)(2,1)S(1)} %collective-permute-done.4.b1) | copy-start | bytes 1769476
  139.6 9.4 %collective-permute-start.6 = (bf16[4,2,48,384]{3,2,1,0:T(8,128)(2,1)S(1)}, bf16[4,2,48,384]{3,2,1,0:T(8,128)(2,1)S(1)}, u32[]{:S(2)}, u32[]{:S(2)}) collective-permute-start(bf16[4,2,48,384]{3,2,1,0:T(8,128)(2,1)S(1)} %slice.28), channel_id=1, source_target_pairs={{0,8},{8,16},{16,24},{24,0},{1,9},{9,17},{17,25},{25,1},{2,10},{10... | collective-permute-start | bytes 884744 | tf_op jit(solution)/shard_map/ppermute | solution.py:31
  145.1 27.4 %copy-start.6 = (bf16[4,2,48,384]{3,2,1,0:T(8,128)(2,1)}, bf16[4,2,48,384]{3,2,1,0:T(8,128)(2,1)S(1)}, u32[]{:S(2)}) copy-start(bf16[4,2,48,384]{3,2,1,0:T(8,128)(2,1)S(1)} %collective-permute-done.7.b4) | copy-start | bytes 884740
  149.0 23.6 %copy-start.7 = (bf16[4,2,48,384]{3,2,1,0:T(8,128)(2,1)}, bf16[4,2,48,384]{3,2,1,0:T(8,128)(2,1)S(1)}, u32[]{:S(2)}) copy-start(bf16[4,2,48,384]{3,2,1,0:T(8,128)(2,1)S(1)} %collective-permute-done.6.b3) | copy-start | bytes 884740
  180.3 30.4 %copy-start.8 = (bf16[512,384]{1,0:T(8,128)(2,1)S(1)}, bf16[512,384]{1,0:T(8,128)(2,1)}, u32[]{:S(2)}) copy-start(bf16[512,384]{1,0:T(8,128)(2,1)} %get-tuple-element.12) | copy-start | bytes 1179652
  180.3 20.5 %collective-permute-start.9 = (bf16[512,384]{1,0:T(8,128)(2,1)}, bf16[512,384]{1,0:T(8,128)(2,1)S(1)}, u32[]{:S(2)}, u32[]{:S(2)}) collective-permute-start(bf16[512,384]{1,0:T(8,128)(2,1)} %get-tuple-element.14), channel_id=1, source_target_pairs={{0,8},{8,16},{16,24},{24,32},{32,40},{40,48},{48,56},{56,64},{64,7... | collective-permute-start | bytes 1179656 | tf_op jit(solution)/shard_map/ppermute | solution.py:256
  190.9 19.8 %collective-permute-start.8 = (bf16[512,384]{1,0:T(8,128)(2,1)}, bf16[512,384]{1,0:T(8,128)(2,1)S(1)}, u32[]{:S(2)}, u32[]{:S(2)}) collective-permute-start(bf16[512,384]{1,0:T(8,128)(2,1)} %get-tuple-element.13), channel_id=1, source_target_pairs={{0,8},{8,16},{16,24},{24,32},{32,40},{40,48},{48,56},{56,64},{64,7... | collective-permute-start | bytes 1179656 | tf_op jit(solution)/shard_map/ppermute | solution.py:256
Sparse Core Ops, SparseCore 0:
  11.1 75.9 all-gather.6
  101.2 71.2 all-gather.8

commit v3 on v2

--- a/solution.py
+++ b/solution.py
@@ -16,6 +16,7 @@
 SIZES = (2, 8, 4, 4, 2)
 EXTENT = dict(zip(AXES, SIZES))
 HALF = 512
+PART = 256
 VMEM = 56 * 1024 * 1024
 PARAMS = pltpu.CompilerParams(vmem_limit_bytes=VMEM)
 SMEM_SPEC = pl.BlockSpec(memory_space=pltpu.SMEM)
@@ -70,43 +71,31 @@
 
 
 def attention_kernel(
-    where, lengths, normed, b0, b1, b2, b3, b4, out, rows, weight, total, qkv, sems
+    where, lengths, normed, b0, b1, b2, b3, b4, out, rows, weight, qkv, sems
 ):
     x, shard = where[0], where[1]
-    ring = ring_pairs((b0, b1, b2, b3, b4), weight, x)
-    made = []
-    for yl in range(2):
-        pairs = ring[yl::2]
-        pairs += [
-            (
-                normed.at[half * HALF : half * HALF + HALF, yl * 1536 : yl * 1536 + 1536],
-                rows.at[yl, half],
-            )
-            for half in range(2)
-        ]
-        made.append(start_all(pairs, sems, 7 * yl))
-    for yl in range(2):
-        for copy in made[yl][:5]:
-            copy.wait()
-        for half in range(2):
-            made[yl][5 + half].wait()
-            part = jnp.dot(
-                rows[yl, half],
-                weight[yl].reshape(1536, 640),
-                preferred_element_type=jnp.float32,
-            )
-            here = slice(half * HALF, half * HALF + HALF)
-            if yl == 0:
-                total[here] = part
-            else:
-                qkv[256 + half * HALF : 256 + half * HALF + HALF] = (total[here] + part).astype(
-                    jnp.bfloat16
-                )
+    made = start_all(ring_pairs((b0, b1, b2, b3, b4), weight, x), sems, 0)
+
+    def start(part):
+        return start_all([(normed.at[part * PART : part * PART + PART], rows.at[part])], sems, 10 + part)
+
+    parts = {0: start(0)}
+    for copy in made:
+        copy.wait()
+    parts[1] = start(1)
     qkv[0:256] = jnp.zeros((256, 640), jnp.bfloat16)
     row = lax.broadcasted_iota(jnp.int32, (BLK, 3 * BLK), 0)
     column = lax.broadcasted_iota(jnp.int32, (BLK, 3 * BLK), 1)
     causal = (column >= 2 * BLK) & (column - 2 * BLK <= row)
     for block in range(8):
+        if block * BLK % PART == 0:
+            part = block * BLK // PART
+            parts[part][0].wait()
+            if part + 2 < 1024 // PART:
+                parts[part + 2] = start(part + 2)
+            qkv[256 + part * PART : 256 + part * PART + PART] = jnp.dot(
+                rows[part], weight[...].reshape(3072, 640), preferred_element_type=jnp.float32
+            ).astype(jnp.bfloat16)
         mine = document_of(lengths, shard, block)
         near, far = (
             (document_of(lengths, shard, block - k) == mine).astype(jnp.int32)
@@ -151,34 +140,49 @@
         in_specs=[SMEM_SPEC] * 2 + [ANY_SPEC] * 6,
         out_specs=VMEM_SPEC,
         scratch_shapes=[
-            pltpu.VMEM((2, 2, HALF, 1536), jnp.bfloat16),
+            pltpu.VMEM((1024 // PART, PART, 3072), jnp.bfloat16),
             pltpu.VMEM((2, 8, 4, 48, 640), jnp.bfloat16),
-            pltpu.VMEM((2 * HALF, 640), jnp.float32),
             pltpu.VMEM((256 + 2 * HALF, 640), jnp.bfloat16),
-            pltpu.SemaphoreType.DMA((14,)),
+            pltpu.SemaphoreType.DMA((10 + 1024 // PART,)),
         ],
         compiler_params=PARAMS,
         name="attend",
     )(where, lengths, normed, *ring)
 
 
-def output_kernel(
-    half, where, lengths, dest, heads, b0, b1, b2, b3, b4, stay, leave, rows, weight, sems
-):
-    x, shard = where[0], where[1]
-    made = start_all(ring_pairs((b0, b1, b2, b3, b4), weight, x), sems, 0)
-    parts = start_all(
-        [(heads.at[t, pl.ds(half * HALF, HALF)], rows.at[t]) for t in range(8)], sems, 10
+def assemble_kernel(where, b0, b1, b2, b3, b4, out, sems):
+    for copy in start_all(ring_pairs((b0, b1, b2, b3, b4), out, where[0]), sems, 0):
+        copy.wait()
+
+
+def assemble(where, ring):
+    return pl.pallas_call(
+        assemble_kernel,
+        out_shape=jax.ShapeDtypeStruct((2, 8, 4, 48, 384), jnp.bfloat16),
+        in_specs=[SMEM_SPEC] + [ANY_SPEC] * 5,
+        out_specs=VMEM_SPEC,
+        scratch_shapes=[pltpu.SemaphoreType.DMA((10,))],
+        compiler_params=PARAMS,
+        name="assemble",
+    )(where, *ring)
+
+
+def output_kernel(half, where, lengths, dest, heads, weight, *rest):
+    result, leave, stay, rows, sems = rest[-5:]
+    shard = where[1]
+    made = start_all(
+        [
+            (heads.at[t, half * HALF : half * HALF + HALF], rows.at[:, t * 384 : t * 384 + 384])
+            for t in range(8)
+        ],
+        sems,
+        0,
     )
     for copy in made:
         copy.wait()
-    total = jnp.zeros((HALF, 384), jnp.float32)
-    for t in range(8):
-        parts[t].wait()
-        part = weight[t >> 2, 2 * (t & 3) : 2 * (t & 3) + 2]
-        total = total + jnp.dot(
-            rows[t], part.reshape(384, 384), preferred_element_type=jnp.float32
-        )
+    total = jnp.dot(
+        rows[...], weight[...].reshape(3072, 384), preferred_element_type=jnp.float32
+    )
     for j in range(4):
         document = document_of(lengths, shard, 4 * half + j)
         target = jnp.where(
@@ -190,23 +194,34 @@
         here = slice(j * BLK, j * BLK + BLK)
         stay[here] = (total[here] * (1.0 - moved)).astype(jnp.bfloat16)
         leave[here] = (total[here] * moved).astype(jnp.bfloat16)
-
-
-def project_output(half, where, lengths, dest, heads, ring):
-    piece = jax.ShapeDtypeStruct((HALF, 384), jnp.bfloat16)
+    copy = pltpu.make_async_copy(
+        stay, result.at[half * HALF : half * HALF + HALF], sems.at[8]
+    )
+    copy.start()
+    copy.wait()
+
+
+def project_output(half, where, lengths, dest, heads, weight, *result):
     return pl.pallas_call(
         functools.partial(output_kernel, half),
-        out_shape=(piece, piece),
-        in_specs=[SMEM_SPEC] * 3 + [ANY_SPEC] * 6,
-        out_specs=(VMEM_SPEC, VMEM_SPEC),
+        out_shape=(
+            jax.ShapeDtypeStruct((4 * HALF, 384), jnp.bfloat16),
+            jax.ShapeDtypeStruct((HALF, 384), jnp.bfloat16),
+        ),
+        in_specs=[SMEM_SPEC] * 3 + [ANY_SPEC, VMEM_SPEC] + [ANY_SPEC] * len(result),
+        out_specs=(ANY_SPEC, VMEM_SPEC),
         scratch_shapes=[
-            pltpu.VMEM((8, HALF, 384), jnp.bfloat16),
-            pltpu.VMEM((2, 8, 4, 48, 384), jnp.bfloat16),
-            pltpu.SemaphoreType.DMA((18,)),
-        ],
+            pltpu.VMEM((HALF, 384), jnp.bfloat16),
+            pltpu.VMEM((HALF, 3072), jnp.bfloat16),
+            pltpu.SemaphoreType.DMA((9,)),
+        ],
+        input_output_aliases={5: 0} if result else {},
+        cost_estimate=pl.CostEstimate(
+            flops=2 * HALF * 3072 * 384, bytes_accessed=6000000, transcendentals=0
+        ),
         compiler_params=PARAMS,
         name="project_output",
-    )(where, lengths, dest, heads, *ring)
+    )(where, lengths, dest, heads, weight, *result)
 
 
 def shards(
@@ -247,14 +262,18 @@
     heads = lax.all_gather(attention, ("yh", "c"), axis=0, tiled=False)
 
     columns = lax.optimization_barrier((packed[..., 640:1024], attention))[0]
-    ring = ring_x(lax.all_gather(columns, "z", axis=0, tiled=False))
+    weight = assemble(where, ring_x(lax.all_gather(columns, "z", axis=0, tiled=False)))
     pairs = [(i, (i + 1) % 64) for i in range(64)]
-    staying, arrived = [], []
+    result, arrived = (), []
     for half in range(2):
-        stay, leave = project_output(half, where, document_lengths, doc_dest, heads, ring)
-        staying.append(stay)
-        arrived.append(lax.ppermute(leave, ("yl", "z", "x"), pairs))
-    return jnp.concatenate(staying + arrived, axis=0)
+        *result, leaving = project_output(
+            half, where, document_lengths, doc_dest, heads, weight, *result
+        )
+        arrived.append(lax.ppermute(leaving, ("yl", "z", "x"), pairs))
+    result = result[0]
+    for half in range(2):
+        result = lax.dynamic_update_slice(result, arrived[half], ((2 + half) * HALF, 0))
+    return result
 
 
 def solution(mesh):

time: 221 us -> 216 us (0.977)
  waiting for transfers between devices: 76.4 us -> 71 us
  other arithmetic: 6.75 us -> 4.4 us
  local copies, waits for them, and re-layouts: 5.3 us -> 7.6 us
    all_gather x1, waiting for transfers between devices: 23.5 us -> 19 us  [shards(): heads = lax.all_gather(attention, ('yh', 'c'), axis=0, tiled=False)]
    concatenate x1 -> x0, other arithmetic: 2.3 us -> none  [shards(): return jnp.concatenate(staying + arrived, axis=0)]
    pallas_call x2 -> x3, Pallas kernels: 15.4 us -> 17.7 us  [the longest x2 13.9 us: project_output(): pl.pallas_call(functools.partial(output_kernel, half), out_shape=(jax.Sha...]
  transfers between devices with their start and end apart: 12 -> 12, of which waited for: 10 -> 10; matrix products, arithmetic and copies ran while one was open for 2% -> 3% of each run, Pallas kernels for 4% -> 5%
where the time goes in v3:
time: 216 us; the launch traced here: 215 us
  waiting for transfers between devices  71 us (33%)
  blocking collectives  54.6 us (25%)
  starting transfers between devices  33.5 us (16%)
  Pallas kernels  30.7 us (14%)
  between operations  13.7 us (6%)
  local copies, waits for them, and re-layouts  7.6 us (4%)
  other arithmetic  4.4 us (2%)
    ppermute x8, waiting for transfers between devices, shift(): lax.ppermute(value, axis, [(i, (i + steps) % count) for i in range(count)])  31.2 us
    all_gather x1, blocking collectives, shards(): ring = ring_x(lax.all_gather(packed[..., 0:640], 'z', axis=0, tiled=False))  28.4 us
    ppermute x8, starting transfers between devices, shift(): lax.ppermute(value, axis, [(i, (i + steps) % count) for i in range(count)])  27.8 us
    all_gather x1, blocking collectives, shards(): lax.all_gather(columns, 'z', axis=0, tiled=False)  21.4 us
    all_gather x1, waiting for transfers between devices, shards(): heads = lax.all_gather(attention, ('yh', 'c'), axis=0, tiled=False)  19 us
    ppermute x2, waiting for transfers between devices, shards(): arrived.append(lax.ppermute(leaving, ('yl', 'z', 'x'), pairs))  15.8 us
    pallas_call x2, Pallas kernels, project_output(): pl.pallas_call(functools.partial(output_kernel, half), out_shape=(jax.Sha...  13.9 us
    pallas_call x1, Pallas kernels, attend(): pl.pallas_call(attention_kernel, out_shape=jax.ShapeDtypeStruct((2 * HALF...  13 us
  transfers between devices with their start and end apart: 12, of which 10 were waited for; matrix products, arithmetic and copies ran while one was open for 3% of the time, Pallas kernels for 5%

profile of v3, /device:TPU:1, one launch (start us, length us, event | category | flops | bytes accessed | tf_op | source)
XLA Modules:
  0.0 215.4 jit_solution(8637937264251854095)
XLA Ops:
  6.5 0.0 copy-start.8
  6.5 0.0 copy-start.9
  6.5 0.0 all-gather.7.cloned.1.call-start
  6.5 1.4 fusion
  7.9 0.7 convert_element_type.10
  8.6 2.3 %fusion.2 = bf16[128,3072]{1,0:T(8,128)(2,1)} fusion(bf16[128,3072]{1,0:T(8,128)(2,1)} %param.9, f32[3072]{0:T(1024)S(1)} %convert_element_type.10, f32[128]{0:T(128)S(1)} %add_rsqrt_fusion), kind=kLoop, calls=%fused_computation.4 | loop fusion | flops 1572864 | bytes 1585664 | tf_op jit(solution)/shard_map/convert_element_type | solution.py:244
  10.9 0.0 all-gather.7.cloned.1.call-update
  11.0 0.0 all-gather.9.cloned.1.call-start
  11.0 0.7 constant_dynamic-slice_fusion
  11.7 0.0 copy-done.8
  11.7 0.0 copy-done.9
  11.8 4.8 %all-gather = bf16[96,1024]{1,0:T(8,128)(2,1)S(1)} all-gather(bf16[48,1024]{1,0:T(8,128)(2,1)S(1)} %pad_maximum_fusion), channel_id=2, replica_groups=mesh['yl'=2,'z'=8,'x'=4,'yh'=4,'c'=2] {'yl'}, dimensions={0}, use_global_device_ids=true | all-gather | bytes 294912 | tf_op jit(solution)/shard_map/all_gather | solution.py:258
  16.6 0.0 copy-start.10
  16.6 28.4 %all-gather.1 = bf16[16,48,640]{2,1,0:T(8,128)(2,1)S(1)} all-gather(bf16[2,48,640]{2,1,0:T(8,128)(2,1)S(1)} %slice.24), channel_id=3, replica_groups=mesh['yl'=2,'z'=8,'x'=4,'yh'=4,'c'=2] {'z'}, dimensions={0}, use_global_device_ids=true | all-gather | bytes 1105920 | tf_op jit(solution)/shard_map/all_gather | solution.py:259
  45.0 0.0 copy-start
  45.0 4.4 %collective-permute-start.1 = (bf16[8,2,48,640]{3,2,1,0:T(8,128)(2,1)S(1)}, bf16[8,2,48,640]{3,2,1,0:T(8,128)(2,1)S(1)}, u32[]{:S(2)}, u32[]{:S(2)}) collective-permute-start(bf16[8,2,48,640]{3,2,1,0:T(8,128)(2,1)S(1)} %bitcast.8), channel_id=1, source_target_pairs={{0,24},{8,0},{16,8},{24,16},{1,25},{9,1},{17,9},{25,17},{2,26},{10... | collective-permute-start | bytes 2949128 | tf_op jit(solution)/shard_map/ppermute | solution.py:32
  49.4 1.9 collective-permute-start
  51.3 12.2 %collective-permute-done.1.b2 = bf16[8,2,48,640]{3,2,1,0:T(8,128)(2,1)S(1)} collective-permute-done((bf16[8,2,48,640]{3,2,1,0:T(8,128)(2,1)S(1)}, bf16[8,2,48,640]{3,2,1,0:T(8,128)(2,1)S(1)}, u32[]{:S(2)}, u32[]{:S(2)}) %collective-permute-start.1) | collective-permute-done | bytes 983072 | tf_op jit(solution)/shard_map/ppermute | solution.py:32
  63.5 0.9 slice.26
  64.4 5.4 %collective-permute-start.3 = (bf16[4,2,48,640]{3,2,1,0:T(8,128)(2,1)}, bf16[4,2,48,640]{3,2,1,0:T(8,128)(2,1)}, u32[]{:S(2)}, u32[]{:S(2)}) collective-permute-start(bf16[4,2,48,640]{3,2,1,0:T(8,128)(2,1)} %slice.26), channel_id=1, source_target_pairs={{0,24},{8,0},{16,8},{24,16},{1,25},{9,1},{17,9},{25,17},{2,26},{10... | collective-permute-start | bytes 1474568 | tf_op jit(solution)/shard_map/ppermute | solution.py:32
  69.9 0.0 collective-permute-done.b1
  69.9 0.0 copy-start.3
  69.9 0.9 slice.25
  70.8 1.9 collective-permute-start.2
  72.7 0.0 copy-done.10
  72.7 0.7 copy.19.lengths
  73.4 1.2 fusion.3.where
  74.7 1.7 collective-permute-done.3.b4
  76.3 5.8 %collective-permute-done.2.b3 = bf16[4,2,48,640]{3,2,1,0:T(8,128)(2,1)} collective-permute-done((bf16[4,2,48,640]{3,2,1,0:T(8,128)(2,1)}, bf16[4,2,48,640]{3,2,1,0:T(8,128)(2,1)}, u32[]{:S(2)}, u32[]{:S(2)}) %collective-permute-start.2) | collective-permute-done | bytes 491552 | tf_op jit(solution)/shard_map/ppermute | solution.py:32
  82.1 4.9 %all-gather.7.cloned.1.call-done.normed = bf16[1024,3072]{1,0:T(8,128)(2,1)} async-done(((bf16[128,3072]{1,0:T(8,128)(2,1)}), bf16[1024,3072]{1,0:T(8,128)(2,1)}) %all-gather.7.cloned.1.call-update) | async-done | bytes 6291472 | tf_op jit(solution)/shard_map/all_gather | solution.py:247
  87.1 0.0 copy-done
  87.1 0.0 copy-done.2
  87.1 0.0 copy-done.3
  87.1 13.0 %attend.1 = bf16[1024,384]{1,0:T(8,128)(2,1)} custom-call(s32[2]{0:T(128)} %fusion.3.where, s32[64,3]{1,0:T(8,128)} %copy.19.lengths, bf16[1024,3072]{1,0:T(8,128)(2,1)} %all-gather.7.cloned.1.call-done.normed, bf16[8,2,48,640]{3,2,1,0:T(8,128)(2,1)} %bitcast.10, bf16[8,2,48,640]{3,2,1,0:T(8,128)(2,1)} %copy-done.3, bf16[8,2,48,640]{3,2,1,0:T(8,128)(2,1)} %copy-done.2, ...), custom_call_target="tpu_custom_call" | custom-call | tf_op jit(solution)/shard_map/attend/pallas_call | solution.py:137
  100.1 0.0 copy-start.11
  100.1 0.0 all-gather.9.cloned.1.call-update
  100.2 21.4 %all-gather.3 = bf16[16,48,384]{2,1,0:T(8,128)(2,1)S(1)} all-gather(bf16[2,48,384]{2,1,0:T(8,128)(2,1)S(1)} %slice.27), channel_id=5, replica_groups=mesh['yl'=2,'z'=8,'x'=4,'yh'=4,'c'=2] {'z'}, dimensions={0}, use_global_device_ids=true | all-gather | bytes 663552 | tf_op jit(solution)/shard_map/all_gather | solution.py:265
  121.5 4.7 %collective-permute-start.5 = (bf16[8,2,48,384]{3,2,1,0:T(8,128)(2,1)S(1)}, bf16[8,2,48,384]{3,2,1,0:T(8,128)(2,1)S(1)}, u32[]{:S(2)}, u32[]{:S(2)}) collective-permute-start(bf16[8,2,48,384]{3,2,1,0:T(8,128)(2,1)S(1)} %bitcast.11), channel_id=1, source_target_pairs={{0,24},{8,0},{16,8},{24,16},{1,25},{9,1},{17,9},{25,17},{2,26},{10... | collective-permute-start | bytes 1769480 | tf_op jit(solution)/shard_map/ppermute | solution.py:32
  126.3 1.9 collective-permute-start.4
  128.2 4.9 %collective-permute-done.5.b2 = bf16[8,2,48,384]{3,2,1,0:T(8,128)(2,1)S(1)} collective-permute-done((bf16[8,2,48,384]{3,2,1,0:T(8,128)(2,1)S(1)}, bf16[8,2,48,384]{3,2,1,0:T(8,128)(2,1)S(1)}, u32[]{:S(2)}, u32[]{:S(2)}) %collective-permute-start.5) | collective-permute-done | bytes 589856 | tf_op jit(solution)/shard_map/ppermute | solution.py:32
  133.1 5.6 %collective-permute-start.7 = (bf16[4,2,48,384]{3,2,1,0:T(8,128)(2,1)S(1)}, bf16[4,2,48,384]{3,2,1,0:T(8,128)(2,1)S(1)}, u32[]{:S(2)}, u32[]{:S(2)}) collective-permute-start(bf16[4,2,48,384]{3,2,1,0:T(8,128)(2,1)S(1)} %slice.29), channel_id=1, source_target_pairs={{0,24},{8,0},{16,8},{24,16},{1,25},{9,1},{17,9},{25,17},{2,26},{10... | collective-permute-start | bytes 884744 | tf_op jit(solution)/shard_map/ppermute | solution.py:32
  138.7 0.0 collective-permute-done.4.b1
  138.7 0.0 copy-start.5
  138.8 1.9 collective-permute-start.6
  140.7 0.0 copy-done.11
  140.7 0.7 copy.20.dest
  141.4 2.8 %collective-permute-done.7.b4 = bf16[4,2,48,384]{3,2,1,0:T(8,128)(2,1)S(1)} collective-permute-done((bf16[4,2,48,384]{3,2,1,0:T(8,128)(2,1)S(1)}, bf16[4,2,48,384]{3,2,1,0:T(8,128)(2,1)S(1)}, u32[]{:S(2)}, u32[]{:S(2)}) %collective-permute-start.7) | collective-permute-done | bytes 294944 | tf_op jit(solution)/shard_map/ppermute | solution.py:32
  144.2 3.8 %collective-permute-done.6.b3 = bf16[4,2,48,384]{3,2,1,0:T(8,128)(2,1)S(1)} collective-permute-done((bf16[4,2,48,384]{3,2,1,0:T(8,128)(2,1)S(1)}, bf16[4,2,48,384]{3,2,1,0:T(8,128)(2,1)S(1)}, u32[]{:S(2)}, u32[]{:S(2)}) %collective-permute-start.6) | collective-permute-done | bytes 294944 | tf_op jit(solution)/shard_map/ppermute | solution.py:32
  148.0 0.0 copy-done.1
  148.1 0.0 copy-done.4
  148.1 0.0 copy-done.5
  148.1 0.0 copy-done.6
  148.1 0.0 copy-start.7
  148.1 0.7 copy-done.7
  148.8 3.8 %assemble.1.weight = bf16[2,8,4,48,384]{4,3,2,1,0:T(8,128)(2,1)} custom-call(s32[2]{0:T(128)} %fusion.3.where, bf16[8,2,48,384]{3,2,1,0:T(8,128)(2,1)} %bitcast.13, bf16[8,2,48,384]{3,2,1,0:T(8,128)(2,1)} %copy-done.5, bf16[8,2,48,384]{3,2,1,0:T(8,128)(2,1)} %copy-done.4, bf16[4,2,48,384]{3,2,1,0:T(8,128)(2,1)} %copy-done.7, bf16[4,2,48,384]{3,2,1,0:T(8,128)(2,1)} %copy-done.6), custom_call_target="tpu_custom_call" | custom-call | tf_op jit(solution)/shard_map/assemble/pallas_call | solution.py:159
  152.6 19.0 %all-gather.9.cloned.1.call-done = bf16[8192,384]{1,0:T(8,128)(2,1)} async-done(((bf16[1024,384]{1,0:T(8,128)(2,1)}), bf16[8192,384]{1,0:T(8,128)(2,1)}) %all-gather.9.cloned.1.call-update) | async-done | bytes 6291472 | tf_op jit(solution)/shard_map/all_gather | solution.py:262
  171.6 6.9 %project_output.2 = (bf16[2048,384]{1,0:T(8,128)(2,1)}, bf16[512,384]{1,0:T(8,128)(2,1)}) custom-call(s32[2]{0:T(128)} %fusion.3.where, s32[64,3]{1,0:T(8,128)} %copy.19.lengths, s32[64,3]{1,0:T(8,128)} %copy.20.dest, bf16[8,1024,384]{2,1,0:T(8,128)(2,1)} %bitcast.6, bf16[2,8,4,48,384]{4,3,2,1,0:T(8,128)(2,1)} %assemble.1.weight), custom_call_target="tpu_custom_call" | custom-call | flops 1207959552 | bytes 6000000 | tf_op jit(solution)/shard_map/project_output/pallas_call | solution.py:205
  178.5 2.5 %collective-permute-start.8 = (bf16[512,384]{1,0:T(8,128)(2,1)}, bf16[512,384]{1,0:T(8,128)(2,1)S(1)}, u32[]{:S(2)}, u32[]{:S(2)}) collective-permute-start(bf16[512,384]{1,0:T(8,128)(2,1)} %get-tuple-element.13), channel_id=1, source_target_pairs={{0,8},{8,16},{16,24},{24,32},{32,40},{40,48},{48,56},{56,64},{64,7... | collective-permute-start | bytes 1179656 | tf_op jit(solution)/shard_map/ppermute | solution.py:272
  181.1 6.9 %project_output.3 = (bf16[2048,384]{1,0:T(8,128)(2,1)}, bf16[512,384]{1,0:T(8,128)(2,1)}) custom-call(s32[2]{0:T(128)} %fusion.3.where, s32[64,3]{1,0:T(8,128)} %copy.19.lengths, s32[64,3]{1,0:T(8,128)} %copy.20.dest, bf16[8,1024,384]{2,1,0:T(8,128)(2,1)} %bitcast.7, bf16[2,8,4,48,384]{4,3,2,1,0:T(8,128)(2,1)} %assemble.1.weight, ...), custom_call_target="tpu_custom_call", output_to_operand_aliasing={{0}: (5, {})} | custom-call | flops 1207959552 | bytes 6000000 | tf_op jit(solution)/shard_map/project_output/pallas_call | solution.py:205
  188.0 3.2 %collective-permute-start.9 = (bf16[512,384]{1,0:T(8,128)(2,1)}, bf16[512,384]{1,0:T(8,128)(2,1)S(1)}, u32[]{:S(2)}, u32[]{:S(2)}) collective-permute-start(bf16[512,384]{1,0:T(8,128)(2,1)} %get-tuple-element.14), channel_id=1, source_target_pairs={{0,8},{8,16},{16,24},{24,32},{32,40},{40,48},{48,56},{56,64},{64,7... | collective-permute-start | bytes 1179656 | tf_op jit(solution)/shard_map/ppermute | solution.py:272
  191.2 7.7 %collective-permute-done.8 = bf16[512,384]{1,0:T(8,128)(2,1)S(1)} collective-permute-done((bf16[512,384]{1,0:T(8,128)(2,1)}, bf16[512,384]{1,0:T(8,128)(2,1)S(1)}, u32[]{:S(2)}, u32[]{:S(2)}) %collective-permute-start.8) | collective-permute-done | bytes 393248 | tf_op jit(solution)/shard_map/ppermute | solution.py:272
  198.9 0.8 constant_dynamic-update-slice_fusion.1
  199.7 8.1 %collective-permute-done.9 = bf16[512,384]{1,0:T(8,128)(2,1)S(1)} collective-permute-done((bf16[512,384]{1,0:T(8,128)(2,1)}, bf16[512,384]{1,0:T(8,128)(2,1)S(1)}, u32[]{:S(2)}, u32[]{:S(2)}) %collective-permute-start.9) | collective-permute-done | bytes 393248 | tf_op jit(solution)/shard_map/ppermute | solution.py:272
  207.8 0.8 constant_dynamic-update-slice_fusion
  (10 shorter events, 0.1 us)
Async XLA Ops:
  6.5 5.2 %copy-start.8 = (bf16[48,384]{1,0:T(8,128)(2,1)S(1)}, bf16[48,384]{1,0:T(8,128)(2,1)}, u32[]{:S(2)}) copy-start(bf16[48,384]{1,0:T(8,128)(2,1)} %param.14) | copy-start | bytes 110596
  6.5 5.2 %copy-start.9 = (bf16[48,384]{1,0:T(8,128)(2,1)S(1)}, bf16[48,384]{1,0:T(8,128)(2,1)}, u32[]{:S(2)}) copy-start(bf16[48,384]{1,0:T(8,128)(2,1)} %param.11) | copy-start | bytes 110596
  6.5 80.5 %all-gather.7.cloned.1.call-start = ((), (), s32[]{:S(2)}) async-start(), calls=%async_computation | async-start | bytes 7077888 | tf_op jit(solution)/shard_map/all_gather | solution.py:247
  11.0 160.6 %all-gather.9.cloned.1.call-start = ((), (), s32[]{:S(2)}) async-start(), calls=%async_computation.1 | async-start | bytes 7077888 | tf_op jit(solution)/shard_map/all_gather | solution.py:262
  16.6 56.2 %copy-start.10 = (s32[64,3]{0,1:T(4,128)S(1)}, s32[64,3]{0,1:T(4,128)}, u32[]{:S(2)}) copy-start(s32[64,3]{0,1:T(4,128)} %param.15) | copy-start | bytes 2308
  45.0 42.0 %copy-start = (bf16[16,48,640]{2,1,0:T(8,128)(2,1)}, bf16[16,48,640]{2,1,0:T(8,128)(2,1)S(1)}, u32[]{:S(2)}) copy-start(bf16[16,48,640]{2,1,0:T(8,128)(2,1)S(1)} %all-gather.1) | copy-start | bytes 2949124
  45.0 18.5 %collective-permute-start.1 = (bf16[8,2,48,640]{3,2,1,0:T(8,128)(2,1)S(1)}, bf16[8,2,48,640]{3,2,1,0:T(8,128)(2,1)S(1)}, u32[]{:S(2)}, u32[]{:S(2)}) collective-permute-start(bf16[8,2,48,640]{3,2,1,0:T(8,128)(2,1)S(1)} %bitcast.8), channel_id=1, source_target_pairs={{0,24},{8,0},{16,8},{24,16},{1,25},{9,1},{17,9},{25,17},{2,26},{10... | collective-permute-start | bytes 2949128 | tf_op jit(solution)/shard_map/ppermute | solution.py:32
  49.4 20.5 %collective-permute-start = (bf16[8,2,48,640]{3,2,1,0:T(8,128)(2,1)S(1)}, bf16[8,2,48,640]{3,2,1,0:T(8,128)(2,1)S(1)}, u32[]{:S(2)}, u32[]{:S(2)}) collective-permute-start(bf16[8,2,48,640]{3,2,1,0:T(8,128)(2,1)S(1)} %bitcast.9), channel_id=1, source_target_pairs={{0,8},{8,16},{16,24},{24,0},{1,9},{9,17},{17,25},{25,1},{2,10},{10... | collective-permute-start | bytes 2949128 | tf_op jit(solution)/shard_map/ppermute | solution.py:32
  63.5 23.5 %copy-start.2 = (bf16[8,2,48,640]{3,2,1,0:T(8,128)(2,1)}, bf16[8,2,48,640]{3,2,1,0:T(8,128)(2,1)S(1)}, u32[]{:S(2)}) copy-start(bf16[8,2,48,640]{3,2,1,0:T(8,128)(2,1)S(1)} %collective-permute-done.1.b2) | copy-start | bytes 2949124
  64.4 11.9 %collective-permute-start.3 = (bf16[4,2,48,640]{3,2,1,0:T(8,128)(2,1)}, bf16[4,2,48,640]{3,2,1,0:T(8,128)(2,1)}, u32[]{:S(2)}, u32[]{:S(2)}) collective-permute-start(bf16[4,2,48,640]{3,2,1,0:T(8,128)(2,1)} %slice.26), channel_id=1, source_target_pairs={{0,24},{8,0},{16,8},{24,16},{1,25},{9,1},{17,9},{25,17},{2,26},{10... | collective-permute-start | bytes 1474568 | tf_op jit(solution)/shard_map/ppermute | solution.py:32
  69.9 17.2 %copy-start.3 = (bf16[8,2,48,640]{3,2,1,0:T(8,128)(2,1)}, bf16[8,2,48,640]{3,2,1,0:T(8,128)(2,1)S(1)}, u32[]{:S(2)}) copy-start(bf16[8,2,48,640]{3,2,1,0:T(8,128)(2,1)S(1)} %collective-permute-done.b1) | copy-start | bytes 2949124
  70.8 11.3 %collective-permute-start.2 = (bf16[4,2,48,640]{3,2,1,0:T(8,128)(2,1)}, bf16[4,2,48,640]{3,2,1,0:T(8,128)(2,1)}, u32[]{:S(2)}, u32[]{:S(2)}) collective-permute-start(bf16[4,2,48,640]{3,2,1,0:T(8,128)(2,1)} %slice.25), channel_id=1, source_target_pairs={{0,8},{8,16},{16,24},{24,0},{1,9},{9,17},{17,25},{25,1},{2,10},{10... | collective-permute-start | bytes 1474568 | tf_op jit(solution)/shard_map/ppermute | solution.py:32
  100.1 40.6 %copy-start.11 = (s32[64,3]{0,1:T(4,128)S(1)}, s32[64,3]{0,1:T(4,128)}, u32[]{:S(2)}) copy-start(s32[64,3]{0,1:T(4,128)} %param.16) | copy-start | bytes 2308
  121.5 26.5 %copy-start.1 = (bf16[16,48,384]{2,1,0:T(8,128)(2,1)}, bf16[16,48,384]{2,1,0:T(8,128)(2,1)S(1)}, u32[]{:S(2)}) copy-start(bf16[16,48,384]{2,1,0:T(8,128)(2,1)S(1)} %all-gather.3) | copy-start | bytes 1769476
  121.5 11.5 %collective-permute-start.5 = (bf16[8,2,48,384]{3,2,1,0:T(8,128)(2,1)S(1)}, bf16[8,2,48,384]{3,2,1,0:T(8,128)(2,1)S(1)}, u32[]{:S(2)}, u32[]{:S(2)}) collective-permute-start(bf16[8,2,48,384]{3,2,1,0:T(8,128)(2,1)S(1)} %bitcast.11), channel_id=1, source_target_pairs={{0,24},{8,0},{16,8},{24,16},{1,25},{9,1},{17,9},{25,17},{2,26},{10... | collective-permute-start | bytes 1769480 | tf_op jit(solution)/shard_map/ppermute | solution.py:32
  126.3 12.4 %collective-permute-start.4 = (bf16[8,2,48,384]{3,2,1,0:T(8,128)(2,1)S(1)}, bf16[8,2,48,384]{3,2,1,0:T(8,128)(2,1)S(1)}, u32[]{:S(2)}, u32[]{:S(2)}) collective-permute-start(bf16[8,2,48,384]{3,2,1,0:T(8,128)(2,1)S(1)} %bitcast.12), channel_id=1, source_target_pairs={{0,8},{8,16},{16,24},{24,0},{1,9},{9,17},{17,25},{25,1},{2,10},{10... | collective-permute-start | bytes 1769480 | tf_op jit(solution)/shard_map/ppermute | solution.py:32
  133.1 15.0 %copy-start.4 = (bf16[8,2,48,384]{3,2,1,0:T(8,128)(2,1)}, bf16[8,2,48,384]{3,2,1,0:T(8,128)(2,1)S(1)}, u32[]{:S(2)}) copy-start(bf16[8,2,48,384]{3,2,1,0:T(8,128)(2,1)S(1)} %collective-permute-done.5.b2) | copy-start | bytes 1769476
  133.1 11.1 %collective-permute-start.7 = (bf16[4,2,48,384]{3,2,1,0:T(8,128)(2,1)S(1)}, bf16[4,2,48,384]{3,2,1,0:T(8,128)(2,1)S(1)}, u32[]{:S(2)}, u32[]{:S(2)}) collective-permute-start(bf16[4,2,48,384]{3,2,1,0:T(8,128)(2,1)S(1)} %slice.29), channel_id=1, source_target_pairs={{0,24},{8,0},{16,8},{24,16},{1,25},{9,1},{17,9},{25,17},{2,26},{10... | collective-permute-start | bytes 884744 | tf_op jit(solution)/shard_map/ppermute | solution.py:32
  138.7 9.4 %copy-start.5 = (bf16[8,2,48,384]{3,2,1,0:T(8,128)(2,1)}, bf16[8,2,48,384]{3,2,1,0:T(8,128)(2,1)S(1)}, u32[]{:S(2)}) copy-start(bf16[8,2,48,384]{3,2,1,0:T(8,128)(2,1)S(1)} %collective-permute-done.4.b1) | copy-start | bytes 1769476
  138.8 9.3 %collective-permute-start.6 = (bf16[4,2,48,384]{3,2,1,0:T(8,128)(2,1)S(1)}, bf16[4,2,48,384]{3,2,1,0:T(8,128)(2,1)S(1)}, u32[]{:S(2)}, u32[]{:S(2)}) collective-permute-start(bf16[4,2,48,384]{3,2,1,0:T(8,128)(2,1)S(1)} %slice.28), channel_id=1, source_target_pairs={{0,8},{8,16},{16,24},{24,0},{1,9},{9,17},{17,25},{25,1},{2,10},{10... | collective-permute-start | bytes 884744 | tf_op jit(solution)/shard_map/ppermute | solution.py:32
  144.2 3.9 %copy-start.6 = (bf16[4,2,48,384]{3,2,1,0:T(8,128)(2,1)}, bf16[4,2,48,384]{3,2,1,0:T(8,128)(2,1)S(1)}, u32[]{:S(2)}) copy-start(bf16[4,2,48,384]{3,2,1,0:T(8,128)(2,1)S(1)} %collective-permute-done.7.b4) | copy-start | bytes 884740
  148.1 0.7 copy-start.7
  178.5 20.4 %collective-permute-start.8 = (bf16[512,384]{1,0:T(8,128)(2,1)}, bf16[512,384]{1,0:T(8,128)(2,1)S(1)}, u32[]{:S(2)}, u32[]{:S(2)}) collective-permute-start(bf16[512,384]{1,0:T(8,128)(2,1)} %get-tuple-element.13), channel_id=1, source_target_pairs={{0,8},{8,16},{16,24},{24,32},{32,40},{40,48},{48,56},{56,64},{64,7... | collective-permute-start | bytes 1179656 | tf_op jit(solution)/shard_map/ppermute | solution.py:272
  188.0 19.8 %collective-permute-start.9 = (bf16[512,384]{1,0:T(8,128)(2,1)}, bf16[512,384]{1,0:T(8,128)(2,1)S(1)}, u32[]{:S(2)}, u32[]{:S(2)}) collective-permute-start(bf16[512,384]{1,0:T(8,128)(2,1)} %get-tuple-element.14), channel_id=1, source_target_pairs={{0,8},{8,16},{16,24},{24,32},{32,40},{40,48},{48,56},{56,64},{64,7... | collective-permute-start | bytes 1179656 | tf_op jit(solution)/shard_map/ppermute | solution.py:272
Sparse Core Ops, SparseCore 0:
  11.1 75.9 all-gather.6
  100.3 71.2 all-gather.8

commit v4 on v3

--- a/solution.py
+++ b/solution.py
@@ -17,10 +17,11 @@
 EXTENT = dict(zip(AXES, SIZES))
 HALF = 512
 PART = 256
-VMEM = 56 * 1024 * 1024
-PARAMS = pltpu.CompilerParams(vmem_limit_bytes=VMEM)
+PARAMS = pltpu.CompilerParams(vmem_limit_bytes=56 * 1024 * 1024)
+SMALL_PARAMS = pltpu.CompilerParams(vmem_limit_bytes=46 * 1024 * 1024)
 SMEM_SPEC = pl.BlockSpec(memory_space=pltpu.SMEM)
 ANY_SPEC = pl.BlockSpec(memory_space=pl.ANY)
+HBM_SPEC = pl.BlockSpec(memory_space=pltpu.HBM)
 VMEM_SPEC = pl.BlockSpec(memory_space=pltpu.VMEM)
 PLACES = np.stack(
     [(np.arange(512) // 8) % 4, np.arange(512) // 8], axis=1
@@ -137,7 +138,7 @@
     return pl.pallas_call(
         attention_kernel,
         out_shape=jax.ShapeDtypeStruct((2 * HALF, 384), jnp.bfloat16),
-        in_specs=[SMEM_SPEC] * 2 + [ANY_SPEC] * 6,
+        in_specs=[SMEM_SPEC] * 2 + [HBM_SPEC] + [ANY_SPEC] * 5,
         out_specs=VMEM_SPEC,
         scratch_shapes=[
             pltpu.VMEM((1024 // PART, PART, 3072), jnp.bfloat16),
@@ -162,7 +163,7 @@
         in_specs=[SMEM_SPEC] + [ANY_SPEC] * 5,
         out_specs=VMEM_SPEC,
         scratch_shapes=[pltpu.SemaphoreType.DMA((10,))],
-        compiler_params=PARAMS,
+        compiler_params=SMALL_PARAMS,
         name="assemble",
     )(where, *ring)
 
@@ -178,11 +179,16 @@
         sems,
         0,
     )
-    for copy in made:
-        copy.wait()
-    total = jnp.dot(
-        rows[...], weight[...].reshape(3072, 384), preferred_element_type=jnp.float32
-    )
+    total = jnp.zeros((HALF, 384), jnp.float32)
+    for yl in range(2):
+        for copy in made[4 * yl : 4 * yl + 4]:
+            copy.wait()
+        total = total + jnp.dot(
+            rows[:, yl * 1536 : yl * 1536 + 1536],
+            weight[yl].reshape(1536, 384),
+            preferred_element_type=jnp.float32,
+        )
+    moved = []
     for j in range(4):
         document = document_of(lengths, shard, 4 * half + j)
         target = jnp.where(
@@ -190,14 +196,16 @@
             dest[shard, 0],
             jnp.where(document == 1, dest[shard, 1], dest[shard, 2]),
         )
-        moved = (target != shard).astype(jnp.float32)
+        moved.append((target != shard).astype(jnp.float32))
         here = slice(j * BLK, j * BLK + BLK)
-        stay[here] = (total[here] * (1.0 - moved)).astype(jnp.bfloat16)
-        leave[here] = (total[here] * moved).astype(jnp.bfloat16)
+        stay[here] = (total[here] * (1.0 - moved[j])).astype(jnp.bfloat16)
     copy = pltpu.make_async_copy(
         stay, result.at[half * HALF : half * HALF + HALF], sems.at[8]
     )
     copy.start()
+    for j in range(4):
+        here = slice(j * BLK, j * BLK + BLK)
+        leave[here] = (total[here] * moved[j]).astype(jnp.bfloat16)
     copy.wait()
 
 
@@ -208,8 +216,8 @@
             jax.ShapeDtypeStruct((4 * HALF, 384), jnp.bfloat16),
             jax.ShapeDtypeStruct((HALF, 384), jnp.bfloat16),
         ),
-        in_specs=[SMEM_SPEC] * 3 + [ANY_SPEC, VMEM_SPEC] + [ANY_SPEC] * len(result),
-        out_specs=(ANY_SPEC, VMEM_SPEC),
+        in_specs=[SMEM_SPEC] * 3 + [HBM_SPEC, VMEM_SPEC] + [HBM_SPEC] * len(result),
+        out_specs=(HBM_SPEC, VMEM_SPEC),
         scratch_shapes=[
             pltpu.VMEM((HALF, 384), jnp.bfloat16),
             pltpu.VMEM((HALF, 3072), jnp.bfloat16),
@@ -219,7 +227,7 @@
         cost_estimate=pl.CostEstimate(
             flops=2 * HALF * 3072 * 384, bytes_accessed=6000000, transcendentals=0
         ),
-        compiler_params=PARAMS,
+        compiler_params=SMALL_PARAMS,
         name="project_output",
     )(where, lengths, dest, heads, weight, *result)
 

time: 216 us -> 217 us (level)
  local copies, waits for them, and re-layouts: 7.6 us -> 13.7 us
  Pallas kernels: 30.7 us -> 26.2 us
  waiting for transfers between devices: 71 us -> 68.7 us
    unnamed x26 -> x34, local copies, waits for them, and re-layouts: 2.16 us -> 8.27 us
    pallas_call x1, Pallas kernels: 3.81 us -> 0.98 us  [assemble(): pl.pallas_call(assemble_kernel, out_shape=jax.ShapeDtypeStruct((2, 8, 4,...]
  transfers between devices with their start and end apart: 12 -> 12, of which waited for: 10 -> 10; matrix products, arithmetic and copies ran while one was open for 3% -> 3% of each run, Pallas kernels for 5% -> 3%
where the time goes in v4:
time: 217 us; the launch traced here: 216 us
  waiting for transfers between devices  68.7 us (32%)
  blocking collectives  54.6 us (25%)
  starting transfers between devices  34.3 us (16%)
  Pallas kernels  26.2 us (12%)
  local copies, waits for them, and re-layouts  13.7 us (6%)
  between operations  13.7 us (6%)
  other arithmetic  4.47 us (2%)
    ppermute x8, waiting for transfers between devices, shift(): lax.ppermute(value, axis, [(i, (i + steps) % count) for i in range(count)])  30.2 us
    all_gather x1, blocking collectives, shards(): ring = ring_x(lax.all_gather(packed[..., 0:640], 'z', axis=0, tiled=False))  28.4 us
    ppermute x8, starting transfers between devices, shift(): lax.ppermute(value, axis, [(i, (i + steps) % count) for i in range(count)])  27.7 us
    all_gather x1, blocking collectives, shards(): lax.all_gather(columns, 'z', axis=0, tiled=False)  21.4 us
    all_gather x1, waiting for transfers between devices, shards(): heads = lax.all_gather(attention, ('yh', 'c'), axis=0, tiled=False)  17.4 us
    ppermute x2, waiting for transfers between devices, shards(): arrived.append(lax.ppermute(leaving, ('yl', 'z', 'x'), pairs))  16.1 us
    pallas_call x1, Pallas kernels, attend(): pl.pallas_call(attention_kernel, out_shape=jax.ShapeDtypeStruct((2 * HALF...  13.1 us
    pallas_call x2, Pallas kernels, project_output(): pl.pallas_call(functools.partial(output_kernel, half), out_shape=(jax.Sha...  12.1 us
  transfers between devices with their start and end apart: 12, of which 10 were waited for; matrix products, arithmetic and copies ran while one was open for 3% of the time, Pallas kernels for 3%

profile of v4, /device:TPU:1, one launch (start us, length us, event | category | flops | bytes accessed | tf_op | source)
XLA Modules:
  0.0 215.6 jit_solution(17097003619065016844)
XLA Ops:
  6.5 0.0 all-gather.7.cloned.1.call-start
  6.5 1.4 fusion
  7.9 0.7 convert_element_type.10
  8.6 2.4 %fusion.2 = bf16[128,3072]{1,0:T(8,128)(2,1)} fusion(bf16[128,3072]{1,0:T(8,128)(2,1)} %param.9, f32[3072]{0:T(1024)S(1)} %convert_element_type.10, f32[128]{0:T(128)S(1)} %add_rsqrt_fusion), kind=kLoop, calls=%fused_computation.4 | loop fusion | flops 1572864 | bytes 1585664 | tf_op jit(solution)/shard_map/convert_element_type | solution.py:252
  11.0 0.0 all-gather.7.cloned.1.call-update
  11.0 0.0 all-gather.9.cloned.1.call-start
  11.1 0.7 constant_dynamic-slice_fusion
  11.8 0.0 copy-done.12
  11.8 0.0 copy-done.13
  11.8 4.8 %all-gather = bf16[96,1024]{1,0:T(8,128)(2,1)S(1)} all-gather(bf16[48,1024]{1,0:T(8,128)(2,1)S(1)} %pad_maximum_fusion), channel_id=2, replica_groups=mesh['yl'=2,'z'=8,'x'=4,'yh'=4,'c'=2] {'yl'}, dimensions={0}, use_global_device_ids=true | all-gather | bytes 294912 | tf_op jit(solution)/shard_map/all_gather | solution.py:266
  16.6 0.0 copy-start.14
  16.7 28.4 %all-gather.1 = bf16[16,48,640]{2,1,0:T(8,128)(2,1)S(1)} all-gather(bf16[2,48,640]{2,1,0:T(8,128)(2,1)S(1)} %slice.24), channel_id=3, replica_groups=mesh['yl'=2,'z'=8,'x'=4,'yh'=4,'c'=2] {'z'}, dimensions={0}, use_global_device_ids=true | all-gather | bytes 1105920 | tf_op jit(solution)/shard_map/all_gather | solution.py:267
  45.1 4.4 %collective-permute-start.1 = (bf16[8,2,48,640]{3,2,1,0:T(8,128)(2,1)S(1)}, bf16[8,2,48,640]{3,2,1,0:T(8,128)(2,1)S(1)}, u32[]{:S(2)}, u32[]{:S(2)}) collective-permute-start(bf16[8,2,48,640]{3,2,1,0:T(8,128)(2,1)S(1)} %bitcast.11), channel_id=1, source_target_pairs={{0,24},{8,0},{16,8},{24,16},{1,25},{9,1},{17,9},{25,17},{2,26},{10... | collective-permute-start | bytes 2949128 | tf_op jit(solution)/shard_map/ppermute | solution.py:33
  49.5 1.9 collective-permute-start
  51.4 12.2 %collective-permute-done.1.b2 = bf16[8,2,48,640]{3,2,1,0:T(8,128)(2,1)S(1)} collective-permute-done((bf16[8,2,48,640]{3,2,1,0:T(8,128)(2,1)S(1)}, bf16[8,2,48,640]{3,2,1,0:T(8,128)(2,1)S(1)}, u32[]{:S(2)}, u32[]{:S(2)}) %collective-permute-start.1) | collective-permute-done | bytes 983072 | tf_op jit(solution)/shard_map/ppermute | solution.py:33
  63.6 0.9 slice.26
  64.5 5.4 %collective-permute-start.3 = (bf16[4,2,48,640]{3,2,1,0:T(8,128)(2,1)}, bf16[4,2,48,640]{3,2,1,0:T(8,128)(2,1)}, u32[]{:S(2)}, u32[]{:S(2)}) collective-permute-start(bf16[4,2,48,640]{3,2,1,0:T(8,128)(2,1)} %slice.26), channel_id=1, source_target_pairs={{0,24},{8,0},{16,8},{24,16},{1,25},{9,1},{17,9},{25,17},{2,26},{10... | collective-permute-start | bytes 1474568 | tf_op jit(solution)/shard_map/ppermute | solution.py:33
  69.9 0.0 collective-permute-done.b1
  69.9 0.0 copy-start.11
  69.9 0.9 slice.25
  70.8 1.9 collective-permute-start.2
  72.8 0.0 copy-done.14
  72.8 0.7 copy.19.lengths
  73.5 1.3 fusion.3.where
  74.8 1.6 collective-permute-done.3.b4
  76.4 5.8 %collective-permute-done.2.b3 = bf16[4,2,48,640]{3,2,1,0:T(8,128)(2,1)} collective-permute-done((bf16[4,2,48,640]{3,2,1,0:T(8,128)(2,1)}, bf16[4,2,48,640]{3,2,1,0:T(8,128)(2,1)}, u32[]{:S(2)}, u32[]{:S(2)}) %collective-permute-start.2) | collective-permute-done | bytes 491552 | tf_op jit(solution)/shard_map/ppermute | solution.py:33
  82.2 5.0 %all-gather.7.cloned.1.call-done.normed = bf16[1024,3072]{1,0:T(8,128)(2,1)} async-done(((bf16[128,3072]{1,0:T(8,128)(2,1)}), bf16[1024,3072]{1,0:T(8,128)(2,1)}) %all-gather.7.cloned.1.call-update) | async-done | bytes 6291472 | tf_op jit(solution)/shard_map/all_gather | solution.py:255
  87.1 0.0 copy-done.9
  87.1 0.0 copy-done.10
  87.1 0.0 copy-done.11
  87.1 13.1 %attend.1 = bf16[1024,384]{1,0:T(8,128)(2,1)} custom-call(s32[2]{0:T(128)} %fusion.3.where, s32[64,3]{1,0:T(8,128)} %copy.19.lengths, bf16[1024,3072]{1,0:T(8,128)(2,1)} %all-gather.7.cloned.1.call-done.normed, bf16[8,2,48,640]{3,2,1,0:T(8,128)(2,1)} %bitcast.13, bf16[8,2,48,640]{3,2,1,0:T(8,128)(2,1)} %copy-done.11, bf16[8,2,48,640]{3,2,1,0:T(8,128)(2,1)} %copy-done.10, ...), custom_call_target="tpu_custom_call" | custom-call | tf_op jit(solution)/shard_map/attend/pallas_call | solution.py:138
  100.2 0.0 copy-start.15
  100.3 0.0 copy-start.8
  100.3 0.0 all-gather.9.cloned.1.call-update
  100.3 21.4 %all-gather.3 = bf16[16,48,384]{2,1,0:T(8,128)(2,1)S(1)} all-gather(bf16[2,48,384]{2,1,0:T(8,128)(2,1)S(1)} %slice.27), channel_id=5, replica_groups=mesh['yl'=2,'z'=8,'x'=4,'yh'=4,'c'=2] {'z'}, dimensions={0}, use_global_device_ids=true | all-gather | bytes 663552 | tf_op jit(solution)/shard_map/all_gather | solution.py:273
  121.7 4.7 %collective-permute-start.5 = (bf16[8,2,48,384]{3,2,1,0:T(8,128)(2,1)S(1)}, bf16[8,2,48,384]{3,2,1,0:T(8,128)(2,1)S(1)}, u32[]{:S(2)}, u32[]{:S(2)}) collective-permute-start(bf16[8,2,48,384]{3,2,1,0:T(8,128)(2,1)S(1)} %bitcast.6), channel_id=1, source_target_pairs={{0,24},{8,0},{16,8},{24,16},{1,25},{9,1},{17,9},{25,17},{2,26},{10... | collective-permute-start | bytes 1769480 | tf_op jit(solution)/shard_map/ppermute | solution.py:33
  126.4 1.9 collective-permute-start.4
  128.3 4.9 %collective-permute-done.5.b2 = bf16[8,2,48,384]{3,2,1,0:T(8,128)(2,1)S(1)} collective-permute-done((bf16[8,2,48,384]{3,2,1,0:T(8,128)(2,1)S(1)}, bf16[8,2,48,384]{3,2,1,0:T(8,128)(2,1)S(1)}, u32[]{:S(2)}, u32[]{:S(2)}) %collective-permute-start.5) | collective-permute-done | bytes 589856 | tf_op jit(solution)/shard_map/ppermute | solution.py:33
  133.2 5.5 %collective-permute-start.7 = (bf16[4,2,48,384]{3,2,1,0:T(8,128)(2,1)S(1)}, bf16[4,2,48,384]{3,2,1,0:T(8,128)(2,1)S(1)}, u32[]{:S(2)}, u32[]{:S(2)}) collective-permute-start(bf16[4,2,48,384]{3,2,1,0:T(8,128)(2,1)S(1)} %slice.29), channel_id=1, source_target_pairs={{0,24},{8,0},{16,8},{24,16},{1,25},{9,1},{17,9},{25,17},{2,26},{10... | collective-permute-start | bytes 884744 | tf_op jit(solution)/shard_map/ppermute | solution.py:33
  138.8 0.0 collective-permute-done.4.b1
  138.8 0.0 copy-start
  138.8 0.8 copy-done
  139.6 1.9 collective-permute-start.6
  141.6 0.0 copy-done.15
  141.6 0.7 copy.20.dest
  142.3 2.0 collective-permute-done.7.b4
  144.3 0.7 copy-done.4
  145.1 3.6 %collective-permute-done.6.b3 = bf16[4,2,48,384]{3,2,1,0:T(8,128)(2,1)S(1)} collective-permute-done((bf16[4,2,48,384]{3,2,1,0:T(8,128)(2,1)S(1)}, bf16[4,2,48,384]{3,2,1,0:T(8,128)(2,1)S(1)}, u32[]{:S(2)}, u32[]{:S(2)}) %collective-permute-start.6) | collective-permute-done | bytes 294944 | tf_op jit(solution)/shard_map/ppermute | solution.py:33
  148.7 0.7 copy-done.6
  149.4 1.1 copy-done.1
  150.5 1.0 copy-done.5
  151.5 1.0 copy-done.7
  152.5 1.0 assemble.1.weight
  153.5 17.4 %all-gather.9.cloned.1.call-done = bf16[8192,384]{1,0:T(8,128)(2,1)} async-done(((bf16[1024,384]{1,0:T(8,128)(2,1)}), bf16[8192,384]{1,0:T(8,128)(2,1)}) %all-gather.9.cloned.1.call-update) | async-done | bytes 6291472 | tf_op jit(solution)/shard_map/all_gather | solution.py:270
  170.8 0.8 copy-done.2
  171.6 0.8 copy-done.3
  172.4 6.0 %project_output.2 = (bf16[2048,384]{1,0:T(8,128)(2,1)}, bf16[512,384]{1,0:T(8,128)(2,1)S(1)}) custom-call(s32[2]{0:T(128)S(1)} %copy-done.8, s32[64,3]{1,0:T(8,128)S(1)} %copy-done.2, s32[64,3]{1,0:T(8,128)S(1)} %copy-done.3, bf16[8,1024,384]{2,1,0:T(8,128)(2,1)} %bitcast.9, bf16[2,8,4,48,384]{4,3,2,1,0:T(8,128)(2,1)S(1)} %assemble.1.weight), custom_call_target="tpu_custom_call" | custom-call | flops 1207959552 | bytes 6000000 | tf_op jit(solution)/shard_map/project_output/pallas_call | solution.py:213
  178.4 3.4 %collective-permute-start.8 = (bf16[512,384]{1,0:T(8,128)(2,1)S(1)}, bf16[512,384]{1,0:T(8,128)(2,1)S(1)}, u32[]{:S(2)}, u32[]{:S(2)}) collective-permute-start(bf16[512,384]{1,0:T(8,128)(2,1)S(1)} %get-tuple-element.13), channel_id=1, source_target_pairs={{0,8},{8,16},{16,24},{24,32},{32,40},{40,48},{48,56},{56,64},{64,7... | collective-permute-start | bytes 1179656 | tf_op jit(solution)/shard_map/ppermute | solution.py:280
  181.8 6.0 %project_output.3 = (bf16[2048,384]{1,0:T(8,128)(2,1)}, bf16[512,384]{1,0:T(8,128)(2,1)S(1)}) custom-call(s32[2]{0:T(128)S(1)} %copy-done.8, s32[64,3]{1,0:T(8,128)S(1)} %copy-done.2, s32[64,3]{1,0:T(8,128)S(1)} %copy-done.3, bf16[8,1024,384]{2,1,0:T(8,128)(2,1)} %bitcast.10, ...), custom_call_target="tpu_custom_call", output_to_operand_aliasing={{0}: (5, {})} | custom-call | flops 1207959552 | bytes 6000000 | tf_op jit(solution)/shard_map/project_output/pallas_call | solution.py:213
  187.9 3.1 %collective-permute-start.9 = (bf16[512,384]{1,0:T(8,128)(2,1)S(1)}, bf16[512,384]{1,0:T(8,128)(2,1)S(1)}, u32[]{:S(2)}, u32[]{:S(2)}) collective-permute-start(bf16[512,384]{1,0:T(8,128)(2,1)S(1)} %get-tuple-element.14), channel_id=1, source_target_pairs={{0,8},{8,16},{16,24},{24,32},{32,40},{40,48},{48,56},{56,64},{64,7... | collective-permute-start | bytes 1179656 | tf_op jit(solution)/shard_map/ppermute | solution.py:280
  191.0 8.5 %collective-permute-done.8 = bf16[512,384]{1,0:T(8,128)(2,1)S(1)} collective-permute-done((bf16[512,384]{1,0:T(8,128)(2,1)S(1)}, bf16[512,384]{1,0:T(8,128)(2,1)S(1)}, u32[]{:S(2)}, u32[]{:S(2)}) %collective-permute-start.8) | collective-permute-done | bytes 393248 | tf_op jit(solution)/shard_map/ppermute | solution.py:280
  199.5 0.8 constant_dynamic-update-slice_fusion.1
  200.3 7.6 %collective-permute-done.9 = bf16[512,384]{1,0:T(8,128)(2,1)S(1)} collective-permute-done((bf16[512,384]{1,0:T(8,128)(2,1)S(1)}, bf16[512,384]{1,0:T(8,128)(2,1)S(1)}, u32[]{:S(2)}, u32[]{:S(2)}) %collective-permute-start.9) | collective-permute-done | bytes 393248 | tf_op jit(solution)/shard_map/ppermute | solution.py:280
  208.0 0.8 constant_dynamic-update-slice_fusion
  (18 shorter events, 0.1 us)
Async XLA Ops:
  6.5 5.3 %copy-start.12 = (bf16[48,384]{1,0:T(8,128)(2,1)S(1)}, bf16[48,384]{1,0:T(8,128)(2,1)}, u32[]{:S(2)}) copy-start(bf16[48,384]{1,0:T(8,128)(2,1)} %param.14) | copy-start | bytes 110596
  6.5 5.3 %copy-start.13 = (bf16[48,384]{1,0:T(8,128)(2,1)S(1)}, bf16[48,384]{1,0:T(8,128)(2,1)}, u32[]{:S(2)}) copy-start(bf16[48,384]{1,0:T(8,128)(2,1)} %param.11) | copy-start | bytes 110596
  6.5 80.6 %all-gather.7.cloned.1.call-start = ((), (), s32[]{:S(2)}) async-start(), calls=%async_computation | async-start | bytes 7077888 | tf_op jit(solution)/shard_map/all_gather | solution.py:255
  11.0 159.8 %all-gather.9.cloned.1.call-start = ((), (), s32[]{:S(2)}) async-start(), calls=%async_computation.1 | async-start | bytes 7077888 | tf_op jit(solution)/shard_map/all_gather | solution.py:270
  16.6 56.1 %copy-start.14 = (s32[64,3]{0,1:T(4,128)S(1)}, s32[64,3]{0,1:T(4,128)}, u32[]{:S(2)}) copy-start(s32[64,3]{0,1:T(4,128)} %param.15) | copy-start | bytes 2308
  45.1 42.0 %copy-start.9 = (bf16[16,48,640]{2,1,0:T(8,128)(2,1)}, bf16[16,48,640]{2,1,0:T(8,128)(2,1)S(1)}, u32[]{:S(2)}) copy-start(bf16[16,48,640]{2,1,0:T(8,128)(2,1)S(1)} %all-gather.1) | copy-start | bytes 2949124
  45.1 18.5 %collective-permute-start.1 = (bf16[8,2,48,640]{3,2,1,0:T(8,128)(2,1)S(1)}, bf16[8,2,48,640]{3,2,1,0:T(8,128)(2,1)S(1)}, u32[]{:S(2)}, u32[]{:S(2)}) collective-permute-start(bf16[8,2,48,640]{3,2,1,0:T(8,128)(2,1)S(1)} %bitcast.11), channel_id=1, source_target_pairs={{0,24},{8,0},{16,8},{24,16},{1,25},{9,1},{17,9},{25,17},{2,26},{10... | collective-permute-start | bytes 2949128 | tf_op jit(solution)/shard_map/ppermute | solution.py:33
  49.5 20.4 %collective-permute-start = (bf16[8,2,48,640]{3,2,1,0:T(8,128)(2,1)S(1)}, bf16[8,2,48,640]{3,2,1,0:T(8,128)(2,1)S(1)}, u32[]{:S(2)}, u32[]{:S(2)}) collective-permute-start(bf16[8,2,48,640]{3,2,1,0:T(8,128)(2,1)S(1)} %bitcast.12), channel_id=1, source_target_pairs={{0,8},{8,16},{16,24},{24,0},{1,9},{9,17},{17,25},{25,1},{2,10},{10... | collective-permute-start | bytes 2949128 | tf_op jit(solution)/shard_map/ppermute | solution.py:33
  63.6 23.5 %copy-start.10 = (bf16[8,2,48,640]{3,2,1,0:T(8,128)(2,1)}, bf16[8,2,48,640]{3,2,1,0:T(8,128)(2,1)S(1)}, u32[]{:S(2)}) copy-start(bf16[8,2,48,640]{3,2,1,0:T(8,128)(2,1)S(1)} %collective-permute-done.1.b2) | copy-start | bytes 2949124
  64.5 11.9 %collective-permute-start.3 = (bf16[4,2,48,640]{3,2,1,0:T(8,128)(2,1)}, bf16[4,2,48,640]{3,2,1,0:T(8,128)(2,1)}, u32[]{:S(2)}, u32[]{:S(2)}) collective-permute-start(bf16[4,2,48,640]{3,2,1,0:T(8,128)(2,1)} %slice.26), channel_id=1, source_target_pairs={{0,24},{8,0},{16,8},{24,16},{1,25},{9,1},{17,9},{25,17},{2,26},{10... | collective-permute-start | bytes 1474568 | tf_op jit(solution)/shard_map/ppermute | solution.py:33
  69.9 17.2 %copy-start.11 = (bf16[8,2,48,640]{3,2,1,0:T(8,128)(2,1)}, bf16[8,2,48,640]{3,2,1,0:T(8,128)(2,1)S(1)}, u32[]{:S(2)}) copy-start(bf16[8,2,48,640]{3,2,1,0:T(8,128)(2,1)S(1)} %collective-permute-done.b1) | copy-start | bytes 2949124
  70.8 11.3 %collective-permute-start.2 = (bf16[4,2,48,640]{3,2,1,0:T(8,128)(2,1)}, bf16[4,2,48,640]{3,2,1,0:T(8,128)(2,1)}, u32[]{:S(2)}, u32[]{:S(2)}) collective-permute-start(bf16[4,2,48,640]{3,2,1,0:T(8,128)(2,1)} %slice.25), channel_id=1, source_target_pairs={{0,8},{8,16},{16,24},{24,0},{1,9},{9,17},{17,25},{25,1},{2,10},{10... | collective-permute-start | bytes 1474568 | tf_op jit(solution)/shard_map/ppermute | solution.py:33
  100.2 41.3 %copy-start.15 = (s32[64,3]{0,1:T(4,128)S(1)}, s32[64,3]{0,1:T(4,128)}, u32[]{:S(2)}) copy-start(s32[64,3]{0,1:T(4,128)} %param.16) | copy-start | bytes 2308
  100.3 49.2 %copy-start.8 = (s32[2]{0:T(128)S(1)}, s32[2]{0:T(128)}, u32[]{:S(2)}) copy-start(s32[2]{0:T(128)} %fusion.3.where) | copy-start | bytes 28
  121.7 11.5 %collective-permute-start.5 = (bf16[8,2,48,384]{3,2,1,0:T(8,128)(2,1)S(1)}, bf16[8,2,48,384]{3,2,1,0:T(8,128)(2,1)S(1)}, u32[]{:S(2)}, u32[]{:S(2)}) collective-permute-start(bf16[8,2,48,384]{3,2,1,0:T(8,128)(2,1)S(1)} %bitcast.6), channel_id=1, source_target_pairs={{0,24},{8,0},{16,8},{24,16},{1,25},{9,1},{17,9},{25,17},{2,26},{10... | collective-permute-start | bytes 1769480 | tf_op jit(solution)/shard_map/ppermute | solution.py:33
  126.4 12.4 %collective-permute-start.4 = (bf16[8,2,48,384]{3,2,1,0:T(8,128)(2,1)S(1)}, bf16[8,2,48,384]{3,2,1,0:T(8,128)(2,1)S(1)}, u32[]{:S(2)}, u32[]{:S(2)}) collective-permute-start(bf16[8,2,48,384]{3,2,1,0:T(8,128)(2,1)S(1)} %bitcast.7), channel_id=1, source_target_pairs={{0,8},{8,16},{16,24},{24,0},{1,9},{9,17},{17,25},{25,1},{2,10},{10... | collective-permute-start | bytes 1769480 | tf_op jit(solution)/shard_map/ppermute | solution.py:33
  133.2 11.1 %collective-permute-start.7 = (bf16[4,2,48,384]{3,2,1,0:T(8,128)(2,1)S(1)}, bf16[4,2,48,384]{3,2,1,0:T(8,128)(2,1)S(1)}, u32[]{:S(2)}, u32[]{:S(2)}) collective-permute-start(bf16[4,2,48,384]{3,2,1,0:T(8,128)(2,1)S(1)} %slice.29), channel_id=1, source_target_pairs={{0,24},{8,0},{16,8},{24,16},{1,25},{9,1},{17,9},{25,17},{2,26},{10... | collective-permute-start | bytes 884744 | tf_op jit(solution)/shard_map/ppermute | solution.py:33
  138.8 0.8 copy-start
  139.6 9.1 %collective-permute-start.6 = (bf16[4,2,48,384]{3,2,1,0:T(8,128)(2,1)S(1)}, bf16[4,2,48,384]{3,2,1,0:T(8,128)(2,1)S(1)}, u32[]{:S(2)}, u32[]{:S(2)}) collective-permute-start(bf16[4,2,48,384]{3,2,1,0:T(8,128)(2,1)S(1)} %slice.28), channel_id=1, source_target_pairs={{0,8},{8,16},{16,24},{24,0},{1,9},{9,17},{17,25},{25,1},{2,10},{10... | collective-permute-start | bytes 884744 | tf_op jit(solution)/shard_map/ppermute | solution.py:33
  144.3 0.7 copy-start.4
  148.7 0.7 copy-start.6
  149.4 1.1 copy-start.1
  150.5 1.0 copy-start.5
  151.5 1.0 copy-start.7
  170.8 0.8 copy-start.2
  171.6 0.8 copy-start.3
  178.4 21.1 %collective-permute-start.8 = (bf16[512,384]{1,0:T(8,128)(2,1)S(1)}, bf16[512,384]{1,0:T(8,128)(2,1)S(1)}, u32[]{:S(2)}, u32[]{:S(2)}) collective-permute-start(bf16[512,384]{1,0:T(8,128)(2,1)S(1)} %get-tuple-element.13), channel_id=1, source_target_pairs={{0,8},{8,16},{16,24},{24,32},{32,40},{40,48},{48,56},{56,64},{64,7... | collective-permute-start | bytes 1179656 | tf_op jit(solution)/shard_map/ppermute | solution.py:280
  187.9 20.1 %collective-permute-start.9 = (bf16[512,384]{1,0:T(8,128)(2,1)S(1)}, bf16[512,384]{1,0:T(8,128)(2,1)S(1)}, u32[]{:S(2)}, u32[]{:S(2)}) collective-permute-start(bf16[512,384]{1,0:T(8,128)(2,1)S(1)} %get-tuple-element.14), channel_id=1, source_target_pairs={{0,8},{8,16},{16,24},{24,32},{32,40},{40,48},{48,56},{56,64},{64,7... | collective-permute-start | bytes 1179656 | tf_op jit(solution)/shard_map/ppermute | solution.py:280
Sparse Core Ops, SparseCore 0:
  11.1 75.9 all-gather.6
  100.4 70.3 all-gather.8

commit v5 on v4

--- a/solution.py
+++ b/solution.py
@@ -232,6 +232,25 @@
     )(where, lengths, dest, heads, weight, *result)
 
 
+def norm_kernel(inputs, gain, out):
+    values = inputs[...].astype(jnp.float32)
+    mean_square = jnp.mean(values * values, axis=1, keepdims=True)
+    out[...] = (
+        values * lax.rsqrt(mean_square + EPS) * gain[...].astype(jnp.float32)
+    ).astype(jnp.bfloat16)
+
+
+def normalize(activations, gain):
+    return pl.pallas_call(
+        norm_kernel,
+        out_shape=jax.ShapeDtypeStruct(activations.shape, jnp.bfloat16),
+        in_specs=[VMEM_SPEC] * 2,
+        out_specs=VMEM_SPEC,
+        compiler_params=SMALL_PARAMS,
+        name="normalize",
+    )(activations, gain.reshape(1, -1))
+
+
 def shards(
     activations,
     norm_gain,
@@ -247,11 +266,7 @@
         jnp.asarray(PLACES), lax.axis_index(AXES), 0, keepdims=False
     )
 
-    inputs = activations.astype(jnp.float32)
-    mean_square = jnp.mean(inputs * inputs, axis=1, keepdims=True)
-    normed = (inputs * lax.rsqrt(mean_square + EPS) * norm_gain.astype(jnp.float32)).astype(
-        jnp.bfloat16
-    )
+    normed = normalize(activations, norm_gain)
     gathered = lax.all_gather(normed, ("yh", "c"), axis=0, tiled=True)
 
     packed = jnp.concatenate(

time: 217 us -> 215 us (level)
  other arithmetic: 4.47 us -> 0.01 us
    convert_element_type x2 -> x0, other arithmetic: 3.07 us -> none  [the longest x1 2.37 us: shards(): (inputs * lax.rsqrt(mean_square + EPS) * norm_gain.astype(jnp.float32)).a...]
    unnamed x34 -> x36, local copies, waits for them, and re-layouts: 8.27 us -> 9.35 us
where the time goes in v5:
time: 215 us; the launch traced here: 214 us
  waiting for transfers between devices  68.7 us (32%)
  blocking collectives  54.6 us (25%)
  starting transfers between devices  34.4 us (16%)
  Pallas kernels  27.6 us (13%)
  local copies, waits for them, and re-layouts  15.4 us (7%)
  between operations  13.7 us (6%)
    ppermute x8, waiting for transfers between devices, shift(): lax.ppermute(value, axis, [(i, (i + steps) % count) for i in range(count)])  30.3 us
    all_gather x1, blocking collectives, shards(): ring = ring_x(lax.all_gather(packed[..., 0:640], 'z', axis=0, tiled=False))  28.4 us
    ppermute x8, starting transfers between devices, shift(): lax.ppermute(value, axis, [(i, (i + steps) % count) for i in range(count)])  27.8 us
    all_gather x1, blocking collectives, shards(): lax.all_gather(columns, 'z', axis=0, tiled=False)  21.3 us
    all_gather x1, waiting for transfers between devices, shards(): heads = lax.all_gather(attention, ('yh', 'c'), axis=0, tiled=False)  17.3 us
    ppermute x2, waiting for transfers between devices, shards(): arrived.append(lax.ppermute(leaving, ('yl', 'z', 'x'), pairs))  16.1 us
    pallas_call x1, Pallas kernels, attend(): pl.pallas_call(attention_kernel, out_shape=jax.ShapeDtypeStruct((2 * HALF...  13.1 us
    pallas_call x2, Pallas kernels, project_output(): pl.pallas_call(functools.partial(output_kernel, half), out_shape=(jax.Sha...  12.1 us
  transfers between devices with their start and end apart: 12, of which 10 were waited for; matrix products, arithmetic and copies ran while one was open for 3% of the time, Pallas kernels for 3%

profile of v5, /device:TPU:1, one launch (start us, length us, event | category | flops | bytes accessed | tf_op | source)
XLA Modules:
  0.0 214.3 jit_solution(808103674493431598)
XLA Ops:
  6.5 0.0 all-gather.7.cloned.1.call-start
  6.5 0.7 reshape.3.gain
  7.2 1.1 copy-done.2
  8.4 1.4 normalize.1
  9.8 0.0 all-gather.7.cloned.1.call-update
  9.8 0.0 all-gather.9.cloned.1.call-start
  9.9 0.7 constant_dynamic-slice_fusion
  10.6 0.0 copy-done.13
  10.6 0.0 copy-done.14
  10.6 4.8 %all-gather = bf16[96,1024]{1,0:T(8,128)(2,1)S(1)} all-gather(bf16[48,1024]{1,0:T(8,128)(2,1)S(1)} %pad_maximum_fusion), channel_id=2, replica_groups=mesh['yl'=2,'z'=8,'x'=4,'yh'=4,'c'=2] {'yl'}, dimensions={0}, use_global_device_ids=true | all-gather | bytes 294912 | tf_op jit(solution)/shard_map/all_gather | solution.py:281
  15.4 0.0 copy-start.15
  15.4 28.4 %all-gather.1 = bf16[16,48,640]{2,1,0:T(8,128)(2,1)S(1)} all-gather(bf16[2,48,640]{2,1,0:T(8,128)(2,1)S(1)} %slice.24), channel_id=3, replica_groups=mesh['yl'=2,'z'=8,'x'=4,'yh'=4,'c'=2] {'z'}, dimensions={0}, use_global_device_ids=true | all-gather | bytes 1105920 | tf_op jit(solution)/shard_map/all_gather | solution.py:282
  43.9 4.4 %collective-permute-start.1 = (bf16[8,2,48,640]{3,2,1,0:T(8,128)(2,1)S(1)}, bf16[8,2,48,640]{3,2,1,0:T(8,128)(2,1)S(1)}, u32[]{:S(2)}, u32[]{:S(2)}) collective-permute-start(bf16[8,2,48,640]{3,2,1,0:T(8,128)(2,1)S(1)} %bitcast.11), channel_id=1, source_target_pairs={{0,24},{8,0},{16,8},{24,16},{1,25},{9,1},{17,9},{25,17},{2,26},{10... | collective-permute-start | bytes 2949128 | tf_op jit(solution)/shard_map/ppermute | solution.py:33
  48.3 1.9 collective-permute-start
  50.2 12.2 %collective-permute-done.1.b2 = bf16[8,2,48,640]{3,2,1,0:T(8,128)(2,1)S(1)} collective-permute-done((bf16[8,2,48,640]{3,2,1,0:T(8,128)(2,1)S(1)}, bf16[8,2,48,640]{3,2,1,0:T(8,128)(2,1)S(1)}, u32[]{:S(2)}, u32[]{:S(2)}) %collective-permute-start.1) | collective-permute-done | bytes 983072 | tf_op jit(solution)/shard_map/ppermute | solution.py:33
  62.4 0.9 slice.26
  63.3 5.4 %collective-permute-start.3 = (bf16[4,2,48,640]{3,2,1,0:T(8,128)(2,1)}, bf16[4,2,48,640]{3,2,1,0:T(8,128)(2,1)}, u32[]{:S(2)}, u32[]{:S(2)}) collective-permute-start(bf16[4,2,48,640]{3,2,1,0:T(8,128)(2,1)} %slice.26), channel_id=1, source_target_pairs={{0,24},{8,0},{16,8},{24,16},{1,25},{9,1},{17,9},{25,17},{2,26},{10... | collective-permute-start | bytes 1474568 | tf_op jit(solution)/shard_map/ppermute | solution.py:33
  68.7 0.0 collective-permute-done.b1
  68.7 0.0 copy-start.12
  68.7 0.9 slice.25
  69.6 1.9 collective-permute-start.2
  71.6 0.0 copy-done.15
  71.6 0.7 copy.19.lengths
  72.3 1.2 fusion.where
  73.4 1.7 collective-permute-done.3.b4
  75.2 5.8 %collective-permute-done.2.b3 = bf16[4,2,48,640]{3,2,1,0:T(8,128)(2,1)} collective-permute-done((bf16[4,2,48,640]{3,2,1,0:T(8,128)(2,1)}, bf16[4,2,48,640]{3,2,1,0:T(8,128)(2,1)}, u32[]{:S(2)}, u32[]{:S(2)}) %collective-permute-start.2) | collective-permute-done | bytes 491552 | tf_op jit(solution)/shard_map/ppermute | solution.py:33
  81.0 5.0 %all-gather.7.cloned.1.call-done.normed = bf16[1024,3072]{1,0:T(8,128)(2,1)} async-done(((bf16[128,3072]{1,0:T(8,128)(2,1)}), bf16[1024,3072]{1,0:T(8,128)(2,1)}) %all-gather.7.cloned.1.call-update) | async-done | bytes 6291472 | tf_op jit(solution)/shard_map/all_gather | solution.py:270
  85.9 0.0 copy-done.10
  85.9 0.0 copy-done.11
  85.9 0.0 copy-done.12
  85.9 13.1 %attend.1 = bf16[1024,384]{1,0:T(8,128)(2,1)} custom-call(s32[2]{0:T(128)} %fusion.where, s32[64,3]{1,0:T(8,128)} %copy.19.lengths, bf16[1024,3072]{1,0:T(8,128)(2,1)} %all-gather.7.cloned.1.call-done.normed, bf16[8,2,48,640]{3,2,1,0:T(8,128)(2,1)} %bitcast.13, bf16[8,2,48,640]{3,2,1,0:T(8,128)(2,1)} %copy-done.12, bf16[8,2,48,640]{3,2,1,0:T(8,128)(2,1)} %copy-done.11, ...), custom_call_target="tpu_custom_call" | custom-call | tf_op jit(solution)/shard_map/attend/pallas_call | solution.py:138
  99.0 0.0 copy-start.16
  99.0 0.0 copy-start.9
  99.1 0.0 all-gather.9.cloned.1.call-update
  99.1 21.3 %all-gather.3 = bf16[16,48,384]{2,1,0:T(8,128)(2,1)S(1)} all-gather(bf16[2,48,384]{2,1,0:T(8,128)(2,1)S(1)} %slice.27), channel_id=5, replica_groups=mesh['yl'=2,'z'=8,'x'=4,'yh'=4,'c'=2] {'z'}, dimensions={0}, use_global_device_ids=true | all-gather | bytes 663552 | tf_op jit(solution)/shard_map/all_gather | solution.py:288
  120.4 4.8 %collective-permute-start.5 = (bf16[8,2,48,384]{3,2,1,0:T(8,128)(2,1)S(1)}, bf16[8,2,48,384]{3,2,1,0:T(8,128)(2,1)S(1)}, u32[]{:S(2)}, u32[]{:S(2)}) collective-permute-start(bf16[8,2,48,384]{3,2,1,0:T(8,128)(2,1)S(1)} %bitcast.6), channel_id=1, source_target_pairs={{0,24},{8,0},{16,8},{24,16},{1,25},{9,1},{17,9},{25,17},{2,26},{10... | collective-permute-start | bytes 1769480 | tf_op jit(solution)/shard_map/ppermute | solution.py:33
  125.2 1.9 collective-permute-start.4
  127.1 4.9 %collective-permute-done.5.b2 = bf16[8,2,48,384]{3,2,1,0:T(8,128)(2,1)S(1)} collective-permute-done((bf16[8,2,48,384]{3,2,1,0:T(8,128)(2,1)S(1)}, bf16[8,2,48,384]{3,2,1,0:T(8,128)(2,1)S(1)}, u32[]{:S(2)}, u32[]{:S(2)}) %collective-permute-start.5) | collective-permute-done | bytes 589856 | tf_op jit(solution)/shard_map/ppermute | solution.py:33
  132.0 5.6 %collective-permute-start.7 = (bf16[4,2,48,384]{3,2,1,0:T(8,128)(2,1)S(1)}, bf16[4,2,48,384]{3,2,1,0:T(8,128)(2,1)S(1)}, u32[]{:S(2)}, u32[]{:S(2)}) collective-permute-start(bf16[4,2,48,384]{3,2,1,0:T(8,128)(2,1)S(1)} %slice.29), channel_id=1, source_target_pairs={{0,24},{8,0},{16,8},{24,16},{1,25},{9,1},{17,9},{25,17},{2,26},{10... | collective-permute-start | bytes 884744 | tf_op jit(solution)/shard_map/ppermute | solution.py:33
  137.6 0.0 collective-permute-done.4.b1
  137.6 0.0 copy-start
  137.7 0.8 copy-done
  138.5 1.9 collective-permute-start.6
  140.4 0.0 copy-done.16
  140.4 0.7 copy.20.dest
  141.1 2.0 collective-permute-done.7.b4
  143.1 0.7 copy-done.5
  143.8 3.7 %collective-permute-done.6.b3 = bf16[4,2,48,384]{3,2,1,0:T(8,128)(2,1)S(1)} collective-permute-done((bf16[4,2,48,384]{3,2,1,0:T(8,128)(2,1)S(1)}, bf16[4,2,48,384]{3,2,1,0:T(8,128)(2,1)S(1)}, u32[]{:S(2)}, u32[]{:S(2)}) %collective-permute-start.6) | collective-permute-done | bytes 294944 | tf_op jit(solution)/shard_map/ppermute | solution.py:33
  147.5 0.7 copy-done.7
  148.2 1.1 copy-done.1
  149.3 1.0 copy-done.6
  150.3 1.0 copy-done.8
  151.3 1.0 assemble.1.weight
  152.3 17.3 %all-gather.9.cloned.1.call-done = bf16[8192,384]{1,0:T(8,128)(2,1)} async-done(((bf16[1024,384]{1,0:T(8,128)(2,1)}), bf16[8192,384]{1,0:T(8,128)(2,1)}) %all-gather.9.cloned.1.call-update) | async-done | bytes 6291472 | tf_op jit(solution)/shard_map/all_gather | solution.py:285
  169.6 0.8 copy-done.3
  170.4 0.8 copy-done.4
  171.1 6.0 %project_output.2 = (bf16[2048,384]{1,0:T(8,128)(2,1)}, bf16[512,384]{1,0:T(8,128)(2,1)S(1)}) custom-call(s32[2]{0:T(128)S(1)} %copy-done.9, s32[64,3]{1,0:T(8,128)S(1)} %copy-done.3, s32[64,3]{1,0:T(8,128)S(1)} %copy-done.4, bf16[8,1024,384]{2,1,0:T(8,128)(2,1)} %bitcast.9, bf16[2,8,4,48,384]{4,3,2,1,0:T(8,128)(2,1)S(1)} %assemble.1.weight), custom_call_target="tpu_custom_call" | custom-call | flops 1207959552 | bytes 6000000 | tf_op jit(solution)/shard_map/project_output/pallas_call | solution.py:213
  177.2 3.4 %collective-permute-start.8 = (bf16[512,384]{1,0:T(8,128)(2,1)S(1)}, bf16[512,384]{1,0:T(8,128)(2,1)S(1)}, u32[]{:S(2)}, u32[]{:S(2)}) collective-permute-start(bf16[512,384]{1,0:T(8,128)(2,1)S(1)} %get-tuple-element.13), channel_id=1, source_target_pairs={{0,8},{8,16},{16,24},{24,32},{32,40},{40,48},{48,56},{56,64},{64,7... | collective-permute-start | bytes 1179656 | tf_op jit(solution)/shard_map/ppermute | solution.py:295
  180.6 6.0 %project_output.3 = (bf16[2048,384]{1,0:T(8,128)(2,1)}, bf16[512,384]{1,0:T(8,128)(2,1)S(1)}) custom-call(s32[2]{0:T(128)S(1)} %copy-done.9, s32[64,3]{1,0:T(8,128)S(1)} %copy-done.3, s32[64,3]{1,0:T(8,128)S(1)} %copy-done.4, bf16[8,1024,384]{2,1,0:T(8,128)(2,1)} %bitcast.10, ...), custom_call_target="tpu_custom_call", output_to_operand_aliasing={{0}: (5, {})} | custom-call | flops 1207959552 | bytes 6000000 | tf_op jit(solution)/shard_map/project_output/pallas_call | solution.py:213
  186.7 3.2 %collective-permute-start.9 = (bf16[512,384]{1,0:T(8,128)(2,1)S(1)}, bf16[512,384]{1,0:T(8,128)(2,1)S(1)}, u32[]{:S(2)}, u32[]{:S(2)}) collective-permute-start(bf16[512,384]{1,0:T(8,128)(2,1)S(1)} %get-tuple-element.14), channel_id=1, source_target_pairs={{0,8},{8,16},{16,24},{24,32},{32,40},{40,48},{48,56},{56,64},{64,7... | collective-permute-start | bytes 1179656 | tf_op jit(solution)/shard_map/ppermute | solution.py:295
  189.8 8.5 %collective-permute-done.8 = bf16[512,384]{1,0:T(8,128)(2,1)S(1)} collective-permute-done((bf16[512,384]{1,0:T(8,128)(2,1)S(1)}, bf16[512,384]{1,0:T(8,128)(2,1)S(1)}, u32[]{:S(2)}, u32[]{:S(2)}) %collective-permute-start.8) | collective-permute-done | bytes 393248 | tf_op jit(solution)/shard_map/ppermute | solution.py:295
  198.3 0.8 constant_dynamic-update-slice_fusion.1
  199.1 7.6 %collective-permute-done.9 = bf16[512,384]{1,0:T(8,128)(2,1)S(1)} collective-permute-done((bf16[512,384]{1,0:T(8,128)(2,1)S(1)}, bf16[512,384]{1,0:T(8,128)(2,1)S(1)}, u32[]{:S(2)}, u32[]{:S(2)}) %collective-permute-start.9) | collective-permute-done | bytes 393248 | tf_op jit(solution)/shard_map/ppermute | solution.py:295
  206.7 0.8 constant_dynamic-update-slice_fusion
  (18 shorter events, 0.1 us)
Async XLA Ops:
  6.5 79.4 %all-gather.7.cloned.1.call-start = ((), (), s32[]{:S(2)}) async-start(), calls=%async_computation | async-start | bytes 7077888 | tf_op jit(solution)/shard_map/all_gather | solution.py:270
  7.2 1.1 copy-start.2
  8.4 2.2 %copy-start.13 = (bf16[48,384]{1,0:T(8,128)(2,1)S(1)}, bf16[48,384]{1,0:T(8,128)(2,1)}, u32[]{:S(2)}) copy-start(bf16[48,384]{1,0:T(8,128)(2,1)} %param.14) | copy-start | bytes 110596
  8.4 2.2 %copy-start.14 = (bf16[48,384]{1,0:T(8,128)(2,1)S(1)}, bf16[48,384]{1,0:T(8,128)(2,1)}, u32[]{:S(2)}) copy-start(bf16[48,384]{1,0:T(8,128)(2,1)} %param.11) | copy-start | bytes 110596
  9.8 159.8 %all-gather.9.cloned.1.call-start = ((), (), s32[]{:S(2)}) async-start(), calls=%async_computation.1 | async-start | bytes 7077888 | tf_op jit(solution)/shard_map/all_gather | solution.py:285
  15.4 56.1 %copy-start.15 = (s32[64,3]{0,1:T(4,128)S(1)}, s32[64,3]{0,1:T(4,128)}, u32[]{:S(2)}) copy-start(s32[64,3]{0,1:T(4,128)} %param.15) | copy-start | bytes 2308
  43.9 42.0 %copy-start.10 = (bf16[16,48,640]{2,1,0:T(8,128)(2,1)}, bf16[16,48,640]{2,1,0:T(8,128)(2,1)S(1)}, u32[]{:S(2)}) copy-start(bf16[16,48,640]{2,1,0:T(8,128)(2,1)S(1)} %all-gather.1) | copy-start | bytes 2949124
  43.9 18.5 %collective-permute-start.1 = (bf16[8,2,48,640]{3,2,1,0:T(8,128)(2,1)S(1)}, bf16[8,2,48,640]{3,2,1,0:T(8,128)(2,1)S(1)}, u32[]{:S(2)}, u32[]{:S(2)}) collective-permute-start(bf16[8,2,48,640]{3,2,1,0:T(8,128)(2,1)S(1)} %bitcast.11), channel_id=1, source_target_pairs={{0,24},{8,0},{16,8},{24,16},{1,25},{9,1},{17,9},{25,17},{2,26},{10... | collective-permute-start | bytes 2949128 | tf_op jit(solution)/shard_map/ppermute | solution.py:33
  48.3 20.5 %collective-permute-start = (bf16[8,2,48,640]{3,2,1,0:T(8,128)(2,1)S(1)}, bf16[8,2,48,640]{3,2,1,0:T(8,128)(2,1)S(1)}, u32[]{:S(2)}, u32[]{:S(2)}) collective-permute-start(bf16[8,2,48,640]{3,2,1,0:T(8,128)(2,1)S(1)} %bitcast.12), channel_id=1, source_target_pairs={{0,8},{8,16},{16,24},{24,0},{1,9},{9,17},{17,25},{25,1},{2,10},{10... | collective-permute-start | bytes 2949128 | tf_op jit(solution)/shard_map/ppermute | solution.py:33
  62.4 23.5 %copy-start.11 = (bf16[8,2,48,640]{3,2,1,0:T(8,128)(2,1)}, bf16[8,2,48,640]{3,2,1,0:T(8,128)(2,1)S(1)}, u32[]{:S(2)}) copy-start(bf16[8,2,48,640]{3,2,1,0:T(8,128)(2,1)S(1)} %collective-permute-done.1.b2) | copy-start | bytes 2949124
  63.3 11.9 %collective-permute-start.3 = (bf16[4,2,48,640]{3,2,1,0:T(8,128)(2,1)}, bf16[4,2,48,640]{3,2,1,0:T(8,128)(2,1)}, u32[]{:S(2)}, u32[]{:S(2)}) collective-permute-start(bf16[4,2,48,640]{3,2,1,0:T(8,128)(2,1)} %slice.26), channel_id=1, source_target_pairs={{0,24},{8,0},{16,8},{24,16},{1,25},{9,1},{17,9},{25,17},{2,26},{10... | collective-permute-start | bytes 1474568 | tf_op jit(solution)/shard_map/ppermute | solution.py:33
  68.7 17.2 %copy-start.12 = (bf16[8,2,48,640]{3,2,1,0:T(8,128)(2,1)}, bf16[8,2,48,640]{3,2,1,0:T(8,128)(2,1)S(1)}, u32[]{:S(2)}) copy-start(bf16[8,2,48,640]{3,2,1,0:T(8,128)(2,1)S(1)} %collective-permute-done.b1) | copy-start | bytes 2949124
  69.6 11.3 %collective-permute-start.2 = (bf16[4,2,48,640]{3,2,1,0:T(8,128)(2,1)}, bf16[4,2,48,640]{3,2,1,0:T(8,128)(2,1)}, u32[]{:S(2)}, u32[]{:S(2)}) collective-permute-start(bf16[4,2,48,640]{3,2,1,0:T(8,128)(2,1)} %slice.25), channel_id=1, source_target_pairs={{0,8},{8,16},{16,24},{24,0},{1,9},{9,17},{17,25},{25,1},{2,10},{10... | collective-permute-start | bytes 1474568 | tf_op jit(solution)/shard_map/ppermute | solution.py:33
  99.0 41.3 %copy-start.16 = (s32[64,3]{0,1:T(4,128)S(1)}, s32[64,3]{0,1:T(4,128)}, u32[]{:S(2)}) copy-start(s32[64,3]{0,1:T(4,128)} %param.16) | copy-start | bytes 2308
  99.0 49.2 %copy-start.9 = (s32[2]{0:T(128)S(1)}, s32[2]{0:T(128)}, u32[]{:S(2)}) copy-start(s32[2]{0:T(128)} %fusion.where) | copy-start | bytes 28
  120.4 11.6 %collective-permute-start.5 = (bf16[8,2,48,384]{3,2,1,0:T(8,128)(2,1)S(1)}, bf16[8,2,48,384]{3,2,1,0:T(8,128)(2,1)S(1)}, u32[]{:S(2)}, u32[]{:S(2)}) collective-permute-start(bf16[8,2,48,384]{3,2,1,0:T(8,128)(2,1)S(1)} %bitcast.6), channel_id=1, source_target_pairs={{0,24},{8,0},{16,8},{24,16},{1,25},{9,1},{17,9},{25,17},{2,26},{10... | collective-permute-start | bytes 1769480 | tf_op jit(solution)/shard_map/ppermute | solution.py:33
  125.2 12.4 %collective-permute-start.4 = (bf16[8,2,48,384]{3,2,1,0:T(8,128)(2,1)S(1)}, bf16[8,2,48,384]{3,2,1,0:T(8,128)(2,1)S(1)}, u32[]{:S(2)}, u32[]{:S(2)}) collective-permute-start(bf16[8,2,48,384]{3,2,1,0:T(8,128)(2,1)S(1)} %bitcast.7), channel_id=1, source_target_pairs={{0,8},{8,16},{16,24},{24,0},{1,9},{9,17},{17,25},{25,1},{2,10},{10... | collective-permute-start | bytes 1769480 | tf_op jit(solution)/shard_map/ppermute | solution.py:33
  132.0 11.1 %collective-permute-start.7 = (bf16[4,2,48,384]{3,2,1,0:T(8,128)(2,1)S(1)}, bf16[4,2,48,384]{3,2,1,0:T(8,128)(2,1)S(1)}, u32[]{:S(2)}, u32[]{:S(2)}) collective-permute-start(bf16[4,2,48,384]{3,2,1,0:T(8,128)(2,1)S(1)} %slice.29), channel_id=1, source_target_pairs={{0,24},{8,0},{16,8},{24,16},{1,25},{9,1},{17,9},{25,17},{2,26},{10... | collective-permute-start | bytes 884744 | tf_op jit(solution)/shard_map/ppermute | solution.py:33
  137.6 0.8 copy-start
  138.5 9.1 %collective-permute-start.6 = (bf16[4,2,48,384]{3,2,1,0:T(8,128)(2,1)S(1)}, bf16[4,2,48,384]{3,2,1,0:T(8,128)(2,1)S(1)}, u32[]{:S(2)}, u32[]{:S(2)}) collective-permute-start(bf16[4,2,48,384]{3,2,1,0:T(8,128)(2,1)S(1)} %slice.28), channel_id=1, source_target_pairs={{0,8},{8,16},{16,24},{24,0},{1,9},{9,17},{17,25},{25,1},{2,10},{10... | collective-permute-start | bytes 884744 | tf_op jit(solution)/shard_map/ppermute | solution.py:33
  143.1 0.7 copy-start.5
  147.5 0.7 copy-start.7
  148.2 1.1 copy-start.1
  149.3 1.0 copy-start.6
  150.3 1.0 copy-start.8
  169.6 0.8 copy-start.3
  170.4 0.8 copy-start.4
  177.2 21.1 %collective-permute-start.8 = (bf16[512,384]{1,0:T(8,128)(2,1)S(1)}, bf16[512,384]{1,0:T(8,128)(2,1)S(1)}, u32[]{:S(2)}, u32[]{:S(2)}) collective-permute-start(bf16[512,384]{1,0:T(8,128)(2,1)S(1)} %get-tuple-element.13), channel_id=1, source_target_pairs={{0,8},{8,16},{16,24},{24,32},{32,40},{40,48},{48,56},{56,64},{64,7... | collective-permute-start | bytes 1179656 | tf_op jit(solution)/shard_map/ppermute | solution.py:295
  186.7 20.0 %collective-permute-start.9 = (bf16[512,384]{1,0:T(8,128)(2,1)S(1)}, bf16[512,384]{1,0:T(8,128)(2,1)S(1)}, u32[]{:S(2)}, u32[]{:S(2)}) collective-permute-start(bf16[512,384]{1,0:T(8,128)(2,1)S(1)} %get-tuple-element.14), channel_id=1, source_target_pairs={{0,8},{8,16},{16,24},{24,32},{32,40},{40,48},{48,56},{56,64},{64,7... | collective-permute-start | bytes 1179656 | tf_op jit(solution)/shard_map/ppermute | solution.py:295
Sparse Core Ops, SparseCore 0:
  9.9 75.9 all-gather.6
  99.2 70.3 all-gather.8
